TPU v7x, 1024 devices: a whole 4x4x32 slice. The times are simulated.
1024 devices in a mesh: dp: 16 (over z_hi, x, core), expert: 64 (over z_lo, y).
Axes of the slice: x: 4, y: 4, z: 32 (z_hi: 2, z_lo: 16; z = z_hi * 16 + z_lo), core: 2. Of those that a mesh axis runs over, the one named last changes fastest.
Arguments:
- out_grad: bfloat16 [2, 1024, 4096], P(None, 'expert', 'dp'), may hold values from -6 to 6
- expert_ids: int32 [2, 1024, 8], P(None, 'expert'), may hold values from 0 to 63, all different within a row; in each aligned block of 16 rows (0 to 15, 16 to 31, ..., all dimensions but the last counted through in order) at most 4 rows name the same one
- probs: bfloat16 [2, 1024, 8], P(None, 'expert'), may hold values from 0.019897461 to 0.5
- saved_inputs: bfloat16 [2, 64, 256, 4096], P(None, 'expert', None, 'dp'), may hold values from -6 to 6
- gate_pre: bfloat16 [2, 64, 256, 768], P(None, 'expert'), may hold values from -6 to 6
- up_pre: bfloat16 [2, 64, 256, 768], P(None, 'expert'), may hold values from -6 to 6
- w_gate: bfloat16 [64, 4096, 768], P('expert', 'dp'), may hold values from -0.09375 to 0.09375
- w_up: bfloat16 [64, 4096, 768], P('expert', 'dp'), may hold values from -0.09375 to 0.09375
- w_down: bfloat16 [64, 768, 4096], P('expert', None, 'dp'), may hold values from -0.21875 to 0.21875
Outputs:
- in_grad: bfloat16 [2, 1024, 4096], P(None, 'expert', 'dp')
- prob_grad: bfloat16 [2, 1024, 8], P(None, 'expert')
- grad_gate: bfloat16 [64, 4096, 768], P('expert', 'dp')
- grad_up: bfloat16 [64, 4096, 768], P('expert', 'dp')
- grad_down: bfloat16 [64, 768, 4096], P('expert', None, 'dp')
Inputs may be any that keep to these rules, and one draw needn't show every extreme that they name: `expert_ids`: in each microbatch, the routes of the 16 tokens of one index of expert name any expert at most 4 times, a bound that some block reaches.
All inputs are finite; a program needn't handle non-finite values.
Results may differ from a plain program's by a relative error of at most 0.0057.
Values may be sent and summed in bfloat16 or wider, within the bound.
No kernel may reach another device: no remote copies, remote signals or barrier semaphores. Data moves between devices by JAX's collectives and lax.ppermute only.
A program may use at most 32 MiB of HBM per device.

v0:
```python
import jax
import jax.numpy as jnp
from jax import lax
from jax.sharding import PartitionSpec as P


def silu_parts(gate_f):
    sig = jax.nn.sigmoid(gate_f)
    return (gate_f * sig, sig * (1.0 + gate_f * (1.0 - sig)))


def contract(left, right, left_dim, right_dim):
    return lax.dot_general(
        left, right, (((left_dim,), (right_dim,)), ((), ())), preferred_element_type=jnp.float32
    )


def route_maps(ids_m, n_expert, cap):
    tok_count, top_count = ids_m.shape
    flat = ids_m.reshape(-1)
    hits = (flat[:, None] == jnp.arange(n_expert, dtype=jnp.int32)[None, :]).astype(jnp.int32)
    earlier = jnp.cumsum(hits, axis=0) - hits
    dest = flat * cap + jnp.sum(earlier * hits, axis=1)
    placed = jnp.arange(n_expert * cap, dtype=jnp.int32)[:, None] == dest[None, :]
    token_map = jnp.sum(
        placed.reshape(n_expert * cap, tok_count, top_count).astype(jnp.int32), axis=2
    )
    return (placed, token_map.astype(jnp.bfloat16))


def pack_rows(out_m, probs_m, placed, token_map, n_expert, cap):
    rows = jnp.dot(token_map, out_m, preferred_element_type=jnp.float32).astype(jnp.bfloat16)
    weights = jnp.sum(jnp.where(placed, probs_m.reshape(1, -1).astype(jnp.float32), 0.0), axis=1)
    return (
        rows.reshape(n_expert, cap, rows.shape[1]),
        weights.astype(jnp.bfloat16).reshape(n_expert, cap),
    )


def unpack_rows(back_rows, back_probs, placed, token_map, shape):
    flat_rows = back_rows.reshape(-1, back_rows.shape[-1])
    grads = contract(token_map, flat_rows, 0, 0).astype(jnp.bfloat16)
    picked = jnp.sum(jnp.where(placed, back_probs.reshape(-1, 1).astype(jnp.float32), 0.0), axis=0)
    return (grads, picked.astype(jnp.bfloat16).reshape(shape))


def slot_grads(summed, act_rows, slope_rows, up_rows, hidden_rows, weight_rows):
    slot_prob = jnp.sum(summed * hidden_rows, axis=1).astype(jnp.bfloat16)
    dh = weight_rows * summed
    dgate = (dh * up_rows * slope_rows).astype(jnp.bfloat16)
    dup = (dh * act_rows).astype(jnp.bfloat16)
    return (dgate, dup, slot_prob)


def expert_pass(rows, weights, inputs_m, gate_m, up_m, w_gate0, w_up0, w_down0, totals):
    slots, width = rows.shape
    acc_gate, acc_up, acc_down = totals
    gate_f = gate_m.astype(jnp.float32)
    up_f = up_m.astype(jnp.float32)
    act, slope = silu_parts(gate_f)
    hidden = act * up_f
    weight_f = weights.astype(jnp.float32)[:, None]
    scaled = (weight_f * hidden).astype(jnp.bfloat16)
    acc_down = acc_down + contract(scaled, rows, 0, 0)
    carry = (
        acc_gate,
        acc_up,
        jnp.zeros((slots, width), jnp.bfloat16),
        jnp.zeros((slots,), jnp.bfloat16),
    )
    summed = lax.psum_scatter(contract(rows, w_down0, 1, 1), "dp", scatter_dimension=0, tiled=True)
    dgate, dup, slot_prob = slot_grads(
        lax.all_gather(summed, "dp", axis=0, tiled=True), act, slope, up_f, hidden, weight_f
    )
    sum_gate, sum_up, slot_rows, slot_probs = carry
    sum_gate = sum_gate + contract(inputs_m, dgate, 0, 0)
    sum_up = sum_up + contract(inputs_m, dup, 0, 0)
    new_rows = (contract(dgate, w_gate0, 1, 1) + contract(dup, w_up0, 1, 1)).astype(jnp.bfloat16)
    slot_rows = new_rows
    slot_probs = slot_prob
    carry = (sum_gate, sum_up, slot_rows, slot_probs)
    sum_gate, sum_up, slot_rows, slot_probs = carry
    return (slot_rows, slot_probs, (sum_gate, sum_up, acc_down))


def local(out_grad, expert_ids, probs, saved_inputs, gate_pre, up_pre, w_gate, w_up, w_down):
    n_expert = lax.axis_size("expert")
    batches = out_grad.shape[0]
    slots = saved_inputs.shape[2]
    cap = slots // n_expert
    width = out_grad.shape[2]
    hidden_units = w_gate.shape[2]
    totals = (
        jnp.zeros((width, hidden_units), jnp.float32),
        jnp.zeros((width, hidden_units), jnp.float32),
        jnp.zeros((hidden_units, width), jnp.float32),
    )
    tables = [route_maps(expert_ids[m], n_expert, cap) for m in range(batches)]
    packed = [
        pack_rows(out_grad[m], probs[m], tables[m][0], tables[m][1], n_expert, cap)
        for m in range(batches)
    ]
    in_grads = []
    prob_grads = []
    for m in range(batches):
        got_rows, got_probs = (
            lax.all_to_all(packed[m][0], "expert", split_axis=0, concat_axis=0, tiled=True),
            lax.all_to_all(packed[m][1], "expert", split_axis=0, concat_axis=0, tiled=True),
        )
        slot_rows, slot_probs, totals = expert_pass(
            got_rows.reshape(slots, width),
            got_probs.reshape(slots),
            saved_inputs[m, 0],
            gate_pre[m, 0],
            up_pre[m, 0],
            w_gate[0],
            w_up[0],
            w_down[0],
            totals,
        )
        back_rows, back_probs = (
            lax.all_to_all(
                slot_rows.reshape(n_expert, cap, width),
                "expert",
                split_axis=0,
                concat_axis=0,
                tiled=True,
            ),
            lax.all_to_all(
                slot_probs.reshape(n_expert, cap), "expert", split_axis=0, concat_axis=0, tiled=True
            ),
        )
        grads, picked = unpack_rows(
            back_rows, back_probs, tables[m][0], tables[m][1], expert_ids.shape[1:]
        )
        in_grads.append(grads)
        prob_grads.append(picked)
    sum_gate, sum_up, sum_down = totals
    return (
        jnp.stack(in_grads, 0),
        jnp.stack(prob_grads, 0),
        sum_gate.astype(jnp.bfloat16)[None],
        sum_up.astype(jnp.bfloat16)[None],
        sum_down.astype(jnp.bfloat16)[None],
    )


def solution(mesh):
    placed = (
        P(None, "expert", "dp"),
        P(None, "expert", None),
        P(None, "expert", None),
        P(None, "expert", None, "dp"),
        P(None, "expert", None, None),
        P(None, "expert", None, None),
        P("expert", "dp", None),
        P("expert", "dp", None),
        P("expert", None, "dp"),
    )
    return jax.shard_map(
        local,
        mesh=mesh,
        in_specs=placed,
        out_specs=(
            P(None, "expert", "dp"),
            P(None, "expert", None),
            P("expert", "dp", None),
            P("expert", "dp", None),
            P("expert", None, "dp"),
        ),
        check_vma=False,
    )
```

profile of v0, /device:TPU:1, one launch (start us, length us, event | category | flops | bytes accessed | tf_op | source)
XLA Modules:
  0.0 654.6 jit_solution(12808939401374671018)
XLA Ops:
  7.2 0.8 fusion.91
  13.2 30.0 %all-to-all-start.4 = ((bf16[64,4,256]{2,1,0:T(4,128)(2,1)}), bf16[64,4,256]{2,1,0:T(4,128)(2,1)S(1)}, u32[]{:S(2)}, u32[]{:S(2)}) async-start(bf16[64,4,256]{2,1,0:T(4,128)(2,1)} %reshape.246), calls=%async_computation.5 | async-start | bytes 262144 | tf_op jit(solution)/shard_map/all_to_all | solution.py:107
  44.7 21.4 %all-to-all-done.4 = bf16[64,4,256]{2,1,0:T(4,128)(2,1)S(1)} async-done(((bf16[64,4,256]{2,1,0:T(4,128)(2,1)}), bf16[64,4,256]{2,1,0:T(4,128)(2,1)S(1)}, u32[]{:S(2)}, u32[]{:S(2)}) %all-to-all-start.4) | async-done | bytes 131104 | tf_op jit(solution)/shard_map/all_to_all | solution.py:107
  66.0 11.1 %all-to-all-start.1 = ((bf16[64,4,256]{2,1,0:T(4,128)(2,1)}), bf16[64,4,256]{2,1,0:T(4,128)(2,1)S(1)}, u32[]{:S(2)}, u32[]{:S(2)}) async-start(bf16[64,4,256]{2,1,0:T(4,128)(2,1)} %reshape.242), calls=%async_computation.1 | async-start | bytes 262144 | tf_op jit(solution)/shard_map/all_to_all | solution.py:107
  77.3 1.2 fusion.57
  78.5 20.8 %all-to-all-done.1 = bf16[64,4,256]{2,1,0:T(4,128)(2,1)S(1)} async-done(((bf16[64,4,256]{2,1,0:T(4,128)(2,1)}), bf16[64,4,256]{2,1,0:T(4,128)(2,1)S(1)}, u32[]{:S(2)}, u32[]{:S(2)}) %all-to-all-start.1) | async-done | bytes 131104 | tf_op jit(solution)/shard_map/all_to_all | solution.py:107
  99.4 1.2 fusion.59
  101.9 135.1 %reduce-scatter.5.cloned.1.call-done = f32[16,768]{1,0:T(8,128)} async-done(((f32[256,768]{1,0:T(8,128)}), f32[16,768]{1,0:T(8,128)}) %reduce-scatter.5.cloned.1.call-update) | async-done | bytes 49168 | tf_op jit(solution)/shard_map/reduce_scatter | solution.py:71
  237.0 72.5 %all_gather.7 = f32[256,768]{1,0:T(8,128)S(1)} all-gather(f32[16,768]{1,0:T(8,128)} %reduce-scatter.5.cloned.1.call-done), channel_id=1, replica_groups=mesh['dp'=16,'expert'=64] {'dp'}, dimensions={0}, use_global_device_ids=true | all-gather | bytes 835584 | tf_op jit(solution)/shard_map/all_gather | solution.py:73
  309.5 75.4 %reduce-scatter.3.cloned.1.call-done = f32[16,768]{1,0:T(8,128)} async-done(((f32[256,768]{1,0:T(8,128)}), f32[16,768]{1,0:T(8,128)}) %reduce-scatter.3.cloned.1.call-update) | async-done | bytes 49168 | tf_op jit(solution)/shard_map/reduce_scatter | solution.py:71
  384.9 72.8 %all_gather.6 = f32[256,768]{1,0:T(8,128)S(1)} all-gather(f32[16,768]{1,0:T(8,128)} %reduce-scatter.3.cloned.1.call-done), channel_id=1, replica_groups=mesh['dp'=16,'expert'=64] {'dp'}, dimensions={0}, use_global_device_ids=true | all-gather | bytes 835584 | tf_op jit(solution)/shard_map/all_gather | solution.py:73
  457.7 1.1 fusion.23
  459.5 0.7 convert_element_type.331
  460.2 22.3 %all-to-all-start.7 = ((bf16[64,1,4]{2,1,0:T(2,128)(2,1)}), bf16[64,1,4]{2,1,0:T(2,128)(2,1)S(1)}, u32[]{:S(2)}, u32[]{:S(2)}) async-start(bf16[64,1,4]{2,1,0:T(2,128)(2,1)} %convert_element_type.331), calls=%async_computation.9 | async-start | bytes 65536 | tf_op jit(solution)/shard_map/all_to_all | solution.py:129
  483.2 0.7 convert_element_type.330
  483.9 19.5 %all-to-all-done.7 = bf16[64,1,4]{2,1,0:T(2,128)(2,1)S(1)} async-done(((bf16[64,1,4]{2,1,0:T(2,128)(2,1)}), bf16[64,1,4]{2,1,0:T(2,128)(2,1)S(1)}, u32[]{:S(2)}, u32[]{:S(2)}) %all-to-all-start.7) | async-done | bytes 544 | tf_op jit(solution)/shard_map/all_to_all | solution.py:129
  503.4 5.2 all-to-all-start.6
  509.5 19.9 %all-to-all-done.6 = bf16[64,1,4]{2,1,0:T(2,128)(2,1)S(1)} async-done(((bf16[64,1,4]{2,1,0:T(2,128)(2,1)}), bf16[64,1,4]{2,1,0:T(2,128)(2,1)S(1)}, u32[]{:S(2)}, u32[]{:S(2)}) %all-to-all-start.6) | async-done | bytes 544 | tf_op jit(solution)/shard_map/all_to_all | solution.py:129
  530.0 0.7 convert_element_type.329
  530.7 4.6 all-to-all-start.3
  535.6 0.7 convert_element_type.328
  537.7 18.5 %all-to-all-done.3 = bf16[64,1,4]{2,1,0:T(2,128)(2,1)S(1)} async-done(((bf16[64,1,4]{2,1,0:T(2,128)(2,1)}), bf16[64,1,4]{2,1,0:T(2,128)(2,1)S(1)}, u32[]{:S(2)}, u32[]{:S(2)}) %all-to-all-start.3) | async-done | bytes 544 | tf_op jit(solution)/shard_map/all_to_all | solution.py:108
  556.2 4.6 all-to-all-start
  561.6 20.0 %all-to-all-done = bf16[64,1,4]{2,1,0:T(2,128)(2,1)S(1)} async-done(((bf16[64,1,4]{2,1,0:T(2,128)(2,1)}), bf16[64,1,4]{2,1,0:T(2,128)(2,1)S(1)}, u32[]{:S(2)}, u32[]{:S(2)}) %all-to-all-start) | async-done | bytes 544 | tf_op jit(solution)/shard_map/all_to_all | solution.py:108
  582.4 2.2 multiply_convert_fusion
  586.7 4.9 all-to-all-start.5
  594.5 0.9 copy.64
  595.5 18.3 %all-to-all-done.5 = bf16[64,4,256]{2,1,0:T(4,128)(2,1)S(1)} async-done(((bf16[64,4,256]{2,1,0:T(4,128)(2,1)}), bf16[64,4,256]{2,1,0:T(4,128)(2,1)S(1)}, u32[]{:S(2)}, u32[]{:S(2)}) %all-to-all-start.5) | async-done | bytes 131104 | tf_op jit(solution)/shard_map/all_to_all | solution.py:122
  614.4 10.3 %all-to-all-start.2 = ((bf16[64,4,256]{2,1,0:T(4,128)(2,1)}), bf16[64,4,256]{2,1,0:T(4,128)(2,1)S(1)}, u32[]{:S(2)}, u32[]{:S(2)}) async-start(bf16[64,4,256]{2,1,0:T(4,128)(2,1)} %reshape.244), calls=%async_computation.3 | async-start | bytes 262144 | tf_op jit(solution)/shard_map/all_to_all | solution.py:122
  625.4 0.9 copy.65
  627.6 1.3 fusion.3
  629.1 17.9 %all-to-all-done.2 = bf16[64,4,256]{2,1,0:T(4,128)(2,1)S(1)} async-done(((bf16[64,4,256]{2,1,0:T(4,128)(2,1)}), bf16[64,4,256]{2,1,0:T(4,128)(2,1)S(1)}, u32[]{:S(2)}, u32[]{:S(2)}) %all-to-all-start.2) | async-done | bytes 131104 | tf_op jit(solution)/shard_map/all_to_all | solution.py:122
  (137 shorter events, 22.4 us)
Async XLA Ops:
  7.2 70.1 %copy-start = (bf16[1,768,256]{2,1,0:T(8,128)(2,1)S(1)}, bf16[1,768,256]{2,1,0:T(8,128)(2,1)}, u32[]{:S(2)}) copy-start(bf16[1,768,256]{2,1,0:T(8,128)(2,1)} %param.17) | copy-start | bytes 1179652
  13.2 52.8 %all-to-all-start.4 = ((bf16[64,4,256]{2,1,0:T(4,128)(2,1)}), bf16[64,4,256]{2,1,0:T(4,128)(2,1)S(1)}, u32[]{:S(2)}, u32[]{:S(2)}) async-start(bf16[64,4,256]{2,1,0:T(4,128)(2,1)} %reshape.246), calls=%async_computation.5 | async-start | bytes 262144 | tf_op jit(solution)/shard_map/all_to_all | solution.py:107
  66.0 33.3 %all-to-all-start.1 = ((bf16[64,4,256]{2,1,0:T(4,128)(2,1)}), bf16[64,4,256]{2,1,0:T(4,128)(2,1)S(1)}, u32[]{:S(2)}, u32[]{:S(2)}) async-start(bf16[64,4,256]{2,1,0:T(4,128)(2,1)} %reshape.242), calls=%async_computation.1 | async-start | bytes 262144 | tf_op jit(solution)/shard_map/all_to_all | solution.py:107
  77.2 159.8 %reduce-scatter.5.cloned.1.call-start = ((), (), s32[]{:S(2)}) async-start(), calls=%async_computation.11 | async-start | bytes 835584 | tf_op jit(solution)/shard_map/reduce_scatter | solution.py:71
  77.3 1.2 copy-start.9
  78.5 306.4 %reduce-scatter.3.cloned.1.call-start = ((), (), s32[]{:S(2)}) async-start(), calls=%async_computation.10 | async-start | bytes 835584 | tf_op jit(solution)/shard_map/reduce_scatter | solution.py:71
  99.4 1.2 copy-start.11
  101.9 355.8 %copy-start.1 = (bf16[2,1,256,768]{3,2,1,0:T(8,128)(2,1)S(1)}, bf16[2,1,256,768]{3,2,1,0:T(8,128)(2,1)}, u32[]{:S(2)}) copy-start(bf16[2,1,256,768]{3,2,1,0:T(8,128)(2,1)} %param.14) | copy-start | bytes 2359300
  101.9 355.8 %copy-start.3 = (bf16[2,1,256,768]{3,2,1,0:T(8,128)(2,1)S(1)}, bf16[2,1,256,768]{3,2,1,0:T(8,128)(2,1)}, u32[]{:S(2)}) copy-start(bf16[2,1,256,768]{3,2,1,0:T(8,128)(2,1)} %param.13) | copy-start | bytes 2359300
  460.2 22.3 %copy-start.26 = (s32[128]{0:T(128)S(1)}, s32[128]{0:T(128)}, u32[]{:S(2)}) copy-start(s32[128]{0:T(128)} %copy-done.25) | copy-start | bytes 1540
  460.2 22.3 %copy-start.35 = (s32[128]{0:T(128)S(1)}, s32[128]{0:T(128)}, u32[]{:S(2)}) copy-start(s32[128]{0:T(128)} %copy-done.34) | copy-start | bytes 1540
  460.2 43.2 %all-to-all-start.7 = ((bf16[64,1,4]{2,1,0:T(2,128)(2,1)}), bf16[64,1,4]{2,1,0:T(2,128)(2,1)S(1)}, u32[]{:S(2)}, u32[]{:S(2)}) async-start(bf16[64,1,4]{2,1,0:T(2,128)(2,1)} %convert_element_type.331), calls=%async_computation.9 | async-start | bytes 65536 | tf_op jit(solution)/shard_map/all_to_all | solution.py:129
  483.9 24.7 %copy-start.24 = (s32[128]{0:T(128)S(1)}, s32[128]{0:T(128)}, u32[]{:S(2)}) copy-start(s32[128]{0:T(128)} %copy-done.23) | copy-start | bytes 1540
  483.9 24.7 %copy-start.33 = (s32[128]{0:T(128)S(1)}, s32[128]{0:T(128)}, u32[]{:S(2)}) copy-start(s32[128]{0:T(128)} %copy-done.32) | copy-start | bytes 1540
  503.4 5.2 copy-start.20
  503.4 26.1 %all-to-all-start.6 = ((bf16[64,1,4]{2,1,0:T(2,128)(2,1)}), bf16[64,1,4]{2,1,0:T(2,128)(2,1)S(1)}, u32[]{:S(2)}, u32[]{:S(2)}) async-start(bf16[64,1,4]{2,1,0:T(2,128)(2,1)} %convert_element_type.330), calls=%async_computation.8 | async-start | bytes 65536 | tf_op jit(solution)/shard_map/all_to_all | solution.py:129
  530.7 25.5 %all-to-all-start.3 = ((bf16[64,1,4]{2,1,0:T(2,128)(2,1)}), bf16[64,1,4]{2,1,0:T(2,128)(2,1)S(1)}, u32[]{:S(2)}, u32[]{:S(2)}) async-start(bf16[64,1,4]{2,1,0:T(2,128)(2,1)} %convert_element_type.329), calls=%async_computation.4 | async-start | bytes 65536 | tf_op jit(solution)/shard_map/all_to_all | solution.py:108
  556.2 25.4 %all-to-all-start = ((bf16[64,1,4]{2,1,0:T(2,128)(2,1)}), bf16[64,1,4]{2,1,0:T(2,128)(2,1)S(1)}, u32[]{:S(2)}, u32[]{:S(2)}) async-start(bf16[64,1,4]{2,1,0:T(2,128)(2,1)} %convert_element_type.328), calls=%async_computation | async-start | bytes 65536 | tf_op jit(solution)/shard_map/all_to_all | solution.py:108
  582.4 2.3 copy-start.5
  584.6 1.0 copy-start.7
  586.0 6.4 copy-start.6
  586.7 4.9 copy-start.21
  586.7 5.0 copy-start.22
  586.7 27.1 %all-to-all-start.5 = ((bf16[64,4,256]{2,1,0:T(4,128)(2,1)}), bf16[64,4,256]{2,1,0:T(4,128)(2,1)S(1)}, u32[]{:S(2)}, u32[]{:S(2)}) async-start(bf16[64,4,256]{2,1,0:T(4,128)(2,1)} %reshape.248), calls=%async_computation.7 | async-start | bytes 262144 | tf_op jit(solution)/shard_map/all_to_all | solution.py:122
  592.9 1.0 copy-start.8
  614.4 32.5 %all-to-all-start.2 = ((bf16[64,4,256]{2,1,0:T(4,128)(2,1)}), bf16[64,4,256]{2,1,0:T(4,128)(2,1)S(1)}, u32[]{:S(2)}, u32[]{:S(2)}) async-start(bf16[64,4,256]{2,1,0:T(4,128)(2,1)} %reshape.244), calls=%async_computation.3 | async-start | bytes 262144 | tf_op jit(solution)/shard_map/all_to_all | solution.py:122
  625.1 1.3 copy-start.4
  625.1 1.3 copy-start.12
  625.1 1.3 copy-start.29
  625.4 1.3 copy-start.2
  627.6 1.3 copy-start.14
  629.1 17.9 %copy-start.16 = (s32[256,16]{0,1:T(8,128)S(1)}, s32[256,16]{0,1:T(8,128)}, u32[]{:S(2)}) copy-start(s32[256,16]{0,1:T(8,128)} %copy-done.15) | copy-start | bytes 49156
  (14 other events, 9.3 us)
Sparse Core Ops, SparseCore 0:
  83.8 153.1 reduce-scatter.4
  242.8 142.0 reduce-scatter.2
where the time goes:
time: 658 us; the launch traced here: 655 us
  waiting for transfers between devices  367 us (56%)
  blocking collectives  145 us (22%)
  starting transfers between devices  93.1 us (14%)
  local copies, waits for them, and re-layouts  21.2 us (3%)
  between operations  14.5 us (2%)
  matrix products  7.28 us (1%)
    reduce_scatter x2, waiting for transfers between devices, expert_pass(): lax.psum_scatter(contract(rows, w_down0, 1, 1), 'dp', scatter_dimension=0...  210 us
    all_gather x2, blocking collectives, expert_pass(): lax.all_gather(summed, 'dp', axis=0, tiled=True)  145 us
    all_to_all x2, waiting for transfers between devices, local(): lax.all_to_all(packed[m][0], 'expert', split_axis=0, concat_axis=0, tiled...  42.2 us
    all_to_all x2, starting transfers between devices, local(): lax.all_to_all(packed[m][0], 'expert', split_axis=0, concat_axis=0, tiled...  41.1 us
    all_to_all x2, waiting for transfers between devices, local(): lax.all_to_all(slot_probs.reshape(n_expert, cap), 'expert', split_axis=0,...  39.4 us
    all_to_all x2, waiting for transfers between devices, local(): lax.all_to_all(packed[m][1], 'expert', split_axis=0, concat_axis=0, tiled...  38.5 us
    all_to_all x2, waiting for transfers between devices, local(): lax.all_to_all(slot_rows.reshape(n_expert, cap, width), 'expert', split_a...  36.2 us
    all_to_all x2, starting transfers between devices, local(): lax.all_to_all(slot_probs.reshape(n_expert, cap), 'expert', split_axis=0,...  27.4 us
  transfers between devices with their start and end apart: 10, of which 10 were waited for; matrix products, arithmetic and copies ran while one was open for 2% of the time, Pallas kernels for 0%

commit v1 on v0

v1 whole, which is shorter than its diff:
```python
import jax
import jax.numpy as jnp
from jax import lax
from jax.sharding import Mesh
from jax.sharding import PartitionSpec as P

BF = jnp.bfloat16
F32 = jnp.float32
DP = ("zh", "x", "core")
EX = ("zl", "y")


def dot(a, b, ca, cb):
    return lax.dot_general(a, b, (((ca,), (cb,)), ((), ())), preferred_element_type=F32)


def silu_parts(g):
    sig = jax.nn.sigmoid(g)
    return g * sig, sig * (1.0 + g * (1.0 - sig))


def route_maps(ids_m, n_expert, cap):
    toks, top = ids_m.shape
    flat = ids_m.reshape(-1)
    hits = (flat[:, None] == jnp.arange(n_expert, dtype=jnp.int32)[None, :]).astype(jnp.int32)
    earlier = jnp.cumsum(hits, axis=0) - hits
    slot = jnp.sum(earlier * hits, axis=1)
    dest = slot * n_expert + flat
    placed = jnp.arange(n_expert * cap, dtype=jnp.int32)[:, None] == dest[None, :]
    token_map = jnp.sum(placed.reshape(n_expert * cap, toks, top).astype(jnp.int32), axis=2)
    return placed, token_map.astype(BF)


def local(out_grad, expert_ids, probs, saved_inputs, gate_pre, up_pre, w_gate, w_up, w_down):
    ne = lax.axis_size(EX)
    mb, toks, top = expert_ids.shape
    slots = saved_inputs.shape[2]
    cap = slots // ne
    width = out_grad.shape[2]
    ff = w_gate.shape[2]
    pad = 128
    line = cap * width + pad

    placed, tmap = zip(*[route_maps(expert_ids[m], ne, cap) for m in range(mb)])
    send = []
    for m in range(mb):
        rows = dot(tmap[m], out_grad[m], 1, 0).astype(BF)
        wts = jnp.sum(jnp.where(placed[m], probs[m].reshape(1, -1).astype(F32), 0.0), axis=1)
        wts = jnp.pad(wts.astype(BF).reshape(cap, ne).T, ((0, 0), (0, pad - cap)))
        parts = [rows[s * ne : (s + 1) * ne] for s in range(cap)] + [wts]
        send.append(jnp.concatenate(parts, axis=1))
    got = lax.all_to_all(jnp.stack(send, 1), EX, 0, 0, tiled=True)

    g = [got[:, m, : cap * width].reshape(slots, width) for m in range(mb)]
    p = [got[:, m, cap * width : cap * width + cap].reshape(slots).astype(F32) for m in range(mb)]
    g_all = jnp.concatenate(g, 0)
    p_all = jnp.concatenate(p, 0)

    part = dot(g_all, w_down[0], 1, 1)
    n_c, n_x = lax.axis_size("core"), lax.axis_size("x")
    r = part.shape[0]
    r_c = r // n_c
    r_x = r_c // n_x
    me_c, me_x = lax.axis_index("core"), lax.axis_index("x")
    t = lax.all_to_all(part.astype(BF).reshape(n_c, r_c, ff), "core", 0, 0, tiled=True)
    half = jnp.sum(t.astype(F32), axis=0)
    t = lax.all_to_all(half.astype(BF).reshape(n_x, r_x, ff), "x", 0, 0, tiled=True)
    eighth = jnp.sum(t.astype(F32), axis=0).astype(BF)
    other = lax.ppermute(eighth, "zh", [(0, 1), (1, 0)])
    u = eighth.astype(F32) + other.astype(F32)

    start = me_c * r_c + me_x * r_x
    gate_all = gate_pre[:, 0].reshape(r, ff)
    up_all = up_pre[:, 0].reshape(r, ff)
    gate_f = lax.dynamic_slice_in_dim(gate_all, start, r_x, 0).astype(F32)
    up_f = lax.dynamic_slice_in_dim(up_all, start, r_x, 0).astype(F32)
    w_f = lax.dynamic_slice_in_dim(p_all, start, r_x, 0)[:, None]
    act, slope = silu_parts(gate_f)
    slot_prob = jnp.sum(u * (act * up_f), axis=1, keepdims=True).astype(BF)
    dh = w_f * u
    dgate = (dh * up_f * slope).astype(BF)
    dup = (dh * act).astype(BF)
    mine = jnp.concatenate([dgate, dup, jnp.pad(slot_prob, ((0, 0), (0, pad - 1)))], axis=1)
    mine = jnp.broadcast_to(mine[None], (n_x,) + mine.shape)
    full = lax.all_to_all(mine, "x", 0, 0, tiled=True).reshape(r_c, -1)
    full = lax.all_gather(full, "core", axis=0, tiled=True)
    dgate, dup = full[:, :ff], full[:, ff : 2 * ff]
    slot_prob = full[:, 2 * ff]

    slot_rows = (dot(dgate, w_gate[0], 1, 1) + dot(dup, w_up[0], 1, 1)).astype(BF)
    back = []
    for m in range(mb):
        rows = slot_rows[m * slots : (m + 1) * slots].reshape(ne, cap * width)
        sp = slot_prob[m * slots : (m + 1) * slots].reshape(ne, cap)
        back.append(jnp.concatenate([rows, jnp.pad(sp, ((0, 0), (0, pad - cap)))], axis=1))
    home = lax.all_to_all(jnp.stack(back, 1), EX, 0, 0, tiled=True)

    x_all = saved_inputs[:, 0].reshape(r, width)
    grad_gate = dot(x_all, dgate, 0, 0).astype(BF)
    grad_up = dot(x_all, dup, 0, 0).astype(BF)
    gate_f = gate_all.astype(F32)
    hidden = gate_f * jax.nn.sigmoid(gate_f) * up_all.astype(F32)
    scaled = (p_all[:, None] * hidden).astype(BF)
    grad_down = dot(scaled, g_all, 0, 0).astype(BF)

    in_grad, prob_grad = [], []
    for m in range(mb):
        rows = jnp.concatenate(
            [home[:, m, s * width : (s + 1) * width] for s in range(cap)], axis=0
        )
        in_grad.append(dot(tmap[m], rows, 0, 0).astype(BF))
        sp = home[:, m, cap * width : cap * width + cap].T.reshape(-1, 1).astype(F32)
        prob_grad.append(
            jnp.sum(jnp.where(placed[m], sp, 0.0), axis=0).astype(BF).reshape(toks, top)
        )
    return (
        jnp.stack(in_grad, 0),
        jnp.stack(prob_grad, 0),
        grad_gate[None],
        grad_up[None],
        grad_down[None],
    )


def solution(mesh):
    n_dp, n_ex = mesh.devices.shape
    fine = Mesh(
        mesh.devices.reshape(2, n_dp // 4, 2, n_ex // 4, 4), ("zh", "x", "core", "zl", "y")
    )
    specs = (
        P(None, EX, DP),
        P(None, EX, None),
        P(None, EX, None),
        P(None, EX, None, DP),
        P(None, EX, None, None),
        P(None, EX, None, None),
        P(EX, DP, None),
        P(EX, DP, None),
        P(EX, None, DP),
    )
    return jax.shard_map(
        local,
        mesh=fine,
        in_specs=specs,
        out_specs=(specs[0], specs[1], specs[6], specs[7], specs[8]),
        check_vma=False,
    )
```

time: 658 us -> 248 us (0.38)
  waiting for transfers between devices: 367 us -> 81.1 us
  blocking collectives: 145 us -> 87.4 us
  starting transfers between devices: 93.1 us -> 36.6 us
  local copies, waits for them, and re-layouts: 21.2 us -> 10.5 us
    reduce_scatter x2 -> x0, waiting for transfers between devices: 210 us -> none  [expert_pass(): lax.psum_scatter(contract(rows, w_down0, 1, 1), 'dp', scatter_dimension=0...]
    all_gather x2 -> x0, blocking collectives: 145 us -> none  [expert_pass(): lax.all_gather(summed, 'dp', axis=0, tiled=True)]
    all_to_all x8 -> x2, waiting for transfers between devices: 156 us -> 33.5 us  [the longest x1 26.7 us: local(): home = lax.all_to_all(jnp.stack(back, 1), EX, 0, 0, tiled=True)]
    all_to_all x0 -> x3, blocking collectives: none -> 87.4 us  [the longest x1 61.8 us: local(): got = lax.all_to_all(jnp.stack(send, 1), EX, 0, 0, tiled=True)]
    all_to_all x8 -> x2, starting transfers between devices: 93 us -> 25.1 us  [the longest x1 21.1 us: local(): home = lax.all_to_all(jnp.stack(back, 1), EX, 0, 0, tiled=True)]
    ppermute x0 -> x1, waiting for transfers between devices: none -> 25 us  [local(): other = lax.ppermute(eighth, 'zh', [(0, 1), (1, 0)])]
    all_gather x0 -> x1, waiting for transfers between devices: none -> 22.6 us  [local(): full = lax.all_gather(full, 'core', axis=0, tiled=True)]
    ppermute x0 -> x1, starting transfers between devices: none -> 11.6 us  [local(): other = lax.ppermute(eighth, 'zh', [(0, 1), (1, 0)])]
  transfers between devices with their start and end apart: 10 -> 4, of which waited for: 10 -> 4; matrix products, arithmetic and copies ran while one was open for 2% -> 2% of each run, Pallas kernels for 0% -> 0%
where the time goes in v1:
time: 248 us; the launch traced here: 244 us
  blocking collectives  87.4 us (35%)
  waiting for transfers between devices  81.1 us (33%)
  starting transfers between devices  36.6 us (15%)
  between operations  14.5 us (6%)
  local copies, waits for them, and re-layouts  10.5 us (4%)
  matrix products  8.1 us (3%)
  other arithmetic  5.4 us (2%)
    all_to_all x1, blocking collectives, local(): got = lax.all_to_all(jnp.stack(send, 1), EX, 0, 0, tiled=True)  61.8 us
    all_to_all x1, waiting for transfers between devices, local(): home = lax.all_to_all(jnp.stack(back, 1), EX, 0, 0, tiled=True)  26.7 us
    ppermute x1, waiting for transfers between devices, local(): other = lax.ppermute(eighth, 'zh', [(0, 1), (1, 0)])  25 us
    all_gather x1, waiting for transfers between devices, local(): full = lax.all_gather(full, 'core', axis=0, tiled=True)  22.6 us
    all_to_all x1, starting transfers between devices, local(): home = lax.all_to_all(jnp.stack(back, 1), EX, 0, 0, tiled=True)  21.1 us
    all_to_all x1, blocking collectives, local(): full = lax.all_to_all(mine, 'x', 0, 0, tiled=True).reshape(r_c, -1)  15.7 us
    ppermute x1, starting transfers between devices, local(): other = lax.ppermute(eighth, 'zh', [(0, 1), (1, 0)])  11.6 us
    all_to_all x1, blocking collectives, local(): lax.all_to_all(part.astype(BF).reshape(n_c, r_c, ff), 'core', 0, 0, tiled...  9.89 us
  transfers between devices with their start and end apart: 4, of which 4 were waited for; matrix products, arithmetic and copies ran while one was open for 2% of the time, Pallas kernels for 0%

profile of v1, /device:TPU:1, one launch (start us, length us, event | category | flops | bytes accessed | tf_op | source)
XLA Modules:
  0.0 243.6 jit_solution(125812556257213982)
XLA Ops:
  7.2 0.8 slice_bitcast_fusion.1
  8.9 0.9 convolution_convert_fusion.4
  9.8 0.7 slice_convert_fusion.3
  11.9 0.9 convolution_convert_fusion.5
  13.5 0.3 copy.94
  13.8 61.8 %all_to_all.25 = bf16[64,2,1152]{2,1,0:T(2,128)(2,1)S(1)} all-to-all(bf16[64,2,1152]{2,1,0:T(2,128)(2,1)S(1)} %copy.94), channel_id=1, replica_groups=mesh['zh'=2,'x'=4,'core'=2,'zl'=16,'y'=4] {'zl','y'}, dimensions={0} | all-to-all | bytes 589824 | tf_op jit(solution)/shard_map/all_to_all | solution.py:52
  75.6 1.1 slice_reduce_fusion
  76.9 0.4 convolution_convert_fusion
  77.3 9.9 %all_to_all.26 = bf16[2,256,768]{2,1,0:T(8,128)(2,1)S(1)} all-to-all(bf16[2,256,768]{2,1,0:T(8,128)(2,1)S(1)} %bitcast.85), channel_id=1, replica_groups=mesh['zh'=2,'x'=4,'core'=2,'zl'=16,'y'=4] {'core'}, dimensions={0} | all-to-all | bytes 1572864 | tf_op jit(solution)/shard_map/all_to_all | solution.py:65
  87.2 1.0 reduce_sum.111
  88.2 4.0 %all-to-all-start.2 = ((bf16[4,64,768]{2,1,0:T(8,128)(2,1)}), bf16[4,64,768]{2,1,0:T(8,128)(2,1)S(1)}, u32[]{:S(2)}, u32[]{:S(2)}) async-start(bf16[4,64,768]{2,1,0:T(8,128)(2,1)} %bitcast.10), calls=%async_computation.2 | async-start | bytes 786432 | tf_op jit(solution)/shard_map/all_to_all | solution.py:67
  92.2 0.2 slice_reduce_fusion.5
  92.6 6.8 %all-to-all-done.2 = bf16[4,64,768]{2,1,0:T(8,128)(2,1)S(1)} async-done(((bf16[4,64,768]{2,1,0:T(8,128)(2,1)}), bf16[4,64,768]{2,1,0:T(8,128)(2,1)S(1)}, u32[]{:S(2)}, u32[]{:S(2)}) %all-to-all-start.2) | async-done | bytes 393248 | tf_op jit(solution)/shard_map/all_to_all | solution.py:67
  99.5 11.6 %collective-permute-start = (bf16[64,768]{1,0:T(8,128)(2,1)S(1)}, bf16[64,768]{1,0:T(8,128)(2,1)S(1)}, u32[]{:S(2)}, u32[]{:S(2)}) collective-permute-start(bf16[64,768]{1,0:T(8,128)(2,1)S(1)} %reduce_sum.112), channel_id=1, source_target_pairs={{0,512},{512,0},{1,513},{513,1},{2,514},{514,2},{3,515},{515,3},{4... | collective-permute-start | bytes 294920 | tf_op jit(solution)/shard_map/ppermute | solution.py:69
  111.2 25.0 %collective-permute-done = bf16[64,768]{1,0:T(8,128)(2,1)S(1)} collective-permute-done((bf16[64,768]{1,0:T(8,128)(2,1)S(1)}, bf16[64,768]{1,0:T(8,128)(2,1)S(1)}, u32[]{:S(2)}, u32[]{:S(2)}) %collective-permute-start) | collective-permute-done | bytes 98336 | tf_op jit(solution)/shard_map/ppermute | solution.py:69
  136.2 1.2 fusion.26
  137.6 15.7 %all_to_all.27 = bf16[4,64,1664]{2,1,0:T(8,128)(2,1)} all-to-all(bf16[4,64,1664]{2,1,0:T(8,128)(2,1)S(1)} %broadcast_in_dim.61), channel_id=1, replica_groups=mesh['zh'=2,'x'=4,'core'=2,'zl'=16,'y'=4] {'x'}, dimensions={0} | all-to-all | bytes 1703936 | tf_op jit(solution)/shard_map/all_to_all | solution.py:85
  153.3 22.6 %all-gather.2.cloned.1.call-done = bf16[512,1664]{1,0:T(8,128)(2,1)} async-done(((bf16[256,1664]{1,0:T(8,128)(2,1)}), bf16[512,1664]{1,0:T(8,128)(2,1)}) %all-gather.2.cloned.1.call-update) | async-done | bytes 1703952 | tf_op jit(solution)/shard_map/all_gather | solution.py:86
  176.0 1.1 slice_reduce_fusion.3
  177.2 1.5 fusion.16
  178.8 0.4 fusion.6
  179.6 1.0 copy.96
  180.6 21.1 %all-to-all-start.4 = ((bf16[64,2,1152]{2,1,0:T(2,128)(2,1)}), bf16[64,2,1152]{2,1,0:T(2,128)(2,1)S(1)}, u32[]{:S(2)}, u32[]{:S(2)}) async-start(bf16[64,2,1152]{2,1,0:T(2,128)(2,1)} %copy.96), calls=%async_computation.4 | async-start | bytes 589824 | tf_op jit(solution)/shard_map/all_to_all | solution.py:96
  201.7 2.8 %fusion.9 = bf16[1,768,256]{2,1,0:T(8,128)(2,1)} fusion(bf16[512,256]{1,0:T(8,128)(2,1)S(1)} %constant_dynamic-update-slice_fusion.2, bf16[512,768]{1,0:T(8,128)(2,1)} %bitcast.103, bf16[512,768]{1,0:T(8,128)(2,1)S(1)} %bitcast.101, f32[512]{0:T(512)S(1)} %maximum_convert_fusion), kind=kOutput, calls=%fused_computation.16 | convolution fusion | flops 205062144 | bytes 2230272 | tf_op jit(solution)/shard_map/dot_general | solution.py:14
  204.5 0.4 fusion.7
  204.9 0.9 copy.108
  205.8 0.4 fusion.8
  206.3 0.9 copy.109
  207.2 26.7 %all-to-all-done.4 = bf16[64,2,1152]{2,1,0:T(2,128)(2,1)S(1)} async-done(((bf16[64,2,1152]{2,1,0:T(2,128)(2,1)}), bf16[64,2,1152]{2,1,0:T(2,128)(2,1)S(1)}, u32[]{:S(2)}, u32[]{:S(2)}) %all-to-all-start.4) | async-done | bytes 294944 | tf_op jit(solution)/shard_map/all_to_all | solution.py:96
  233.8 0.4 fusion.68
  235.2 0.7 copy.107
  236.2 0.6 pad_maximum_fusion.2
  (96 shorter events, 5.3 us)
Async XLA Ops:
  7.2 69.7 %copy-start = (bf16[1,768,256]{2,1,0:T(8,128)(2,1)S(1)}, bf16[1,768,256]{2,1,0:T(8,128)(2,1)}, u32[]{:S(2)}) copy-start(bf16[1,768,256]{2,1,0:T(8,128)(2,1)} %param.17) | copy-start | bytes 1179652
  88.2 11.2 %all-to-all-start.2 = ((bf16[4,64,768]{2,1,0:T(8,128)(2,1)}), bf16[4,64,768]{2,1,0:T(8,128)(2,1)S(1)}, u32[]{:S(2)}, u32[]{:S(2)}) async-start(bf16[4,64,768]{2,1,0:T(8,128)(2,1)} %bitcast.10), calls=%async_computation.2 | async-start | bytes 786432 | tf_op jit(solution)/shard_map/all_to_all | solution.py:67
  92.2 83.7 %all-gather.2.cloned.1.call-start = ((), (), s32[]{:S(2)}) async-start(), calls=%async_computation.5 | async-start | bytes 2555904 | tf_op jit(solution)/shard_map/all_gather | solution.py:86
  99.5 36.7 %collective-permute-start = (bf16[64,768]{1,0:T(8,128)(2,1)S(1)}, bf16[64,768]{1,0:T(8,128)(2,1)S(1)}, u32[]{:S(2)}, u32[]{:S(2)}) collective-permute-start(bf16[64,768]{1,0:T(8,128)(2,1)S(1)} %reduce_sum.112), channel_id=1, source_target_pairs={{0,512},{512,0},{1,513},{513,1},{2,514},{514,2},{3,515},{515,3},{4... | collective-permute-start | bytes 294920 | tf_op jit(solution)/shard_map/ppermute | solution.py:69
  137.6 39.6 %copy-start.4 = (bf16[1,256,768]{2,1,0:T(8,128)(2,1)S(1)}, bf16[1,256,768]{2,1,0:T(8,128)(2,1)}, u32[]{:S(2)}) copy-start(bf16[1,256,768]{2,1,0:T(8,128)(2,1)} %param.15) | copy-start | bytes 1179652
  153.3 25.4 %copy-start.2 = (bf16[1,256,768]{2,1,0:T(8,128)(2,1)S(1)}, bf16[1,256,768]{2,1,0:T(8,128)(2,1)}, u32[]{:S(2)}) copy-start(bf16[1,256,768]{2,1,0:T(8,128)(2,1)} %param.16) | copy-start | bytes 1179652
  176.0 2.8 %copy-start.1 = (bf16[512,1664]{1,0:T(8,128)(2,1)S(1)}, bf16[512,1664]{1,0:T(8,128)(2,1)}, u32[]{:S(2)}) copy-start(bf16[512,1664]{1,0:T(8,128)(2,1)} %all-gather.2.cloned.1.call-done) | copy-start | bytes 5111812
  179.5 22.1 %copy-start.3 = (bf16[2,1,256,768]{3,2,1,0:T(8,128)(2,1)S(1)}, bf16[2,1,256,768]{3,2,1,0:T(8,128)(2,1)}, u32[]{:S(2)}) copy-start(bf16[2,1,256,768]{3,2,1,0:T(8,128)(2,1)} %param.13) | copy-start | bytes 2359300
  180.6 53.2 %all-to-all-start.4 = ((bf16[64,2,1152]{2,1,0:T(2,128)(2,1)}), bf16[64,2,1152]{2,1,0:T(2,128)(2,1)S(1)}, u32[]{:S(2)}, u32[]{:S(2)}) async-start(bf16[64,2,1152]{2,1,0:T(2,128)(2,1)} %copy.96), calls=%async_computation.4 | async-start | bytes 589824 | tf_op jit(solution)/shard_map/all_to_all | solution.py:96
  201.7 2.8 %copy-start.5 = (bf16[2,1,256,256]{3,2,1,0:T(8,128)(2,1)S(1)}, bf16[2,1,256,256]{3,2,1,0:T(8,128)(2,1)}, u32[]{:S(2)}) copy-start(bf16[2,1,256,256]{3,2,1,0:T(8,128)(2,1)} %param.12) | copy-start | bytes 786436
  204.5 1.4 copy-start.6
Sparse Core Ops, SparseCore 0:
  153.5 22.4 all-gather.1

commit v2 on v1

v2 whole, which is shorter than its diff:
```python
import jax
import jax.numpy as jnp
from jax import lax
from jax.sharding import Mesh
from jax.sharding import PartitionSpec as P

BF = jnp.bfloat16
F32 = jnp.float32
DP = ("zh", "x", "core")
EX = ("zl", "y")


def dot(a, b, ca, cb):
    return lax.dot_general(a, b, (((ca,), (cb,)), ((), ())), preferred_element_type=F32)


def silu_parts(g):
    sig = jax.nn.sigmoid(g)
    return g * sig, sig * (1.0 + g * (1.0 - sig))


def route_maps(ids_m, n_expert, cap):
    toks, top = ids_m.shape
    experts = jnp.arange(n_expert, dtype=jnp.int32)
    picks = (ids_m[:, :, None] == experts).astype(F32)
    hits = jnp.sum(picks, axis=1)
    earlier = jnp.tril(jnp.ones((toks, toks), F32), -1)
    slot = dot(earlier.astype(BF), hits.astype(BF), 1, 0)
    maps = [(hits * (slot == s)).astype(BF) for s in range(cap)]
    return picks, maps


def local(out_grad, expert_ids, probs, saved_inputs, gate_pre, up_pre, w_gate, w_up, w_down):
    ne = lax.axis_size(EX)
    mb, toks, top = expert_ids.shape
    slots = saved_inputs.shape[2]
    cap = slots // ne
    width = out_grad.shape[2]
    ff = w_gate.shape[2]
    pad = 128
    me_c = lax.axis_index("core")

    def turn(v):
        return jnp.where(me_c == 0, v, v[::-1])

    out_grad, expert_ids, probs = turn(out_grad), turn(expert_ids), turn(probs)
    saved_inputs, gate_pre, up_pre = turn(saved_inputs), turn(gate_pre), turn(up_pre)
    line = cap * width + pad

    picks, maps = zip(*[route_maps(expert_ids[m], ne, cap) for m in range(mb)])
    columns = jnp.arange(pad)
    send = []
    for m in range(mb):
        rows = [dot(k, out_grad[m], 0, 0).astype(BF) for k in maps[m]]
        prob = jnp.sum(picks[m] * probs[m].astype(F32)[:, :, None], axis=1).astype(BF)
        wts = sum(
            dot(k * prob, jnp.broadcast_to((columns == s).astype(BF), (toks, pad)), 0, 0)
            for s, k in enumerate(maps[m])
        )
        send.append(jnp.concatenate(rows + [wts.astype(BF)], axis=1))
    got = lax.all_to_all(jnp.stack(send, 1), EX, 0, 0, tiled=True)

    g = [got[:, m, : cap * width].reshape(slots, width) for m in range(mb)]
    p = [got[:, m, cap * width : cap * width + cap].reshape(slots).astype(F32) for m in range(mb)]
    g_all = jnp.concatenate(g, 0)
    p_all = jnp.concatenate(p, 0)

    n_x = lax.axis_size("x")
    r_x = slots // n_x
    swap = [(0, 1), (1, 0)]
    away = lax.ppermute(dot(g[1], w_down[0], 1, 1), "core", swap)
    half = dot(g[0], w_down[0], 1, 1) + away
    t = lax.all_to_all(half.astype(BF).reshape(n_x, r_x, ff), "x", 0, 0, tiled=True)
    eighth = jnp.sum(t.astype(F32), axis=0).astype(BF)
    other = lax.ppermute(eighth, "zh", swap)
    u = (eighth.astype(F32) + other.astype(F32)).astype(BF)
    u = jnp.broadcast_to(u[None], (n_x,) + u.shape)
    u_mine = lax.all_to_all(u, "x", 0, 0, tiled=True).reshape(slots, ff)
    u_all = [u_mine, lax.ppermute(u_mine, "core", swap)]

    dgates, dups, back = [], [], []
    for m in range(mb):
        gate_f = gate_pre[m, 0].astype(F32)
        up_f = up_pre[m, 0].astype(F32)
        act, slope = silu_parts(gate_f)
        u = u_all[m].astype(F32)
        slot_prob = jnp.sum(u * (act * up_f), axis=1).astype(BF)
        dh = p[m][:, None] * u
        dgate = (dh * up_f * slope).astype(BF)
        dup = (dh * act).astype(BF)
        rows = (dot(dgate, w_gate[0], 1, 1) + dot(dup, w_up[0], 1, 1)).astype(BF)
        sp = jnp.pad(slot_prob.reshape(ne, cap), ((0, 0), (0, pad - cap)))
        back.append(jnp.concatenate([rows.reshape(ne, cap * width), sp], axis=1))
        dgates.append(dgate)
        dups.append(dup)
    dgate = jnp.concatenate(dgates, 0)
    dup = jnp.concatenate(dups, 0)
    home = lax.all_to_all(jnp.stack(back, 1), EX, 0, 0, tiled=True)

    r = mb * slots
    x_all = saved_inputs[:, 0].reshape(r, width)
    grad_gate = dot(x_all, dgate, 0, 0).astype(BF)
    grad_up = dot(x_all, dup, 0, 0).astype(BF)
    gate_f = gate_pre[:, 0].reshape(r, ff).astype(F32)
    hidden = gate_f * jax.nn.sigmoid(gate_f) * up_pre[:, 0].reshape(r, ff).astype(F32)
    scaled = (p_all[:, None] * hidden).astype(BF)
    grad_down = dot(scaled, g_all, 0, 0).astype(BF)

    in_grad, prob_grad = [], []
    for m in range(mb):
        grads = sum(
            dot(k, home[:, m, s * width : (s + 1) * width], 1, 0) for s, k in enumerate(maps[m])
        )
        in_grad.append(grads.astype(BF))
        sp = home[:, m, cap * width : cap * width + cap].astype(F32)
        sp = sum(k.astype(F32) * sp[None, :, s] for s, k in enumerate(maps[m]))
        prob_grad.append(jnp.sum(picks[m] * sp[:, None, :], axis=2).astype(BF))
    return (
        turn(jnp.stack(in_grad, 0)),
        turn(jnp.stack(prob_grad, 0)),
        grad_gate[None],
        grad_up[None],
        grad_down[None],
    )


def solution(mesh):
    n_dp, n_ex = mesh.devices.shape
    fine = Mesh(
        mesh.devices.reshape(2, n_dp // 4, 2, n_ex // 4, 4), ("zh", "x", "core", "zl", "y")
    )
    specs = (
        P(None, EX, DP),
        P(None, EX, None),
        P(None, EX, None),
        P(None, EX, None, DP),
        P(None, EX, None, None),
        P(None, EX, None, None),
        P(EX, DP, None),
        P(EX, DP, None),
        P(EX, None, DP),
    )
    return jax.shard_map(
        local,
        mesh=fine,
        in_specs=specs,
        out_specs=(specs[0], specs[1], specs[6], specs[7], specs[8]),
        check_vma=False,
    )
```

time: 248 us -> 203 us (0.82)
  blocking collectives: 87.4 us -> 61.8 us
  waiting for transfers between devices: 81.1 us -> 66.7 us
  between operations: 14.5 us -> 1.22 us
  other arithmetic: 5.4 us -> 13.3 us
    all_to_all x2 -> x0, blocking collectives: 25.6 us -> none  [the longest x1 15.7 us: local(): full = lax.all_to_all(mine, 'x', 0, 0, tiled=True).reshape(r_c, -1)]
    all_gather x1 -> x0, waiting for transfers between devices: 22.6 us -> none  [local(): full = lax.all_gather(full, 'core', axis=0, tiled=True)]
    all_to_all x1, starting transfers between devices: 21.1 us -> 8.26 us  [local(): home = lax.all_to_all(jnp.stack(back, 1), EX, 0, 0, tiled=True)]
    ppermute x1 -> x3, starting transfers between devices: 11.6 us -> 22.7 us  [the longest x1 11.6 us: local(): other = lax.ppermute(eighth, 'zh', swap)]
    all_to_all x0 -> x1, waiting for transfers between devices: none -> 7.07 us  [local(): u_mine = lax.all_to_all(u, 'x', 0, 0, tiled=True).reshape(slots, ff)]
    select_n x0 -> x7, other arithmetic: none -> 5.29 us  [turn(): return jnp.where(me_c == 0, v, v[::-1])]
    convert_element_type x1 -> x2, other arithmetic: 1.2 us -> 4.78 us  [local(): dgate = (dh * up_f * slope).astype(BF)]
    all_to_all x0 -> x1, starting transfers between devices: none -> 3.46 us  [local(): u_mine = lax.all_to_all(u, 'x', 0, 0, tiled=True).reshape(slots, ff)]
  transfers between devices with their start and end apart: 4 -> 6, of which waited for: 4 -> 5; matrix products, arithmetic and copies ran while one was open for 2% -> 5% of each run, Pallas kernels for 0% -> 0%
where the time goes in v2:
time: 203 us; the launch traced here: 200 us
  waiting for transfers between devices  66.7 us (33%)
  blocking collectives  61.8 us (30%)
  starting transfers between devices  38.5 us (19%)
  other arithmetic  13.3 us (7%)
  matrix products  10.3 us (5%)
  local copies, waits for them, and re-layouts  8.03 us (4%)
    all_to_all x1, blocking collectives, local(): got = lax.all_to_all(jnp.stack(send, 1), EX, 0, 0, tiled=True)  61.8 us
    all_to_all x1, waiting for transfers between devices, local(): home = lax.all_to_all(jnp.stack(back, 1), EX, 0, 0, tiled=True)  28.2 us
    ppermute x1, waiting for transfers between devices, local(): other = lax.ppermute(eighth, 'zh', swap)  24.2 us
    ppermute x1, starting transfers between devices, local(): other = lax.ppermute(eighth, 'zh', swap)  11.6 us
    dot_general x35, matrix products, dot(): lax.dot_general(a, b, (((ca,), (cb,)), ((), ())), preferred_element_type=...  10.3 us
    all_to_all x1, starting transfers between devices, local(): home = lax.all_to_all(jnp.stack(back, 1), EX, 0, 0, tiled=True)  8.26 us
    ppermute x1, starting transfers between devices, local(): away = lax.ppermute(dot(g[1], w_down[0], 1, 1), 'core', swap)  7.81 us
    all_to_all x1, waiting for transfers between devices, local(): u_mine = lax.all_to_all(u, 'x', 0, 0, tiled=True).reshape(slots, ff)  7.07 us
  transfers between devices with their start and end apart: 6, of which 5 were waited for; matrix products, arithmetic and copies ran while one was open for 5% of the time, Pallas kernels for 0%

profile of v2, /device:TPU:1, one launch (start us, length us, event | category | flops | bytes accessed | tf_op | source)
XLA Modules:
  0.0 199.9 jit_solution(9954959463947525885)
XLA Ops:
  0.7 0.8 reverse_select_fusion.5
  1.6 0.8 reverse_select_fusion.7
  2.4 0.8 reverse_select_fusion.4
  7.4 61.8 %all_to_all.20 = bf16[64,2,1152]{2,1,0:T(2,128)(2,1)S(1)} all-to-all(bf16[64,2,1152]{2,1,0:T(2,128)(2,1)S(1)} %copy.67), channel_id=1, replica_groups=mesh['zh'=2,'x'=4,'core'=2,'zl'=16,'y'=4] {'zl','y'}, dimensions={0} | all-to-all | bytes 589824 | tf_op jit(solution)/shard_map/all_to_all | solution.py:61
  69.2 1.1 slice_reduce_fusion.1
  70.4 0.6 copy-done.8
  71.3 7.8 %collective-permute-start = (f32[256,768]{1,0:T(8,128)S(1)}, f32[256,768]{1,0:T(8,128)S(1)}, u32[]{:S(2)}, u32[]{:S(2)}) collective-permute-start(f32[256,768]{1,0:T(8,128)S(1)} %fusion.66), channel_id=1, source_target_pairs={{0,64},{64,0},{1,65},{65,1},{2,66},{66,2},{3,67},{67,3},{4,68},{68... | collective-permute-start | bytes 2359304 | tf_op jit(solution)/shard_map/ppermute | solution.py:71
  79.3 1.8 collective-permute-done
  81.0 1.0 fusion.6
  82.1 4.1 %all-to-all-start.1 = ((bf16[4,64,768]{2,1,0:T(8,128)(2,1)}), bf16[4,64,768]{2,1,0:T(8,128)(2,1)S(1)}, u32[]{:S(2)}, u32[]{:S(2)}) async-start(bf16[4,64,768]{2,1,0:T(8,128)(2,1)} %bitcast.9), calls=%async_computation.1 | async-start | bytes 786432 | tf_op jit(solution)/shard_map/all_to_all | solution.py:73
  86.2 1.7 reverse_select_fusion
  88.0 5.5 %all-to-all-done.1 = bf16[4,64,768]{2,1,0:T(8,128)(2,1)S(1)} async-done(((bf16[4,64,768]{2,1,0:T(8,128)(2,1)}), bf16[4,64,768]{2,1,0:T(8,128)(2,1)S(1)}, u32[]{:S(2)}, u32[]{:S(2)}) %all-to-all-start.1) | async-done | bytes 393248 | tf_op jit(solution)/shard_map/all_to_all | solution.py:73
  93.5 11.6 %collective-permute-start.1 = (bf16[64,768]{1,0:T(8,128)(2,1)S(1)}, bf16[64,768]{1,0:T(8,128)(2,1)S(1)}, u32[]{:S(2)}, u32[]{:S(2)}) collective-permute-start(bf16[64,768]{1,0:T(8,128)(2,1)S(1)} %reduce_sum.88), channel_id=1, source_target_pairs={{0,512},{512,0},{1,513},{513,1},{2,514},{514,2},{3,515},{515,3},{4... | collective-permute-start | bytes 294920 | tf_op jit(solution)/shard_map/ppermute | solution.py:75
  105.1 0.9 slice_convert_fusion
  106.0 24.2 %collective-permute-done.1 = bf16[64,768]{1,0:T(8,128)(2,1)S(1)} collective-permute-done((bf16[64,768]{1,0:T(8,128)(2,1)S(1)}, bf16[64,768]{1,0:T(8,128)(2,1)S(1)}, u32[]{:S(2)}, u32[]{:S(2)}) %collective-permute-start.1) | collective-permute-done | bytes 98336 | tf_op jit(solution)/shard_map/ppermute | solution.py:75
  130.2 0.8 broadcast_in_dim.58
  131.0 3.5 %all-to-all-start.2 = ((bf16[4,64,768]{2,1,0:T(8,128)(2,1)}), bf16[4,64,768]{2,1,0:T(8,128)(2,1)S(1)}, u32[]{:S(2)}, u32[]{:S(2)}) async-start(bf16[4,64,768]{2,1,0:T(8,128)(2,1)} %broadcast_in_dim.58), calls=%async_computation.2 | async-start | bytes 786432 | tf_op jit(solution)/shard_map/all_to_all | solution.py:78
  135.0 7.1 %all-to-all-done.2 = bf16[4,64,768]{2,1,0:T(8,128)(2,1)S(1)} async-done(((bf16[4,64,768]{2,1,0:T(8,128)(2,1)}), bf16[4,64,768]{2,1,0:T(8,128)(2,1)S(1)}, u32[]{:S(2)}, u32[]{:S(2)}) %all-to-all-start.2) | async-done | bytes 393248 | tf_op jit(solution)/shard_map/all_to_all | solution.py:78
  142.1 3.3 %collective-permute-start.2 = (bf16[256,768]{1,0:T(8,128)(2,1)S(1)}, bf16[256,768]{1,0:T(8,128)(2,1)}, u32[]{:S(2)}, u32[]{:S(2)}) collective-permute-start(bf16[256,768]{1,0:T(8,128)(2,1)S(1)} %bitcast.180), channel_id=1, source_target_pairs={{0,64},{64,0},{1,65},{65,1},{2,66},{66,2},{3,67},{67,3},{4,68},{68... | collective-permute-start | bytes 1179656 | tf_op jit(solution)/shard_map/ppermute | solution.py:79
  145.4 1.8 fusion.33
  147.5 0.7 copy-done.3
  148.7 0.7 fusion.75
  149.4 3.0 %fusion.38 = (bf16[256,768]{1,0:T(8,128)(2,1)S(1)}, bf16[256]{0:T(256)(128)(2,1)S(1)}, bf16[256,768]{1,0:T(8,128)(2,1)}, bf16[256,768]{1,0:T(8,128)(2,1)S(1)}, bf16[256,768]{1,0:T(8,128)(2,1)}) fusion(bf16[256,768]{1,0:T(8,128)(2,1)} %collective-permute-done.2, f32[256]{0:T(256)S(1)} %reshape.137, bf16[2,1,256,768]{3,2,1,0:T(8,128)(2,1)S(1)} %get-tuple-element.52, ...), kind=kLoop, calls=%fused_computation.77 | loop fusion | flops 7274240 | bytes 3934720 | tf_op jit(solution)/shard_map/convert_element_type | solution.py:89
  154.1 1.0 copy.68
  155.1 8.3 %all-to-all-start.3 = ((bf16[64,2,1152]{2,1,0:T(2,128)(2,1)}), bf16[64,2,1152]{2,1,0:T(2,128)(2,1)S(1)}, u32[]{:S(2)}, u32[]{:S(2)}) async-start(bf16[64,2,1152]{2,1,0:T(2,128)(2,1)} %copy.68), calls=%async_computation.3 | async-start | bytes 589824 | tf_op jit(solution)/shard_map/all_to_all | solution.py:98
  163.4 0.5 fusion.5
  164.4 1.2 fusion.9
  165.6 1.1 fusion.8
  166.8 1.1 fusion.7
  167.9 28.2 %all-to-all-done.3 = bf16[64,2,1152]{2,1,0:T(2,128)(2,1)S(1)} async-done(((bf16[64,2,1152]{2,1,0:T(2,128)(2,1)}), bf16[64,2,1152]{2,1,0:T(2,128)(2,1)S(1)}, u32[]{:S(2)}, u32[]{:S(2)}) %all-to-all-start.3) | async-done | bytes 294944 | tf_op jit(solution)/shard_map/all_to_all | solution.py:98
  197.2 0.6 reverse_select_fusion.6
  199.3 0.6 reverse_select_fusion.3
  (137 shorter events, 10.8 us)
Async XLA Ops:
  0.6 70.4 %copy-start = (bf16[1,768,256]{2,1,0:T(8,128)(2,1)S(1)}, bf16[1,768,256]{2,1,0:T(8,128)(2,1)}, u32[]{:S(2)}) copy-start(bf16[1,768,256]{2,1,0:T(8,128)(2,1)} %param.17) | copy-start | bytes 1179652
  3.7 1.1 copy-start.27
  3.7 3.3 %copy-start.17 = (bf16[16,64]{1,0:T(8,128)(2,1)}, bf16[16,64]{1,0:T(8,128)(2,1)S(1)}, u32[]{:S(2)}) copy-start(bf16[16,64]{1,0:T(8,128)(2,1)S(1)} %get-tuple-element.39) | copy-start | bytes 6148
  3.7 3.3 %copy-start.21 = (bf16[16,64]{1,0:T(8,128)(2,1)}, bf16[16,64]{1,0:T(8,128)(2,1)S(1)}, u32[]{:S(2)}) copy-start(bf16[16,64]{1,0:T(8,128)(2,1)S(1)} %get-tuple-element.40) | copy-start | bytes 6148
  3.7 3.3 %copy-start.25 = (bf16[16,64]{1,0:T(8,128)(2,1)}, bf16[16,64]{1,0:T(8,128)(2,1)S(1)}, u32[]{:S(2)}) copy-start(bf16[16,64]{1,0:T(8,128)(2,1)S(1)} %get-tuple-element.41) | copy-start | bytes 6148
  4.0 3.0 %copy-start.15 = (bf16[16,64]{1,0:T(8,128)(2,1)}, bf16[16,64]{1,0:T(8,128)(2,1)S(1)}, u32[]{:S(2)}) copy-start(bf16[16,64]{1,0:T(8,128)(2,1)S(1)} %get-tuple-element.43) | copy-start | bytes 6148
  4.0 3.0 %copy-start.19 = (bf16[16,64]{1,0:T(8,128)(2,1)}, bf16[16,64]{1,0:T(8,128)(2,1)S(1)}, u32[]{:S(2)}) copy-start(bf16[16,64]{1,0:T(8,128)(2,1)S(1)} %get-tuple-element.44) | copy-start | bytes 6148
  4.0 3.0 %copy-start.23 = (bf16[16,64]{1,0:T(8,128)(2,1)}, bf16[16,64]{1,0:T(8,128)(2,1)S(1)}, u32[]{:S(2)}) copy-start(bf16[16,64]{1,0:T(8,128)(2,1)S(1)} %get-tuple-element.45) | copy-start | bytes 6148
  71.3 9.7 %collective-permute-start = (f32[256,768]{1,0:T(8,128)S(1)}, f32[256,768]{1,0:T(8,128)S(1)}, u32[]{:S(2)}, u32[]{:S(2)}) collective-permute-start(f32[256,768]{1,0:T(8,128)S(1)} %fusion.66), channel_id=1, source_target_pairs={{0,64},{64,0},{1,65},{65,1},{2,66},{66,2},{3,67},{67,3},{4,68},{68... | collective-permute-start | bytes 2359304 | tf_op jit(solution)/shard_map/ppermute | solution.py:71
  79.2 2.8 %copy-start.10 = (bf16[256,256]{1,0:T(8,128)(2,1)}, bf16[256,256]{1,0:T(8,128)(2,1)S(1)}, u32[]{:S(2)}) copy-start(bf16[256,256]{1,0:T(8,128)(2,1)S(1)} %reshape_squeeze.6) | copy-start | bytes 393220
  82.1 4.2 %copy-start.6 = (bf16[2,1,256,768]{3,2,1,0:T(8,128)(2,1)S(1)}, bf16[2,1,256,768]{3,2,1,0:T(8,128)(2,1)}, u32[]{:S(2)}) copy-start(bf16[2,1,256,768]{3,2,1,0:T(8,128)(2,1)} %param.13) | copy-start | bytes 2359300
  82.1 11.4 %all-to-all-start.1 = ((bf16[4,64,768]{2,1,0:T(8,128)(2,1)}), bf16[4,64,768]{2,1,0:T(8,128)(2,1)S(1)}, u32[]{:S(2)}, u32[]{:S(2)}) async-start(bf16[4,64,768]{2,1,0:T(8,128)(2,1)} %bitcast.9), calls=%async_computation.1 | async-start | bytes 786432 | tf_op jit(solution)/shard_map/all_to_all | solution.py:73
  93.5 36.7 %collective-permute-start.1 = (bf16[64,768]{1,0:T(8,128)(2,1)S(1)}, bf16[64,768]{1,0:T(8,128)(2,1)S(1)}, u32[]{:S(2)}, u32[]{:S(2)}) collective-permute-start(bf16[64,768]{1,0:T(8,128)(2,1)S(1)} %reduce_sum.88), channel_id=1, source_target_pairs={{0,512},{512,0},{1,513},{513,1},{2,514},{514,2},{3,515},{515,3},{4... | collective-permute-start | bytes 294920 | tf_op jit(solution)/shard_map/ppermute | solution.py:75
  131.0 11.1 %all-to-all-start.2 = ((bf16[4,64,768]{2,1,0:T(8,128)(2,1)}), bf16[4,64,768]{2,1,0:T(8,128)(2,1)S(1)}, u32[]{:S(2)}, u32[]{:S(2)}) async-start(bf16[4,64,768]{2,1,0:T(8,128)(2,1)} %broadcast_in_dim.58), calls=%async_computation.2 | async-start | bytes 786432 | tf_op jit(solution)/shard_map/all_to_all | solution.py:78
  142.1 7.3 %collective-permute-start.2 = (bf16[256,768]{1,0:T(8,128)(2,1)S(1)}, bf16[256,768]{1,0:T(8,128)(2,1)}, u32[]{:S(2)}, u32[]{:S(2)}) collective-permute-start(bf16[256,768]{1,0:T(8,128)(2,1)S(1)} %bitcast.180), channel_id=1, source_target_pairs={{0,64},{64,0},{1,65},{65,1},{2,66},{66,2},{3,67},{67,3},{4,68},{68... | collective-permute-start | bytes 1179656 | tf_op jit(solution)/shard_map/ppermute | solution.py:79
  145.4 1.8 copy-start.1
  147.2 1.0 copy-start.3
  149.4 3.0 %copy-start.2 = (bf16[1,256,768]{2,1,0:T(8,128)(2,1)S(1)}, bf16[1,256,768]{2,1,0:T(8,128)(2,1)}, u32[]{:S(2)}) copy-start(bf16[1,256,768]{2,1,0:T(8,128)(2,1)} %param.15) | copy-start | bytes 1179652
  154.0 9.3 %copy-start.14 = (bf16[2,1,256,256]{3,2,1,0:T(8,128)(2,1)S(1)}, bf16[2,1,256,256]{3,2,1,0:T(8,128)(2,1)}, u32[]{:S(2)}) copy-start(bf16[2,1,256,256]{3,2,1,0:T(8,128)(2,1)} %param.12) | copy-start | bytes 786436
  155.1 41.0 %all-to-all-start.3 = ((bf16[64,2,1152]{2,1,0:T(2,128)(2,1)}), bf16[64,2,1152]{2,1,0:T(2,128)(2,1)S(1)}, u32[]{:S(2)}, u32[]{:S(2)}) async-start(bf16[64,2,1152]{2,1,0:T(2,128)(2,1)} %copy.68), calls=%async_computation.3 | async-start | bytes 589824 | tf_op jit(solution)/shard_map/all_to_all | solution.py:98
  163.4 1.0 copy-start.11
  164.4 1.2 copy-start.5
  164.4 1.2 copy-start.13
  165.6 1.1 copy-start.12
  166.7 29.6 %copy-start.18 = (bf16[16,64]{1,0:T(8,128)(2,1)S(1)}, bf16[16,64]{1,0:T(8,128)(2,1)}, u32[]{:S(2)}) copy-start(bf16[16,64]{1,0:T(8,128)(2,1)} %copy-done.17) | copy-start | bytes 6148
  166.7 29.6 %copy-start.22 = (bf16[16,64]{1,0:T(8,128)(2,1)S(1)}, bf16[16,64]{1,0:T(8,128)(2,1)}, u32[]{:S(2)}) copy-start(bf16[16,64]{1,0:T(8,128)(2,1)} %copy-done.21) | copy-start | bytes 6148
  166.7 29.7 %copy-start.26 = (bf16[16,64]{1,0:T(8,128)(2,1)S(1)}, bf16[16,64]{1,0:T(8,128)(2,1)}, u32[]{:S(2)}) copy-start(bf16[16,64]{1,0:T(8,128)(2,1)} %copy-done.25) | copy-start | bytes 6148
  166.7 29.7 %copy-start.28 = (bf16[16,64]{1,0:T(8,128)(2,1)S(1)}, bf16[16,64]{1,0:T(8,128)(2,1)}, u32[]{:S(2)}) copy-start(bf16[16,64]{1,0:T(8,128)(2,1)} %copy-done.27) | copy-start | bytes 6148
  166.7 30.2 %copy-start.16 = (bf16[16,64]{1,0:T(8,128)(2,1)S(1)}, bf16[16,64]{1,0:T(8,128)(2,1)}, u32[]{:S(2)}) copy-start(bf16[16,64]{1,0:T(8,128)(2,1)} %copy-done.15) | copy-start | bytes 6148
  166.7 30.2 %copy-start.20 = (bf16[16,64]{1,0:T(8,128)(2,1)S(1)}, bf16[16,64]{1,0:T(8,128)(2,1)}, u32[]{:S(2)}) copy-start(bf16[16,64]{1,0:T(8,128)(2,1)} %copy-done.19) | copy-start | bytes 6148
  166.7 30.2 %copy-start.24 = (bf16[16,64]{1,0:T(8,128)(2,1)S(1)}, bf16[16,64]{1,0:T(8,128)(2,1)}, u32[]{:S(2)}) copy-start(bf16[16,64]{1,0:T(8,128)(2,1)} %copy-done.23) | copy-start | bytes 6148
  166.8 30.2 %copy-start.30 = (bf16[16,64]{1,0:T(8,128)(2,1)S(1)}, bf16[16,64]{1,0:T(8,128)(2,1)}, u32[]{:S(2)}) copy-start(bf16[16,64]{1,0:T(8,128)(2,1)} %copy-done.29) | copy-start | bytes 6148
  (5 other events, 3.9 us)

commit v3 on v2

v3 whole, which is shorter than its diff:
```python
import functools

import jax
import jax.numpy as jnp
from jax import lax
from jax.experimental import pallas as pl
from jax.experimental.pallas import tpu as pltpu
from jax.sharding import Mesh
from jax.sharding import PartitionSpec as P

BF = jnp.bfloat16
F32 = jnp.float32
DP = ("zh", "x", "core")
EX = ("zl", "y")
PAD = 128
SWAP = [(0, 1), (1, 0)]
VMEM = pl.BlockSpec(memory_space=pltpu.VMEM)
SMEM = pl.BlockSpec(memory_space=pltpu.SMEM)


def dot(a, b, ca, cb):
    return lax.dot_general(a, b, (((ca,), (cb,)), ((), ())), preferred_element_type=F32)


def iota(shape, dim):
    return lax.broadcasted_iota(jnp.int32, shape, dim)


def call(body, outs, n_in, flops, bytes_moved, limit=24, has_me=True):
    first = [SMEM] if has_me else []
    return pl.pallas_call(
        body,
        out_shape=outs,
        in_specs=first + [VMEM] * n_in,
        out_specs=[VMEM] * len(outs),
        cost_estimate=pl.CostEstimate(flops=flops, bytes_accessed=bytes_moved, transcendentals=0),
        compiler_params=pltpu.CompilerParams(vmem_limit_bytes=limit << 20),
    )


def route_maps(ids, ne, cap):
    toks, top = ids.shape
    experts = iota((toks, ne), 1)
    picks = [(ids[:, k : k + 1] == experts).astype(F32) for k in range(top)]
    hits = functools.reduce(jnp.add, picks)
    lower = (iota((toks, toks), 0) > iota((toks, toks), 1)).astype(F32)
    slot = dot(lower.astype(BF), hits.astype(BF), 1, 0)
    maps = [jnp.where(slot == s, hits, 0.0) for s in range(cap)]
    return picks, maps


def pack_kernel(ne, cap, me, ids, probs, rows, out):
    mb, toks, width = rows.shape
    line = cap * width + PAD
    for m in range(mb):
        at = me[0] ^ m
        picks, maps = route_maps(ids[at], ne, cap)
        prob = probs[at].astype(F32)
        held = functools.reduce(
            jnp.add, [k * prob[:, i : i + 1] for i, k in enumerate(picks)]
        )
        tail = jnp.zeros((ne, PAD), F32)
        grads = rows[at]
        for s, k in enumerate(maps):
            base = m * line + s * width
            out[:, base : base + width] = dot(k.astype(BF), grads, 0, 0).astype(BF)
            column = (iota((toks, PAD), 1) == s).astype(BF)
            tail = tail + dot((k * held).astype(BF), column, 0, 0)
        base = m * line + cap * width
        out[:, base : base + PAD] = tail.astype(BF)


def spread(ne, cap, s):
    shape = (ne * cap, ne)
    return (iota(shape, 0) == iota(shape, 1) * cap + s).astype(BF)


def down_kernel(ne, cap, m, got, w_down, part, rows, probs):
    width = rows.shape[1]
    base = m * (cap * width + PAD)
    total = jnp.zeros(rows.shape, F32)
    for s in range(cap):
        total = total + dot(
            spread(ne, cap, s), got[:, base + s * width : base + (s + 1) * width], 1, 0
        )
    mine = total.astype(BF)
    rows[...] = mine
    part[...] = dot(mine, w_down[...], 1, 1)
    shape = (ne * cap, ne)
    source = iota(shape, 0)
    repeat = ((source >= iota(shape, 1) * cap) & (source < (iota(shape, 1) + 1) * cap)).astype(BF)
    tail = dot(repeat, got[:, base + cap * width : base + cap * width + PAD], 1, 0)
    shape = (ne * cap, PAD)
    probs[...] = jnp.sum(
        jnp.where(iota(shape, 1) == lax.rem(iota(shape, 0), cap), tail, 0.0), axis=1, keepdims=True
    )


def act_kernel(me, gate, up, probs0, probs1, rows0, rows1, f_gate, f_up, hidden, grad):
    total = None
    for m, (probs, rows) in enumerate(((probs0, rows0), (probs1, rows1))):
        gate_f = gate[me[0] ^ m].astype(F32)
        up_f = up[me[0] ^ m].astype(F32)
        p = probs[...]
        sig = 1.0 / (1.0 + jnp.exp(-gate_f))
        act = gate_f * sig
        h = act * up_f
        f_gate[m] = p * up_f * (sig * (1.0 + gate_f * (1.0 - sig)))
        f_up[m] = p * act
        hidden[m] = h
        term = dot((p * h).astype(BF), rows[...], 0, 0)
        total = term if total is None else total + term
    grad[...] = total.astype(BF)


def slot_kernel(ne, cap, m, u_ref, f_gate, f_up, hidden, w_gate, w_up, dgate, dup, out):
    u = u_ref[...].astype(F32)
    dg = (u * f_gate[m]).astype(BF)
    du = (u * f_up[m]).astype(BF)
    dgate[...] = dg
    dup[...] = du
    rows = (dot(dg, w_gate[...], 1, 1) + dot(du, w_up[...], 1, 1)).astype(BF)
    width = rows.shape[1]
    for s in range(cap):
        out[:, s * width : (s + 1) * width] = dot(spread(ne, cap, s), rows, 0, 0).astype(BF)
    slot_prob = jnp.sum(u * hidden[m], axis=1, keepdims=True)
    shape = (ne * cap, PAD)
    tail = jnp.where(iota(shape, 1) == lax.rem(iota(shape, 0), cap), slot_prob, 0.0).astype(BF)
    shape = (ne, ne * cap)
    slot = iota(shape, 1)
    gather = ((slot >= iota(shape, 0) * cap) & (slot < (iota(shape, 0) + 1) * cap)).astype(BF)
    out[:, cap * width :] = dot(gather, tail, 1, 0).astype(BF)


def weight_kernel(me, inputs, dgate0, dup0, dgate1, dup1, grad_gate, grad_up):
    first, second = inputs[me[0]], inputs[me[0] ^ 1]
    grad_gate[...] = (dot(first, dgate0[...], 0, 0) + dot(second, dgate1[...], 0, 0)).astype(BF)
    grad_up[...] = (dot(first, dup0[...], 0, 0) + dot(second, dup1[...], 0, 0)).astype(BF)


def unpack_kernel(ne, cap, me, ids, home, in_grad, prob_grad):
    mb, toks, width = in_grad.shape
    top = ids.shape[2]
    line = cap * width + PAD
    for m in range(mb):
        at = me[0] ^ m
        picks, maps = route_maps(ids[at], ne, cap)
        total = jnp.zeros((toks, width), F32)
        held = jnp.zeros((toks, ne), F32)
        tail = home[:, m * line + cap * width : (m + 1) * line]
        for s, k in enumerate(maps):
            base = m * line + s * width
            total = total + dot(k.astype(BF), home[:, base : base + width], 1, 0)
            column = (iota((toks, PAD), 1) == s).astype(BF)
            held = held + k * dot(column, tail, 1, 1)
        in_grad[at] = total.astype(BF)
        lane = iota((toks, top), 1)
        picked = jnp.zeros((toks, top), F32)
        for i, k in enumerate(picks):
            picked = jnp.where(lane == i, jnp.sum(k * held, axis=1, keepdims=True), picked)
        prob_grad[at] = picked.astype(BF)


def local(out_grad, expert_ids, probs, saved_inputs, gate_pre, up_pre, w_gate, w_up, w_down):
    sds = jax.ShapeDtypeStruct
    ne = lax.axis_size(EX)
    n_x = lax.axis_size("x")
    mb, toks, top = expert_ids.shape
    slots = saved_inputs.shape[2]
    cap = slots // ne
    width = out_grad.shape[2]
    ff = w_gate.shape[2]
    line = cap * width + PAD
    w_gate, w_up, w_down = w_gate[0], w_up[0], w_down[0]
    core = lax.axis_index("core")
    me = core.astype(jnp.int32).reshape(1)
    product = 2 * slots * width * ff

    send = call(
        functools.partial(pack_kernel, ne, cap),
        [sds((ne, mb * line), BF)],
        3,
        product // 8,
        ne * mb * line * 2,
    )(me, expert_ids, probs, out_grad)[0]
    got = lax.all_to_all(send.reshape(ne, mb, line), EX, 0, 0, tiled=True).reshape(ne, mb * line)

    def down(m):
        return call(
            functools.partial(down_kernel, ne, cap, m),
            [sds((slots, ff), F32), sds((slots, width), BF), sds((slots, 1), F32)],
            2,
            product,
            slots * ff * 4,
            has_me=False,
        )(got, w_down)

    part1, rows1, probs1 = down(1)
    away = lax.ppermute(part1, "core", SWAP)
    part0, rows0, probs0 = down(0)
    half = (part0 + away).astype(BF).reshape(n_x, slots // n_x, ff)
    half = lax.all_to_all(half, "x", 0, 0, tiled=True)
    eighth = jnp.sum(half.astype(F32), axis=0).astype(BF)
    both = lax.all_to_all(jnp.broadcast_to(eighth[None], (2,) + eighth.shape), "zh", 0, 0, tiled=True)

    f_gate, f_up, hidden, grad_down = call(
        act_kernel,
        [sds((mb, slots, ff), F32)] * 3 + [sds((ff, width), BF)],
        6,
        2 * product,
        mb * slots * ff * 16,
        limit=32,
    )(me, gate_pre[:, 0], up_pre[:, 0], probs0, probs1, rows0, rows1)

    u = jnp.sum(both.astype(F32), axis=0).astype(BF)
    u = jnp.broadcast_to(u[None], (n_x,) + u.shape)
    u0 = lax.all_to_all(u, "x", 0, 0, tiled=True).reshape(slots, ff)
    u1 = lax.ppermute(u0, "core", SWAP)

    def slot(m, u_m):
        return call(
            functools.partial(slot_kernel, ne, cap, m),
            [sds((slots, ff), BF), sds((slots, ff), BF), sds((ne, line), BF)],
            6,
            2 * product,
            slots * ff * 16,
            has_me=False,
        )(u_m, f_gate, f_up, hidden, w_gate, w_up)

    dgate0, dup0, back0 = slot(0, u0)
    dgate1, dup1, back1 = slot(1, u1)
    back = jnp.stack([back0, back1], axis=1)
    home = lax.all_to_all(back, EX, 0, 0, tiled=True).reshape(ne, mb * line)
    grad_gate, grad_up = call(
        weight_kernel, [sds((width, ff), BF)] * 2, 5, 4 * product, slots * ff * 12
    )(me, saved_inputs[:, 0], dgate0, dup0, dgate1, dup1)
    in_grad, prob_grad = call(
        functools.partial(unpack_kernel, ne, cap),
        [sds((mb, toks, width), BF), sds((mb, toks, top), BF)],
        2,
        product // 8,
        ne * mb * line * 2,
    )(me, expert_ids, home)
    return in_grad, prob_grad, grad_gate[None], grad_up[None], grad_down[None]


def solution(mesh):
    n_dp, n_ex = mesh.devices.shape
    fine = Mesh(
        mesh.devices.reshape(2, n_dp // 4, 2, n_ex // 4, 4), ("zh", "x", "core", "zl", "y")
    )
    specs = (
        P(None, EX, DP),
        P(None, EX, None),
        P(None, EX, None),
        P(None, EX, None, DP),
        P(None, EX, None, None),
        P(None, EX, None, None),
        P(EX, DP, None),
        P(EX, DP, None),
        P(EX, None, DP),
    )
    return jax.shard_map(
        local,
        mesh=fine,
        in_specs=specs,
        out_specs=(specs[0], specs[1], specs[6], specs[7], specs[8]),
        check_vma=False,
    )
```

time: 203 us -> 201 us (level)
  blocking collectives: 61.8 us -> 115 us
  waiting for transfers between devices: 66.7 us -> 32.7 us
  other arithmetic: 13.3 us -> 0.21 us
  matrix products: 10.3 us -> 0 us
  Pallas kernels: 0 us -> 8.06 us
  local copies, waits for them, and re-layouts: 8.03 us -> 4.21 us
    all_to_all x1 -> x4, blocking collectives: 61.8 us -> 115 us  [the longest x1 61.8 us: local(): lax.all_to_all(send.reshape(ne, mb, line), EX, 0, 0, tiled=True)]
    ppermute x3 -> x2, waiting for transfers between devices: 26 us -> 1.13 us  [the longest x1 1.13 us: local(): away = lax.ppermute(part1, 'core', SWAP)]
    dot_general x35 -> x0, matrix products: 10.3 us -> none  [dot(): lax.dot_general(a, b, (((ca,), (cb,)), ((), ())), preferred_element_type=...]
    all_to_all x3 -> x1, waiting for transfers between devices: 40.7 us -> 31.5 us  [local(): home = lax.all_to_all(back, EX, 0, 0, tiled=True).reshape(ne, mb * line)]
    pallas_call x0 -> x8, Pallas kernels: none -> 8.06 us  [the longest x1 1.96 us: local(): call(act_kernel, [sds((mb, slots, ff), F32)] * 3 + [sds((ff, width), BF)]...]
    convert_element_type x14 -> x1, other arithmetic: 6.6 us -> 0.09 us  [local(): half = (part0 + away).astype(BF).reshape(n_x, slots // n_x, ff)]
    ppermute x3 -> x2, starting transfers between devices: 22.7 us -> 16.7 us  [the longest x1 8.89 us: local(): u1 = lax.ppermute(u0, 'core', SWAP)]
    select_n x7 -> x0, other arithmetic: 5.29 us -> none  [turn(): return jnp.where(me_c == 0, v, v[::-1])]
  transfers between devices with their start and end apart: 6 -> 3, of which waited for: 5 -> 2; matrix products, arithmetic and copies ran while one was open for 5% -> 0% of each run, Pallas kernels for 0% -> 2%
where the time goes in v3:
time: 201 us; the launch traced here: 198 us
  blocking collectives  115 us (57%)
  starting transfers between devices  37.2 us (19%)
  waiting for transfers between devices  32.7 us (16%)
  Pallas kernels  8.06 us (4%)
  local copies, waits for them, and re-layouts  4.21 us (2%)
    all_to_all x1, blocking collectives, local(): lax.all_to_all(send.reshape(ne, mb, line), EX, 0, 0, tiled=True)  61.8 us
    all_to_all x1, blocking collectives, local(): lax.all_to_all(jnp.broadcast_to(eighth[None], (2,) + eighth.shape), 'zh',...  33.1 us
    all_to_all x1, waiting for transfers between devices, local(): home = lax.all_to_all(back, EX, 0, 0, tiled=True).reshape(ne, mb * line)  31.5 us
    all_to_all x1, starting transfers between devices, local(): home = lax.all_to_all(back, EX, 0, 0, tiled=True).reshape(ne, mb * line)  20.5 us
    all_to_all x1, blocking collectives, local(): half = lax.all_to_all(half, 'x', 0, 0, tiled=True)  11 us
    ppermute x1, starting transfers between devices, local(): u1 = lax.ppermute(u0, 'core', SWAP)  8.89 us
    all_to_all x1, blocking collectives, local(): u0 = lax.all_to_all(u, 'x', 0, 0, tiled=True).reshape(slots, ff)  8.76 us
    ppermute x1, starting transfers between devices, local(): away = lax.ppermute(part1, 'core', SWAP)  7.81 us
  transfers between devices with their start and end apart: 3, of which 2 were waited for; matrix products, arithmetic and copies ran while one was open for 0% of the time, Pallas kernels for 2%

profile of v3, /device:TPU:1, one launch (start us, length us, event | category | flops | bytes accessed | tf_op | source)
XLA Modules:
  0.0 197.9 jit_solution(2773820340032078679)
XLA Ops:
  0.6 0.0 copy-start.2
  0.6 0.8 copy.25.probs
  1.5 0.8 copy.27.ids
  2.2 0.7 copy-done.6
  3.0 0.7 shard_map.128
  3.7 0.1 reshape.31
  3.7 61.8 %all_to_all.25 = bf16[64,2,1152]{2,1,0:T(2,128)(2,1)S(1)} all-to-all(bf16[64,2,1152]{2,1,0:T(2,128)(2,1)S(1)} %reshape.31), channel_id=1, replica_groups=mesh['zh'=2,'x'=4,'core'=2,'zl'=16,'y'=4] {'zl','y'}, dimensions={0} | all-to-all | bytes 589824 | tf_op jit(solution)/shard_map/all_to_all | solution.py:186
  65.6 0.7 shard_map.130
  66.3 7.8 %collective-permute-start = (f32[256,768]{1,0:T(8,128)S(1)}, f32[256,768]{1,0:T(8,128)S(1)}, u32[]{:S(2)}, u32[]{:S(2)}) collective-permute-start(f32[256,768]{1,0:T(8,128)S(1)} %get-tuple-element.26), channel_id=1, source_target_pairs={{0,64},{64,0},{1,65},{65,1},{2,66},{66,2},{3,67},{67,3},{4,68},{68... | collective-permute-start | bytes 2359304 | tf_op jit(solution)/shard_map/ppermute | solution.py:199
  74.2 0.8 shard_map.129
  74.9 1.1 collective-permute-done
  76.0 0.1 add_convert_fusion
  76.1 11.0 %all_to_all.26 = bf16[4,64,768]{2,1,0:T(8,128)(2,1)S(1)} all-to-all(bf16[4,64,768]{2,1,0:T(8,128)(2,1)S(1)} %bitcast.34), channel_id=1, replica_groups=mesh['zh'=2,'x'=4,'core'=2,'zl'=16,'y'=4] {'x'}, dimensions={0} | all-to-all | bytes 786432 | tf_op jit(solution)/shard_map/all_to_all | solution.py:202
  87.2 0.1 reduce_sum.24
  87.2 33.1 %all_to_all.27 = bf16[2,64,768]{2,1,0:T(8,128)(2,1)S(1)} all-to-all(bf16[2,64,768]{2,1,0:T(8,128)(2,1)S(1)} %broadcast_in_dim.10), channel_id=1, replica_groups=mesh['zh'=2,'x'=4,'core'=2,'zl'=16,'y'=4] {'zh'}, dimensions={0} | all-to-all | bytes 393216 | tf_op jit(solution)/shard_map/all_to_all | solution.py:204
  120.4 0.0 copy-start
  120.4 0.0 copy-start.1
  120.5 8.8 %all_to_all.28 = bf16[4,64,768]{2,1,0:T(8,128)(2,1)S(1)} all-to-all(bf16[4,64,768]{2,1,0:T(8,128)(2,1)S(1)} %broadcast_in_dim.22), channel_id=1, replica_groups=mesh['zh'=2,'x'=4,'core'=2,'zl'=16,'y'=4] {'x'}, dimensions={0} | all-to-all | bytes 786432 | tf_op jit(solution)/shard_map/all_to_all | solution.py:217
  129.2 8.9 %collective-permute-start.1 = (bf16[256,768]{1,0:T(8,128)(2,1)S(1)}, bf16[256,768]{1,0:T(8,128)(2,1)S(1)}, u32[]{:S(2)}, u32[]{:S(2)}) collective-permute-start(bf16[256,768]{1,0:T(8,128)(2,1)S(1)} %bitcast.24), channel_id=1, source_target_pairs={{0,64},{64,0},{1,65},{65,1},{2,66},{66,2},{3,67},{67,3},{4,68},{68... | collective-permute-start | bytes 1179656 | tf_op jit(solution)/shard_map/ppermute | solution.py:218
  138.1 2.0 shard_map.131
  140.1 0.0 copy-done.1
  140.1 0.8 shard_map.132
  140.9 0.0 collective-permute-done.1.u_ref
  140.9 0.8 shard_map.133
  141.7 0.0 copy-start.5
  141.7 1.0 copy.26
  142.7 20.5 %all-to-all-start.4 = ((bf16[64,2,1152]{2,1,0:T(2,128)(2,1)}), bf16[64,2,1152]{2,1,0:T(2,128)(2,1)S(1)}, u32[]{:S(2)}, u32[]{:S(2)}) async-start(bf16[64,2,1152]{2,1,0:T(2,128)(2,1)} %copy.26), calls=%async_computation.4 | async-start | bytes 589824 | tf_op jit(solution)/shard_map/all_to_all | solution.py:233
  163.3 0.0 copy-done.5
  163.3 1.3 shard_map.135
  164.6 31.5 %all-to-all-done.4 = bf16[64,2,1152]{2,1,0:T(2,128)(2,1)S(1)} async-done(((bf16[64,2,1152]{2,1,0:T(2,128)(2,1)}), bf16[64,2,1152]{2,1,0:T(2,128)(2,1)S(1)}, u32[]{:S(2)}, u32[]{:S(2)}) %all-to-all-start.4) | async-done | bytes 294944 | tf_op jit(solution)/shard_map/all_to_all | solution.py:233
  196.2 1.0 shard_map.134
  197.2 0.7 copy.28
  (13 shorter events, 0.2 us)
Async XLA Ops:
  0.6 64.9 %copy-start.2 = (bf16[1,768,256]{2,1,0:T(8,128)(2,1)S(1)}, bf16[1,768,256]{2,1,0:T(8,128)(2,1)}, u32[]{:S(2)}) copy-start(bf16[1,768,256]{2,1,0:T(8,128)(2,1)} %param.17) | copy-start | bytes 1179652
  2.2 0.7 copy-start.6
  66.3 9.7 %collective-permute-start = (f32[256,768]{1,0:T(8,128)S(1)}, f32[256,768]{1,0:T(8,128)S(1)}, u32[]{:S(2)}, u32[]{:S(2)}) collective-permute-start(f32[256,768]{1,0:T(8,128)S(1)} %get-tuple-element.26), channel_id=1, source_target_pairs={{0,64},{64,0},{1,65},{65,1},{2,66},{66,2},{3,67},{67,3},{4,68},{68... | collective-permute-start | bytes 2359304 | tf_op jit(solution)/shard_map/ppermute | solution.py:199
  87.2 51.0 %copy-start.3 = (bf16[2,1,256,768]{3,2,1,0:T(8,128)(2,1)S(1)}, bf16[2,1,256,768]{3,2,1,0:T(8,128)(2,1)}, u32[]{:S(2)}) copy-start(bf16[2,1,256,768]{3,2,1,0:T(8,128)(2,1)} %param.13) | copy-start | bytes 2359300
  87.2 51.0 %copy-start.4 = (bf16[2,1,256,768]{3,2,1,0:T(8,128)(2,1)S(1)}, bf16[2,1,256,768]{3,2,1,0:T(8,128)(2,1)}, u32[]{:S(2)}) copy-start(bf16[2,1,256,768]{3,2,1,0:T(8,128)(2,1)} %param.14) | copy-start | bytes 2359300
  120.4 19.7 %copy-start = (bf16[1,256,768]{2,1,0:T(8,128)(2,1)S(1)}, bf16[1,256,768]{2,1,0:T(8,128)(2,1)}, u32[]{:S(2)}) copy-start(bf16[1,256,768]{2,1,0:T(8,128)(2,1)} %param.15) | copy-start | bytes 1179652
  120.4 19.6 %copy-start.1 = (bf16[1,256,768]{2,1,0:T(8,128)(2,1)S(1)}, bf16[1,256,768]{2,1,0:T(8,128)(2,1)}, u32[]{:S(2)}) copy-start(bf16[1,256,768]{2,1,0:T(8,128)(2,1)} %param.16) | copy-start | bytes 1179652
  129.2 11.7 %collective-permute-start.1 = (bf16[256,768]{1,0:T(8,128)(2,1)S(1)}, bf16[256,768]{1,0:T(8,128)(2,1)S(1)}, u32[]{:S(2)}, u32[]{:S(2)}) collective-permute-start(bf16[256,768]{1,0:T(8,128)(2,1)S(1)} %bitcast.24), channel_id=1, source_target_pairs={{0,64},{64,0},{1,65},{65,1},{2,66},{66,2},{3,67},{67,3},{4,68},{68... | collective-permute-start | bytes 1179656 | tf_op jit(solution)/shard_map/ppermute | solution.py:218
  141.7 21.6 %copy-start.5 = (bf16[2,1,256,256]{3,2,1,0:T(8,128)(2,1)S(1)}, bf16[2,1,256,256]{3,2,1,0:T(8,128)(2,1)}, u32[]{:S(2)}) copy-start(bf16[2,1,256,256]{3,2,1,0:T(8,128)(2,1)} %param.12) | copy-start | bytes 786436
  142.7 53.4 %all-to-all-start.4 = ((bf16[64,2,1152]{2,1,0:T(2,128)(2,1)}), bf16[64,2,1152]{2,1,0:T(2,128)(2,1)S(1)}, u32[]{:S(2)}, u32[]{:S(2)}) async-start(bf16[64,2,1152]{2,1,0:T(2,128)(2,1)} %copy.26), calls=%async_computation.4 | async-start | bytes 589824 | tf_op jit(solution)/shard_map/all_to_all | solution.py:233

commit v4 on v3

v4 whole, which is shorter than its diff:
```python
import functools

import jax
import jax.numpy as jnp
from jax import lax
from jax.experimental import pallas as pl
from jax.experimental.pallas import tpu as pltpu
from jax.sharding import Mesh
from jax.sharding import PartitionSpec as P

BF = jnp.bfloat16
F32 = jnp.float32
DP = ("zh", "x", "core")
EX = ("za", "zb", "y")
PLANE = ("zb", "y")
PAD = 128
SWAP = [(0, 1), (1, 0)]
VMEM = pl.BlockSpec(memory_space=pltpu.VMEM)
SMEM = pl.BlockSpec(memory_space=pltpu.SMEM)


def dot(a, b, ca, cb):
    return lax.dot_general(a, b, (((ca,), (cb,)), ((), ())), preferred_element_type=F32)


def iota(shape, dim):
    return lax.broadcasted_iota(jnp.int32, shape, dim)


def call(body, outs, n_in, flops, bytes_moved, limit=24, has_me=True):
    first = [SMEM] if has_me else []
    return pl.pallas_call(
        body,
        out_shape=outs,
        in_specs=first + [VMEM] * n_in,
        out_specs=[VMEM] * len(outs),
        cost_estimate=pl.CostEstimate(flops=flops, bytes_accessed=bytes_moved, transcendentals=0),
        compiler_params=pltpu.CompilerParams(vmem_limit_bytes=limit << 20),
    )


def flat_kernel(me, ids, probs, rows, out):
    mb, toks, width = rows.shape
    top = ids.shape[2]
    lane = iota((toks, PAD), 1)
    for m in range(mb):
        at = me[0] ^ m
        held = probs[at].astype(F32)
        names = ids[at].astype(F32)
        tail = jnp.zeros((toks, PAD), F32)
        for k in range(top):
            tail = jnp.where(lane == k, names[:, k : k + 1], tail)
            tail = jnp.where(lane == top + k, held[:, k : k + 1], tail)
        for peer in range(out.shape[0]):
            out[peer, m * toks : (m + 1) * toks, :width] = rows[at]
            out[peer, m * toks : (m + 1) * toks, width:] = tail.astype(BF)


def route_maps(names, first, size, nq, toks, cap):
    tokens, top = names.shape
    shape = (tokens, size)
    column = iota(shape, 1)
    expert = (first + lax.div(column, nq)).astype(F32)
    same = lax.div(iota(shape, 0), toks) == lax.rem(column, nq)
    picks = [jnp.where(same & (names[:, k : k + 1] == expert), 1.0, 0.0) for k in range(top)]
    hits = functools.reduce(jnp.add, picks)
    lower = jnp.where(iota((tokens, tokens), 0) > iota((tokens, tokens), 1), 1.0, 0.0)
    slot = dot(lower.astype(BF), hits.astype(BF), 1, 0)
    return picks, [jnp.where(slot == s, hits, 0.0) for s in range(cap)]


def pack_kernel(dims, first, lines, out):
    nd, nq, toks, top, cap, width = dims
    tail_in = lines[:, width:].astype(F32)
    picks, maps = route_maps(tail_in[:, :top], first[0], nd * nq, nq, toks, cap)
    grads = lines[:, :width]
    tokens = grads.shape[0]
    held = functools.reduce(
        jnp.add, [k * tail_in[:, top + i : top + i + 1] for i, k in enumerate(picks)]
    )
    tail = jnp.zeros((nd * nq, PAD), F32)
    for s, k in enumerate(maps):
        out[:, s * width : (s + 1) * width] = dot(k.astype(BF), grads, 0, 0).astype(BF)
        lane = jnp.where(iota((tokens, PAD), 1) == s, 1.0, 0.0).astype(BF)
        tail = tail + dot((k * held).astype(BF), lane, 0, 0)
    out[:, cap * width :] = tail.astype(BF)


def unpack_kernel(dims, first, lines, home, out):
    nd, nq, toks, top, cap, width = dims
    names = lines[:, width:].astype(F32)[:, :top]
    picks, maps = route_maps(names, first[0], nd * nq, nq, toks, cap)
    tokens = names.shape[0]
    total = jnp.zeros((tokens, width), F32)
    held = jnp.zeros((tokens, nd * nq), F32)
    tail = home[:, cap * width :]
    for s, k in enumerate(maps):
        total = total + dot(k.astype(BF), home[:, s * width : (s + 1) * width], 1, 0)
        lane = jnp.where(iota((tokens, PAD), 1) == s, 1.0, 0.0).astype(BF)
        held = held + k * dot(lane, tail, 1, 1)
    out[:, :width] = total.astype(BF)
    lane = iota((tokens, PAD), 1)
    picked = jnp.zeros((tokens, PAD), F32)
    for i, k in enumerate(picks):
        picked = jnp.where(lane == i, jnp.sum(k * held, axis=1, keepdims=True), picked)
    out[:, width:] = picked.astype(BF)


def total_kernel(me, parts, in_grad, prob_grad):
    mb, toks, width = in_grad.shape
    top = prob_grad.shape[2]
    for m in range(mb):
        total = functools.reduce(
            jnp.add,
            [
                parts[i, m * toks : (m + 1) * toks, :].astype(F32)
                for i in range(parts.shape[0])
            ],
        )
        in_grad[me[0] ^ m] = total[:, :width].astype(BF)
        prob_grad[me[0] ^ m] = total[:, width : width + top].astype(BF)


def first_row(shape, nd, nq, mb, cap):
    column = iota(shape, 1)
    return (lax.div(lax.rem(column, nq), mb) * nd + lax.div(column, nq)) * cap


def spread(nd, nq, mb, cap, m, s=None):
    rows = (nd * nq // mb) * cap
    shape = (rows, nd * nq)
    ahead = iota(shape, 0) - first_row(shape, nd, nq, mb, cap)
    here = (ahead >= 0) & (ahead < cap) if s is None else ahead == s
    here = here & (lax.rem(iota(shape, 1), mb) == m)
    return jnp.where(here, 1.0, 0.0).astype(BF)


def down_kernel(nd, nq, mb, cap, m, got, w_down, part, rows, probs):
    slots, width = rows.shape
    total = jnp.zeros((slots, width), F32)
    for s in range(cap):
        total = total + dot(
            spread(nd, nq, mb, cap, m, s), got[:, s * width : (s + 1) * width], 1, 0
        )
    mine = total.astype(BF)
    rows[...] = mine
    part[...] = dot(mine, w_down[...], 1, 1)
    tail = dot(spread(nd, nq, mb, cap, m), got[:, cap * width :], 1, 0)
    shape = (slots, PAD)
    probs[...] = jnp.sum(
        jnp.where(iota(shape, 1) == lax.rem(iota(shape, 0), cap), tail, 0.0), axis=1, keepdims=True
    )


def sum_kernel(mine, own, others, out):
    n = others.shape[0]
    total = functools.reduce(
        jnp.add, [jnp.where(mine[0] == i, own[i], others[i].astype(F32)) for i in range(n)]
    ).astype(BF)
    for i in range(out.shape[0]):
        out[i] = total


def pair_kernel(both, out):
    total = (both[0].astype(F32) + both[1].astype(F32)).astype(BF)
    for i in range(out.shape[0]):
        out[i] = total


def act_kernel(me, gate, up, probs0, probs1, rows0, rows1, f_gate, f_up, hidden, grad):
    total = None
    for m, (probs, rows) in enumerate(((probs0, rows0), (probs1, rows1))):
        gate_f = gate[me[0] ^ m].astype(F32)
        up_f = up[me[0] ^ m].astype(F32)
        p = probs[...]
        sig = 1.0 / (1.0 + jnp.exp(-gate_f))
        act = gate_f * sig
        h = act * up_f
        f_gate[m] = p * up_f * (sig * (1.0 + gate_f * (1.0 - sig)))
        f_up[m] = p * act
        hidden[m] = h
        term = dot((p * h).astype(BF), rows[...], 0, 0)
        total = term if total is None else total + term
    grad[...] = total.astype(BF)


def slot_kernel(nd, nq, mb, cap, m, u_ref, f_gate, f_up, hidden, w_gate, w_up, *rest):
    before, (dgate, dup, out) = rest[:-3], rest[-3:]
    u = u_ref[...].astype(F32)
    dg = (u * f_gate[m]).astype(BF)
    du = (u * f_up[m]).astype(BF)
    dgate[...] = dg
    dup[...] = du
    rows = (dot(dg, w_gate[...], 1, 1) + dot(du, w_up[...], 1, 1)).astype(BF)
    slots, width = rows.shape

    def put(low, high, value):
        if before:
            value = value + before[0][:, low:high].astype(F32)
        out[:, low:high] = value.astype(BF)

    for s in range(cap):
        put(s * width, (s + 1) * width, dot(spread(nd, nq, mb, cap, m, s), rows, 0, 0))
    slot_prob = jnp.sum(u * hidden[m], axis=1, keepdims=True)
    shape = (slots, PAD)
    tail = jnp.where(iota(shape, 1) == lax.rem(iota(shape, 0), cap), slot_prob, 0.0).astype(BF)
    put(cap * width, cap * width + PAD, dot(spread(nd, nq, mb, cap, m), tail, 0, 0))


def weight_kernel(me, inputs, dgate0, dup0, dgate1, dup1, grad_gate, grad_up):
    first, second = inputs[me[0]], inputs[me[0] ^ 1]
    grad_gate[...] = (dot(first, dgate0[...], 0, 0) + dot(second, dgate1[...], 0, 0)).astype(BF)
    grad_up[...] = (dot(first, dup0[...], 0, 0) + dot(second, dup1[...], 0, 0)).astype(BF)


def local(out_grad, expert_ids, probs, saved_inputs, gate_pre, up_pre, w_gate, w_up, w_down):
    sds = jax.ShapeDtypeStruct
    ne = lax.axis_size(EX)
    n_x = lax.axis_size("x")
    mb, toks, top = expert_ids.shape
    slots = saved_inputs.shape[2]
    cap = slots // ne
    width = out_grad.shape[2]
    ff = w_gate.shape[2]
    line = cap * width + PAD
    w_gate, w_up, w_down = w_gate[0], w_up[0], w_down[0]
    core = lax.axis_index("core")
    me = core.astype(jnp.int32).reshape(1)
    product = 2 * slots * width * ff

    n_a, nd = lax.axis_size("za"), lax.axis_size(PLANE)
    nq = n_a * mb
    dims = (nd, nq, toks, top, cap, width)
    first = (lax.axis_index("za").astype(jnp.int32) * nd).reshape(1)

    flat = call(flat_kernel, [sds((n_a, mb * toks, width + PAD), BF)], 3, 0, toks * width * 20)(
        me, expert_ids, probs, out_grad
    )[0]
    lines = lax.all_to_all(flat, "za", 0, 0, tiled=True).reshape(nq * toks, width + PAD)
    send = call(
        functools.partial(pack_kernel, dims), [sds((nd * nq, line), BF)], 1, product // 4, nd * nq * line * 2
    )(first, lines)[0]
    got = lax.all_to_all(send.reshape(nd, nq, line), PLANE, 0, 0, tiled=True).reshape(nd * nq, line)

    def down(m):
        return call(
            functools.partial(down_kernel, nd, nq, mb, cap, m),
            [sds((slots, ff), F32), sds((slots, width), BF), sds((slots, 1), F32)],
            2,
            product,
            slots * ff * 4,
            has_me=False,
        )(got, w_down)

    part1, rows1, probs1 = down(1)
    away = lax.ppermute(part1, "core", SWAP)
    part0, rows0, probs0 = down(0)
    half = (part0 + away).reshape(n_x, slots // n_x, ff)
    others = lax.all_to_all(half.astype(BF), "x", 0, 0, tiled=True)
    mine = lax.axis_index("x").astype(jnp.int32).reshape(1)
    piece = (slots // n_x, ff)
    eighth = call(
        sum_kernel, [sds((2,) + piece, BF)], 2, 0, slots * ff * 6
    )(mine, half, others)[0]
    both = lax.all_to_all(eighth, "zh", 0, 0, tiled=True)

    f_gate, f_up, hidden, grad_down = call(
        act_kernel,
        [sds((mb, slots, ff), F32)] * 3 + [sds((ff, width), BF)],
        6,
        2 * product,
        mb * slots * ff * 16,
        limit=32,
    )(me, gate_pre[:, 0], up_pre[:, 0], probs0, probs1, rows0, rows1)

    u = call(
        pair_kernel, [sds((n_x,) + piece, BF)], 1, 0, slots * ff * 2, has_me=False
    )(both)[0]
    u0 = lax.all_to_all(u, "x", 0, 0, tiled=True).reshape(slots, ff)
    u1 = lax.ppermute(u0, "core", SWAP)

    def slot(m, u_m, *before):
        return call(
            functools.partial(slot_kernel, nd, nq, mb, cap, m),
            [sds((slots, ff), BF), sds((slots, ff), BF), sds((nd * nq, line), BF)],
            6 + len(before),
            2 * product,
            slots * ff * 16,
            has_me=False,
        )(u_m, f_gate, f_up, hidden, w_gate, w_up, *before)

    dgate0, dup0, back = slot(0, u0)
    dgate1, dup1, back = slot(1, u1, back)
    home = lax.all_to_all(back.reshape(nd, nq, line), PLANE, 0, 0, tiled=True)
    part = call(
        functools.partial(unpack_kernel, dims),
        [sds((nq * toks, width + PAD), BF)],
        2,
        product // 4,
        nd * nq * line * 2,
    )(first, lines, home.reshape(nd * nq, line))[0]
    part = lax.all_to_all(part.reshape(n_a, mb * toks, width + PAD), "za", 0, 0, tiled=True)
    grad_gate, grad_up = call(
        weight_kernel, [sds((width, ff), BF)] * 2, 5, 4 * product, slots * ff * 12
    )(me, saved_inputs[:, 0], dgate0, dup0, dgate1, dup1)
    in_grad, prob_grad = call(
        total_kernel,
        [sds((mb, toks, width), BF), sds((mb, toks, top), BF)],
        1,
        0,
        toks * width * 20,
    )(me, part)
    return in_grad, prob_grad, grad_gate[None], grad_up[None], grad_down[None]


def solution(mesh):
    n_dp, n_ex = mesh.devices.shape
    n_a = 4 if n_ex >= 64 else 2
    fine = Mesh(
        mesh.devices.reshape(2, n_dp // 4, 2, n_a, n_ex // (4 * n_a), 4),
        ("zh", "x", "core", "za", "zb", "y"),
    )
    specs = (
        P(None, EX, DP),
        P(None, EX, None),
        P(None, EX, None),
        P(None, EX, None, DP),
        P(None, EX, None, None),
        P(None, EX, None, None),
        P(EX, DP, None),
        P(EX, DP, None),
        P(EX, None, DP),
    )
    return jax.shard_map(
        local,
        mesh=fine,
        in_specs=specs,
        out_specs=(specs[0], specs[1], specs[6], specs[7], specs[8]),
        check_vma=False,
    )
```

time: 201 us -> 191 us (0.950)
  blocking collectives: 115 us -> 86.4 us
  starting transfers between devices: 37.2 us -> 46.6 us
  waiting for transfers between devices: 32.7 us -> 40.1 us
    all_to_all x3, blocking collectives: 106 us -> 77.4 us  [the longest x1 35.8 us: local(): both = lax.all_to_all(eighth, 'zh', 0, 0, tiled=True)]
    all_to_all x1 -> x3, starting transfers between devices: 20.5 us -> 33.4 us  [the longest x1 22.3 us: local(): lax.all_to_all(flat, 'za', 0, 0, tiled=True).reshape(nq * toks, width + PAD)]
    all_to_all x1 -> x3, waiting for transfers between devices: 31.5 us -> 39 us  [the longest x1 16.4 us: local(): lax.all_to_all(flat, 'za', 0, 0, tiled=True).reshape(nq * toks, width + PAD)]
    ppermute x1, starting transfers between devices: 7.81 us -> 5.38 us  [local(): away = lax.ppermute(part1, 'core', SWAP)]
    pallas_call x6 -> x10, Pallas kernels: 4.75 us -> 6.56 us  [the longest x2 1.74 us: slot(): call(functools.partial(slot_kernel, nd, nq, mb, cap, m), [sds((slots, ff)...]
  transfers between devices with their start and end apart: 3 -> 5, of which waited for: 2 -> 4; matrix products, arithmetic and copies ran while one was open for 0% -> 0% of each run, Pallas kernels for 2% -> 3%
where the time goes in v4:
time: 191 us; the launch traced here: 188 us
  blocking collectives  86.4 us (45%)
  starting transfers between devices  46.6 us (24%)
  waiting for transfers between devices  40.1 us (21%)
  Pallas kernels  9.9 us (5%)
  local copies, waits for them, and re-layouts  3.01 us (2%)
    all_to_all x1, blocking collectives, local(): both = lax.all_to_all(eighth, 'zh', 0, 0, tiled=True)  35.8 us
    all_to_all x1, blocking collectives, local(): home = lax.all_to_all(back.reshape(nd, nq, line), PLANE, 0, 0, tiled=True)  24.1 us
    all_to_all x1, starting transfers between devices, local(): lax.all_to_all(flat, 'za', 0, 0, tiled=True).reshape(nq * toks, width + PAD)  22.3 us
    all_to_all x1, blocking collectives, local(): lax.all_to_all(send.reshape(nd, nq, line), PLANE, 0, 0, tiled=True)  17.5 us
    all_to_all x1, waiting for transfers between devices, local(): lax.all_to_all(flat, 'za', 0, 0, tiled=True).reshape(nq * toks, width + PAD)  16.4 us
    all_to_all x1, waiting for transfers between devices, local(): lax.all_to_all(part.reshape(n_a, mb * toks, width + PAD), 'za', 0, 0, til...  15.4 us
    all_to_all x1, blocking collectives, local(): u0 = lax.all_to_all(u, 'x', 0, 0, tiled=True).reshape(slots, ff)  8.99 us
    ppermute x1, starting transfers between devices, local(): u1 = lax.ppermute(u0, 'core', SWAP)  7.9 us
  transfers between devices with their start and end apart: 5, of which 4 were waited for; matrix products, arithmetic and copies ran while one was open for 0% of the time, Pallas kernels for 3%

profile of v4, /device:TPU:1, one launch (start us, length us, event | category | flops | bytes accessed | tf_op | source)
XLA Modules:
  0.0 187.7 jit_solution(7041684656634498392)
XLA Ops:
  0.6 0.8 copy.15.probs
  1.5 0.8 copy.14.ids
  2.2 0.7 copy-done.6
  3.0 0.8 shard_map.128
  3.7 22.3 %all-to-all-start = ((bf16[4,32,384]{2,1,0:T(8,128)(2,1)}), bf16[4,32,384]{2,1,0:T(8,128)(2,1)S(1)}, u32[]{:S(2)}, u32[]{:S(2)}) async-start(bf16[4,32,384]{2,1,0:T(8,128)(2,1)} %shard_map.128), calls=%async_computation | async-start | bytes 196608 | tf_op jit(solution)/shard_map/all_to_all | solution.py:239
  26.0 16.4 %all-to-all-done = bf16[4,32,384]{2,1,0:T(8,128)(2,1)S(1)} async-done(((bf16[4,32,384]{2,1,0:T(8,128)(2,1)}), bf16[4,32,384]{2,1,0:T(8,128)(2,1)S(1)}, u32[]{:S(2)}, u32[]{:S(2)}) %all-to-all-start) | async-done | bytes 98336 | tf_op jit(solution)/shard_map/all_to_all | solution.py:239
  42.4 0.6 shard_map.129
  43.0 17.5 %all_to_all.35 = bf16[16,8,1152]{2,1,0:T(8,128)(2,1)S(1)} all-to-all(bf16[16,8,1152]{2,1,0:T(8,128)(2,1)S(1)} %bitcast.33), channel_id=1, replica_groups=mesh['zh'=2,'x'=4,'core'=2,'za'=4,'zb'=4,'y'=4] {'zb','y'}, dimensions={0} | all-to-all | bytes 589824 | tf_op jit(solution)/shard_map/all_to_all | solution.py:243
  60.5 0.8 shard_map.131
  61.2 5.4 %collective-permute-start = (f32[256,768]{1,0:T(8,128)S(1)}, f32[256,768]{1,0:T(8,128)S(1)}, u32[]{:S(2)}, u32[]{:S(2)}) collective-permute-start(f32[256,768]{1,0:T(8,128)S(1)} %get-tuple-element.26), channel_id=1, source_target_pairs={{0,64},{64,0},{1,65},{65,1},{2,66},{66,2},{3,67},{67,3},{4,68},{68... | collective-permute-start | bytes 2359304 | tf_op jit(solution)/shard_map/ppermute | solution.py:256
  66.6 0.8 shard_map.130
  67.4 1.1 collective-permute-done
  68.5 0.1 add.3
  68.6 0.8 convert_element_type.3
  69.4 4.0 %all-to-all-start.2 = ((bf16[4,64,768]{2,1,0:T(8,128)(2,1)}), bf16[4,64,768]{2,1,0:T(8,128)(2,1)S(1)}, u32[]{:S(2)}, u32[]{:S(2)}) async-start(bf16[4,64,768]{2,1,0:T(8,128)(2,1)} %convert_element_type.3), calls=%async_computation.2 | async-start | bytes 786432 | tf_op jit(solution)/shard_map/all_to_all | solution.py:259
  73.4 7.2 %all-to-all-done.2.others = bf16[4,64,768]{2,1,0:T(8,128)(2,1)S(1)} async-done(((bf16[4,64,768]{2,1,0:T(8,128)(2,1)}), bf16[4,64,768]{2,1,0:T(8,128)(2,1)S(1)}, u32[]{:S(2)}, u32[]{:S(2)}) %all-to-all-start.2) | async-done | bytes 393248 | tf_op jit(solution)/shard_map/all_to_all | solution.py:259
  80.6 0.1 shard_map.132
  80.7 35.8 %all_to_all.36.both = bf16[2,64,768]{2,1,0:T(8,128)(2,1)S(1)} all-to-all(bf16[2,64,768]{2,1,0:T(8,128)(2,1)S(1)} %shard_map.132), channel_id=1, replica_groups=mesh['zh'=2,'x'=4,'core'=2,'za'=4,'zb'=4,'y'=4] {'zh'}, dimensions={0} | all-to-all | bytes 393216 | tf_op jit(solution)/shard_map/all_to_all | solution.py:265
  116.6 0.0 copy-start
  116.6 0.0 copy-start.1
  116.6 9.0 %all_to_all.37 = bf16[4,64,768]{2,1,0:T(8,128)(2,1)S(1)} all-to-all(bf16[4,64,768]{2,1,0:T(8,128)(2,1)S(1)} %shard_map.133), channel_id=1, replica_groups=mesh['zh'=2,'x'=4,'core'=2,'za'=4,'zb'=4,'y'=4] {'x'}, dimensions={0} | all-to-all | bytes 786432 | tf_op jit(solution)/shard_map/all_to_all | solution.py:279
  125.6 7.9 %collective-permute-start.1 = (bf16[256,768]{1,0:T(8,128)(2,1)S(1)}, bf16[256,768]{1,0:T(8,128)(2,1)S(1)}, u32[]{:S(2)}, u32[]{:S(2)}) collective-permute-start(bf16[256,768]{1,0:T(8,128)(2,1)S(1)} %bitcast.28), channel_id=1, source_target_pairs={{0,64},{64,0},{1,65},{65,1},{2,66},{66,2},{3,67},{67,3},{4,68},{68... | collective-permute-start | bytes 1179656 | tf_op jit(solution)/shard_map/ppermute | solution.py:280
  133.5 2.0 %shard_map.134 = (f32[2,256,768]{2,1,0:T(8,128)S(1)}, f32[2,256,768]{2,1,0:T(8,128)S(1)}, f32[2,256,768]{2,1,0:T(8,128)S(1)}, bf16[768,256]{1,0:T(8,128)(2,1)}) custom-call(s32[1]{0:T(128)} %bitcast.me, bf16[2,256,768]{2,1,0:T(8,128)(2,1)S(1)} %bitcast.36, bf16[2,256,768]{2,1,0:T(8,128)(2,1)S(1)} %bitcast.37, f32[256,1]{1,0:T(8,128)S(1)} %get-tuple-element.27.probs0, ...), custom_call_target="tpu_custom_call" | custom-call | flops 201326592 | bytes 6291456 | tf_op jit(solution)/shard_map/pallas_call | solution.py:267
  135.5 0.9 shard_map.135
  136.4 0.9 shard_map.136
  137.3 24.1 %all_to_all.38 = bf16[16,8,1152]{2,1,0:T(8,128)(2,1)S(1)} all-to-all(bf16[16,8,1152]{2,1,0:T(8,128)(2,1)S(1)} %bitcast.38), channel_id=1, replica_groups=mesh['zh'=2,'x'=4,'core'=2,'za'=4,'zb'=4,'y'=4] {'zb','y'}, dimensions={0} | all-to-all | bytes 589824 | tf_op jit(solution)/shard_map/all_to_all | solution.py:294
  161.4 1.2 shard_map.137
  162.6 7.1 %all-to-all-start.6 = ((bf16[4,32,384]{2,1,0:T(8,128)(2,1)}), bf16[4,32,384]{2,1,0:T(8,128)(2,1)S(1)}, u32[]{:S(2)}, u32[]{:S(2)}) async-start(bf16[4,32,384]{2,1,0:T(8,128)(2,1)} %bitcast.15), calls=%async_computation.6 | async-start | bytes 196608 | tf_op jit(solution)/shard_map/all_to_all | solution.py:302
  169.7 1.3 shard_map.139
  171.0 15.4 %all-to-all-done.6.parts = bf16[4,32,384]{2,1,0:T(8,128)(2,1)S(1)} async-done(((bf16[4,32,384]{2,1,0:T(8,128)(2,1)}), bf16[4,32,384]{2,1,0:T(8,128)(2,1)S(1)}, u32[]{:S(2)}, u32[]{:S(2)}) %all-to-all-start.6) | async-done | bytes 98336 | tf_op jit(solution)/shard_map/all_to_all | solution.py:302
  186.4 0.6 shard_map.138
  187.0 0.7 copy.16
  (13 shorter events, 0.1 us)
Async XLA Ops:
  0.6 59.8 %copy-start.2 = (bf16[1,768,256]{2,1,0:T(8,128)(2,1)S(1)}, bf16[1,768,256]{2,1,0:T(8,128)(2,1)}, u32[]{:S(2)}) copy-start(bf16[1,768,256]{2,1,0:T(8,128)(2,1)} %param.17) | copy-start | bytes 1179652
  2.2 0.7 copy-start.6
  3.7 38.7 %all-to-all-start = ((bf16[4,32,384]{2,1,0:T(8,128)(2,1)}), bf16[4,32,384]{2,1,0:T(8,128)(2,1)S(1)}, u32[]{:S(2)}, u32[]{:S(2)}) async-start(bf16[4,32,384]{2,1,0:T(8,128)(2,1)} %shard_map.128), calls=%async_computation | async-start | bytes 196608 | tf_op jit(solution)/shard_map/all_to_all | solution.py:239
  61.2 7.3 %collective-permute-start = (f32[256,768]{1,0:T(8,128)S(1)}, f32[256,768]{1,0:T(8,128)S(1)}, u32[]{:S(2)}, u32[]{:S(2)}) collective-permute-start(f32[256,768]{1,0:T(8,128)S(1)} %get-tuple-element.26), channel_id=1, source_target_pairs={{0,64},{64,0},{1,65},{65,1},{2,66},{66,2},{3,67},{67,3},{4,68},{68... | collective-permute-start | bytes 2359304 | tf_op jit(solution)/shard_map/ppermute | solution.py:256
  69.4 11.2 %all-to-all-start.2 = ((bf16[4,64,768]{2,1,0:T(8,128)(2,1)}), bf16[4,64,768]{2,1,0:T(8,128)(2,1)S(1)}, u32[]{:S(2)}, u32[]{:S(2)}) async-start(bf16[4,64,768]{2,1,0:T(8,128)(2,1)} %convert_element_type.3), calls=%async_computation.2 | async-start | bytes 786432 | tf_op jit(solution)/shard_map/all_to_all | solution.py:259
  80.6 52.9 %copy-start.3 = (bf16[2,1,256,768]{3,2,1,0:T(8,128)(2,1)S(1)}, bf16[2,1,256,768]{3,2,1,0:T(8,128)(2,1)}, u32[]{:S(2)}) copy-start(bf16[2,1,256,768]{3,2,1,0:T(8,128)(2,1)} %param.13) | copy-start | bytes 2359300
  80.6 52.9 %copy-start.4 = (bf16[2,1,256,768]{3,2,1,0:T(8,128)(2,1)S(1)}, bf16[2,1,256,768]{3,2,1,0:T(8,128)(2,1)}, u32[]{:S(2)}) copy-start(bf16[2,1,256,768]{3,2,1,0:T(8,128)(2,1)} %param.14) | copy-start | bytes 2359300
  116.6 18.9 %copy-start = (bf16[1,256,768]{2,1,0:T(8,128)(2,1)S(1)}, bf16[1,256,768]{2,1,0:T(8,128)(2,1)}, u32[]{:S(2)}) copy-start(bf16[1,256,768]{2,1,0:T(8,128)(2,1)} %param.15) | copy-start | bytes 1179652
  116.6 18.9 %copy-start.1 = (bf16[1,256,768]{2,1,0:T(8,128)(2,1)S(1)}, bf16[1,256,768]{2,1,0:T(8,128)(2,1)}, u32[]{:S(2)}) copy-start(bf16[1,256,768]{2,1,0:T(8,128)(2,1)} %param.16) | copy-start | bytes 1179652
  125.6 10.8 %collective-permute-start.1 = (bf16[256,768]{1,0:T(8,128)(2,1)S(1)}, bf16[256,768]{1,0:T(8,128)(2,1)S(1)}, u32[]{:S(2)}, u32[]{:S(2)}) collective-permute-start(bf16[256,768]{1,0:T(8,128)(2,1)S(1)} %bitcast.28), channel_id=1, source_target_pairs={{0,64},{64,0},{1,65},{65,1},{2,66},{66,2},{3,67},{67,3},{4,68},{68... | collective-permute-start | bytes 1179656 | tf_op jit(solution)/shard_map/ppermute | solution.py:280
  136.4 33.3 %copy-start.5 = (bf16[2,1,256,256]{3,2,1,0:T(8,128)(2,1)S(1)}, bf16[2,1,256,256]{3,2,1,0:T(8,128)(2,1)}, u32[]{:S(2)}) copy-start(bf16[2,1,256,256]{3,2,1,0:T(8,128)(2,1)} %param.12) | copy-start | bytes 786436
  162.6 23.8 %all-to-all-start.6 = ((bf16[4,32,384]{2,1,0:T(8,128)(2,1)}), bf16[4,32,384]{2,1,0:T(8,128)(2,1)S(1)}, u32[]{:S(2)}, u32[]{:S(2)}) async-start(bf16[4,32,384]{2,1,0:T(8,128)(2,1)} %bitcast.15), calls=%async_computation.6 | async-start | bytes 196608 | tf_op jit(solution)/shard_map/all_to_all | solution.py:302

commit v5 on v4

--- a/solution.py
+++ b/solution.py
@@ -41,16 +41,12 @@
 
 def flat_kernel(me, ids, probs, rows, out):
     mb, toks, width = rows.shape
-    top = ids.shape[2]
-    lane = iota((toks, PAD), 1)
+    top = ids.shape[1]
+    ahead = iota((top, PAD), 1) - iota((top, PAD), 0)
     for m in range(mb):
         at = me[0] ^ m
-        held = probs[at].astype(F32)
-        names = ids[at].astype(F32)
-        tail = jnp.zeros((toks, PAD), F32)
-        for k in range(top):
-            tail = jnp.where(lane == k, names[:, k : k + 1], tail)
-            tail = jnp.where(lane == top + k, held[:, k : k + 1], tail)
+        tail = dot(ids[at].astype(F32).astype(BF), (ahead == 0).astype(F32).astype(BF), 0, 0)
+        tail = tail + dot(probs[at], (ahead == top).astype(F32).astype(BF), 0, 0)
         for peer in range(out.shape[0]):
             out[peer, m * toks : (m + 1) * toks, :width] = rows[at]
             out[peer, m * toks : (m + 1) * toks, width:] = tail.astype(BF)
@@ -108,7 +104,8 @@
 
 def total_kernel(me, parts, in_grad, prob_grad):
     mb, toks, width = in_grad.shape
-    top = prob_grad.shape[2]
+    top = prob_grad.shape[1]
+    column = (iota((top, PAD), 1) == iota((top, PAD), 0)).astype(F32).astype(BF)
     for m in range(mb):
         total = functools.reduce(
             jnp.add,
@@ -118,7 +115,7 @@
             ],
         )
         in_grad[me[0] ^ m] = total[:, :width].astype(BF)
-        prob_grad[me[0] ^ m] = total[:, width : width + top].astype(BF)
+        prob_grad[me[0] ^ m] = dot(column, total[:, width:].astype(BF), 1, 1).astype(BF)
 
 
 def first_row(shape, nd, nq, mb, cap):
@@ -156,13 +153,12 @@
     n = others.shape[0]
     total = functools.reduce(
         jnp.add, [jnp.where(mine[0] == i, own[i], others[i].astype(F32)) for i in range(n)]
-    ).astype(BF)
-    for i in range(out.shape[0]):
-        out[i] = total
-
-
-def pair_kernel(both, out):
-    total = (both[0].astype(F32) + both[1].astype(F32)).astype(BF)
+    )
+    out[...] = total.astype(BF)
+
+
+def pair_kernel(first, second, out):
+    total = (first[...].astype(F32) + second[...].astype(F32)).astype(BF)
     for i in range(out.shape[0]):
         out[i] = total
 
@@ -234,7 +230,7 @@
     first = (lax.axis_index("za").astype(jnp.int32) * nd).reshape(1)
 
     flat = call(flat_kernel, [sds((n_a, mb * toks, width + PAD), BF)], 3, 0, toks * width * 20)(
-        me, expert_ids, probs, out_grad
+        me, jnp.swapaxes(expert_ids, 1, 2), jnp.swapaxes(probs, 1, 2), out_grad
     )[0]
     lines = lax.all_to_all(flat, "za", 0, 0, tiled=True).reshape(nq * toks, width + PAD)
     send = call(
@@ -260,9 +256,9 @@
     mine = lax.axis_index("x").astype(jnp.int32).reshape(1)
     piece = (slots // n_x, ff)
     eighth = call(
-        sum_kernel, [sds((2,) + piece, BF)], 2, 0, slots * ff * 6
+        sum_kernel, [sds(piece, BF)], 2, 0, slots * ff * 6
     )(mine, half, others)[0]
-    both = lax.all_to_all(eighth, "zh", 0, 0, tiled=True)
+    other = lax.ppermute(eighth, "zh", SWAP)
 
     f_gate, f_up, hidden, grad_down = call(
         act_kernel,
@@ -273,9 +269,10 @@
         limit=32,
     )(me, gate_pre[:, 0], up_pre[:, 0], probs0, probs1, rows0, rows1)
 
+    other, f_gate, f_up, hidden = lax.optimization_barrier((other, f_gate, f_up, hidden))
     u = call(
-        pair_kernel, [sds((n_x,) + piece, BF)], 1, 0, slots * ff * 2, has_me=False
-    )(both)[0]
+        pair_kernel, [sds((n_x,) + piece, BF)], 2, 0, slots * ff * 2, has_me=False
+    )(eighth, other)[0]
     u0 = lax.all_to_all(u, "x", 0, 0, tiled=True).reshape(slots, ff)
     u1 = lax.ppermute(u0, "core", SWAP)
 
@@ -305,11 +302,12 @@
     )(me, saved_inputs[:, 0], dgate0, dup0, dgate1, dup1)
     in_grad, prob_grad = call(
         total_kernel,
-        [sds((mb, toks, width), BF), sds((mb, toks, top), BF)],
+        [sds((mb, toks, width), BF), sds((mb, top, toks), BF)],
         1,
         0,
         toks * width * 20,
     )(me, part)
+    prob_grad = jnp.swapaxes(prob_grad, 1, 2)
     return in_grad, prob_grad, grad_gate[None], grad_up[None], grad_down[None]
 
 

time: 191 us -> 176 us (0.921)
  the two profiles are of different devices: /device:TPU:1 before, /device:TPU:2 now
where the time goes in v5:
time: 176 us; the launch traced here: 175 us
  waiting for transfers between devices  64.1 us (36%)
  starting transfers between devices  50.3 us (29%)
  blocking collectives  46.7 us (27%)
  Pallas kernels  9.87 us (6%)
  local copies, waits for them, and re-layouts  2.17 us (1%)
    all_to_all x1, starting transfers between devices, local(): lax.all_to_all(flat, 'za', 0, 0, tiled=True).reshape(nq * toks, width + PAD)  21.7 us
    all_to_all x1, waiting for transfers between devices, local(): lax.all_to_all(part.reshape(n_a, mb * toks, width + PAD), 'za', 0, 0, til...  18.9 us
    all_to_all x1, blocking collectives, local(): home = lax.all_to_all(back.reshape(nd, nq, line), PLANE, 0, 0, tiled=True)  18.7 us
    all_to_all x1, waiting for transfers between devices, local(): lax.all_to_all(flat, 'za', 0, 0, tiled=True).reshape(nq * toks, width + PAD)  18.3 us
    all_to_all x1, blocking collectives, local(): lax.all_to_all(send.reshape(nd, nq, line), PLANE, 0, 0, tiled=True)  18.1 us
    ppermute x1, waiting for transfers between devices, local(): other = lax.ppermute(eighth, 'zh', SWAP)  17.7 us
    ppermute x1, starting transfers between devices, local(): other = lax.ppermute(eighth, 'zh', SWAP)  14.5 us
    all_to_all x1, blocking collectives, local(): u0 = lax.all_to_all(u, 'x', 0, 0, tiled=True).reshape(slots, ff)  9.94 us
  transfers between devices with their start and end apart: 6, of which 6 were waited for; matrix products, arithmetic and copies ran while one was open for 0% of the time, Pallas kernels for 3%

profile of v5, /device:TPU:2, one launch (start us, length us, event | category | flops | bytes accessed | tf_op | source)
XLA Modules:
  0.0 174.9 jit_solution(15565182896914342921)
XLA Ops:
  0.7 0.8 copy-done.6
  1.4 0.7 copy-done.7
  2.1 0.7 copy-done.8
  2.8 0.8 shard_map.128
  3.6 21.7 %all-to-all-start = ((bf16[4,32,384]{2,1,0:T(8,128)(2,1)}), bf16[4,32,384]{2,1,0:T(8,128)(2,1)S(1)}, u32[]{:S(2)}, u32[]{:S(2)}) async-start(bf16[4,32,384]{2,1,0:T(8,128)(2,1)} %shard_map.128), calls=%async_computation | async-start | bytes 196608 | tf_op jit(solution)/shard_map/all_to_all | solution.py:235
  25.3 18.3 %all-to-all-done = bf16[4,32,384]{2,1,0:T(8,128)(2,1)S(1)} async-done(((bf16[4,32,384]{2,1,0:T(8,128)(2,1)}), bf16[4,32,384]{2,1,0:T(8,128)(2,1)S(1)}, u32[]{:S(2)}, u32[]{:S(2)}) %all-to-all-start) | async-done | bytes 98336 | tf_op jit(solution)/shard_map/all_to_all | solution.py:235
  43.6 0.6 shard_map.129
  44.2 18.1 %all_to_all.30 = bf16[16,8,1152]{2,1,0:T(8,128)(2,1)S(1)} all-to-all(bf16[16,8,1152]{2,1,0:T(8,128)(2,1)S(1)} %bitcast.36), channel_id=1, replica_groups=mesh['zh'=2,'x'=4,'core'=2,'za'=4,'zb'=4,'y'=4] {'zb','y'}, dimensions={0} | all-to-all | bytes 589824 | tf_op jit(solution)/shard_map/all_to_all | solution.py:239
  62.3 0.8 shard_map.131
  63.1 1.9 %collective-permute-start = (f32[256,768]{1,0:T(8,128)S(1)}, f32[256,768]{1,0:T(8,128)S(1)}, u32[]{:S(2)}, u32[]{:S(2)}) collective-permute-start(f32[256,768]{1,0:T(8,128)S(1)} %get-tuple-element.30), channel_id=1, source_target_pairs={{0,64},{64,0},{1,65},{65,1},{2,66},{66,2},{3,67},{67,3},{4,68},{68... | collective-permute-start | bytes 2359304 | tf_op jit(solution)/shard_map/ppermute | solution.py:252
  65.0 0.8 shard_map.130
  65.8 1.5 collective-permute-done
  67.3 0.1 add.3
  67.4 0.8 convert_element_type.3
  68.2 4.8 %all-to-all-start.2 = ((bf16[4,64,768]{2,1,0:T(8,128)(2,1)}), bf16[4,64,768]{2,1,0:T(8,128)(2,1)S(1)}, u32[]{:S(2)}, u32[]{:S(2)}) async-start(bf16[4,64,768]{2,1,0:T(8,128)(2,1)} %convert_element_type.3), calls=%async_computation.2 | async-start | bytes 786432 | tf_op jit(solution)/shard_map/all_to_all | solution.py:255
  73.0 6.9 %all-to-all-done.2.others = bf16[4,64,768]{2,1,0:T(8,128)(2,1)S(1)} async-done(((bf16[4,64,768]{2,1,0:T(8,128)(2,1)}), bf16[4,64,768]{2,1,0:T(8,128)(2,1)S(1)}, u32[]{:S(2)}, u32[]{:S(2)}) %all-to-all-start.2) | async-done | bytes 393248 | tf_op jit(solution)/shard_map/all_to_all | solution.py:255
  79.9 0.1 shard_map.132.first
  80.0 14.5 %collective-permute-start.1 = (bf16[64,768]{1,0:T(8,128)(2,1)S(1)}, bf16[64,768]{1,0:T(8,128)(2,1)S(1)}, u32[]{:S(2)}, u32[]{:S(2)}) collective-permute-start(bf16[64,768]{1,0:T(8,128)(2,1)S(1)} %shard_map.132.first), channel_id=1, source_target_pairs={{0,512},{512,0},{1,513},{513,1},{2,514},{514,2},{3,515},{515,3},{4... | collective-permute-start | bytes 294920 | tf_op jit(solution)/shard_map/ppermute | solution.py:261
  94.5 0.0 copy-start.1
  94.5 2.0 %shard_map.133 = (f32[2,256,768]{2,1,0:T(8,128)S(1)}, f32[2,256,768]{2,1,0:T(8,128)S(1)}, f32[2,256,768]{2,1,0:T(8,128)S(1)}, bf16[768,256]{1,0:T(8,128)(2,1)}) custom-call(s32[1]{0:T(128)} %bitcast.me, bf16[2,256,768]{2,1,0:T(8,128)(2,1)S(1)} %bitcast.39, bf16[2,256,768]{2,1,0:T(8,128)(2,1)S(1)} %bitcast.40, f32[256,1]{1,0:T(8,128)S(1)} %get-tuple-element.31.probs0, ...), custom_call_target="tpu_custom_call" | custom-call | flops 201326592 | bytes 6291456 | tf_op jit(solution)/shard_map/pallas_call | solution.py:263
  96.5 17.7 %collective-permute-done.1.second = bf16[64,768]{1,0:T(8,128)(2,1)S(1)} collective-permute-done((bf16[64,768]{1,0:T(8,128)(2,1)S(1)}, bf16[64,768]{1,0:T(8,128)(2,1)S(1)}, u32[]{:S(2)}, u32[]{:S(2)}) %collective-permute-start.1) | collective-permute-done | bytes 98336 | tf_op jit(solution)/shard_map/ppermute | solution.py:261
  114.2 9.9 %all_to_all.31 = bf16[4,64,768]{2,1,0:T(8,128)(2,1)S(1)} all-to-all(bf16[4,64,768]{2,1,0:T(8,128)(2,1)S(1)} %shard_map.134), channel_id=1, replica_groups=mesh['zh'=2,'x'=4,'core'=2,'za'=4,'zb'=4,'y'=4] {'x'}, dimensions={0} | all-to-all | bytes 786432 | tf_op jit(solution)/shard_map/all_to_all | solution.py:276
  124.1 1.9 %collective-permute-start.2 = (bf16[256,768]{1,0:T(8,128)(2,1)S(1)}, bf16[256,768]{1,0:T(8,128)(2,1)S(1)}, u32[]{:S(2)}, u32[]{:S(2)}) collective-permute-start(bf16[256,768]{1,0:T(8,128)(2,1)S(1)} %bitcast.31), channel_id=1, source_target_pairs={{0,64},{64,0},{1,65},{65,1},{2,66},{66,2},{3,67},{67,3},{4,68},{68... | collective-permute-start | bytes 1179656 | tf_op jit(solution)/shard_map/ppermute | solution.py:277
  126.1 0.8 shard_map.135
  126.9 0.9 collective-permute-done.2.u_ref
  127.7 0.8 shard_map.136
  128.5 18.7 %all_to_all.32 = bf16[16,8,1152]{2,1,0:T(8,128)(2,1)S(1)} all-to-all(bf16[16,8,1152]{2,1,0:T(8,128)(2,1)S(1)} %bitcast.41), channel_id=1, replica_groups=mesh['zh'=2,'x'=4,'core'=2,'za'=4,'zb'=4,'y'=4] {'zb','y'}, dimensions={0} | all-to-all | bytes 589824 | tf_op jit(solution)/shard_map/all_to_all | solution.py:291
  147.2 1.2 shard_map.137
  148.4 5.5 %all-to-all-start.5 = ((bf16[4,32,384]{2,1,0:T(8,128)(2,1)}), bf16[4,32,384]{2,1,0:T(8,128)(2,1)S(1)}, u32[]{:S(2)}, u32[]{:S(2)}) async-start(bf16[4,32,384]{2,1,0:T(8,128)(2,1)} %bitcast.17), calls=%async_computation.5 | async-start | bytes 196608 | tf_op jit(solution)/shard_map/all_to_all | solution.py:299
  154.0 1.3 shard_map.139
  155.3 18.9 %all-to-all-done.5.parts = bf16[4,32,384]{2,1,0:T(8,128)(2,1)S(1)} async-done(((bf16[4,32,384]{2,1,0:T(8,128)(2,1)}), bf16[4,32,384]{2,1,0:T(8,128)(2,1)S(1)}, u32[]{:S(2)}, u32[]{:S(2)}) %all-to-all-start.5) | async-done | bytes 98336 | tf_op jit(solution)/shard_map/all_to_all | solution.py:299
  174.2 0.7 shard_map.138
  (15 shorter events, 0.1 us)
Async XLA Ops:
  0.6 61.7 %copy-start.2 = (bf16[1,768,256]{2,1,0:T(8,128)(2,1)S(1)}, bf16[1,768,256]{2,1,0:T(8,128)(2,1)}, u32[]{:S(2)}) copy-start(bf16[1,768,256]{2,1,0:T(8,128)(2,1)} %param.17) | copy-start | bytes 1179652
  0.6 0.8 copy-start.6
  1.4 0.7 copy-start.7
  2.1 0.7 copy-start.8
  3.6 40.0 %all-to-all-start = ((bf16[4,32,384]{2,1,0:T(8,128)(2,1)}), bf16[4,32,384]{2,1,0:T(8,128)(2,1)S(1)}, u32[]{:S(2)}, u32[]{:S(2)}) async-start(bf16[4,32,384]{2,1,0:T(8,128)(2,1)} %shard_map.128), calls=%async_computation | async-start | bytes 196608 | tf_op jit(solution)/shard_map/all_to_all | solution.py:235
  63.1 4.2 %collective-permute-start = (f32[256,768]{1,0:T(8,128)S(1)}, f32[256,768]{1,0:T(8,128)S(1)}, u32[]{:S(2)}, u32[]{:S(2)}) collective-permute-start(f32[256,768]{1,0:T(8,128)S(1)} %get-tuple-element.30), channel_id=1, source_target_pairs={{0,64},{64,0},{1,65},{65,1},{2,66},{66,2},{3,67},{67,3},{4,68},{68... | collective-permute-start | bytes 2359304 | tf_op jit(solution)/shard_map/ppermute | solution.py:252
  67.4 27.1 %copy-start.3 = (bf16[2,1,256,768]{3,2,1,0:T(8,128)(2,1)S(1)}, bf16[2,1,256,768]{3,2,1,0:T(8,128)(2,1)}, u32[]{:S(2)}) copy-start(bf16[2,1,256,768]{3,2,1,0:T(8,128)(2,1)} %param.13) | copy-start | bytes 2359300
  67.4 27.1 %copy-start.4 = (bf16[2,1,256,768]{3,2,1,0:T(8,128)(2,1)S(1)}, bf16[2,1,256,768]{3,2,1,0:T(8,128)(2,1)}, u32[]{:S(2)}) copy-start(bf16[2,1,256,768]{3,2,1,0:T(8,128)(2,1)} %param.14) | copy-start | bytes 2359300
  68.2 11.7 %all-to-all-start.2 = ((bf16[4,64,768]{2,1,0:T(8,128)(2,1)}), bf16[4,64,768]{2,1,0:T(8,128)(2,1)S(1)}, u32[]{:S(2)}, u32[]{:S(2)}) async-start(bf16[4,64,768]{2,1,0:T(8,128)(2,1)} %convert_element_type.3), calls=%async_computation.2 | async-start | bytes 786432 | tf_op jit(solution)/shard_map/all_to_all | solution.py:255
  80.0 34.2 %collective-permute-start.1 = (bf16[64,768]{1,0:T(8,128)(2,1)S(1)}, bf16[64,768]{1,0:T(8,128)(2,1)S(1)}, u32[]{:S(2)}, u32[]{:S(2)}) collective-permute-start(bf16[64,768]{1,0:T(8,128)(2,1)S(1)} %shard_map.132.first), channel_id=1, source_target_pairs={{0,512},{512,0},{1,513},{513,1},{2,514},{514,2},{3,515},{515,3},{4... | collective-permute-start | bytes 294920 | tf_op jit(solution)/shard_map/ppermute | solution.py:261
  94.5 31.6 %copy-start = (bf16[1,256,768]{2,1,0:T(8,128)(2,1)S(1)}, bf16[1,256,768]{2,1,0:T(8,128)(2,1)}, u32[]{:S(2)}) copy-start(bf16[1,256,768]{2,1,0:T(8,128)(2,1)} %param.15) | copy-start | bytes 1179652
  94.5 31.6 %copy-start.1 = (bf16[1,256,768]{2,1,0:T(8,128)(2,1)S(1)}, bf16[1,256,768]{2,1,0:T(8,128)(2,1)}, u32[]{:S(2)}) copy-start(bf16[1,256,768]{2,1,0:T(8,128)(2,1)} %param.16) | copy-start | bytes 1179652
  124.1 3.6 %collective-permute-start.2 = (bf16[256,768]{1,0:T(8,128)(2,1)S(1)}, bf16[256,768]{1,0:T(8,128)(2,1)S(1)}, u32[]{:S(2)}, u32[]{:S(2)}) collective-permute-start(bf16[256,768]{1,0:T(8,128)(2,1)S(1)} %bitcast.31), channel_id=1, source_target_pairs={{0,64},{64,0},{1,65},{65,1},{2,66},{66,2},{3,67},{67,3},{4,68},{68... | collective-permute-start | bytes 1179656 | tf_op jit(solution)/shard_map/ppermute | solution.py:277
  127.7 26.2 %copy-start.5 = (bf16[2,1,256,256]{3,2,1,0:T(8,128)(2,1)S(1)}, bf16[2,1,256,256]{3,2,1,0:T(8,128)(2,1)}, u32[]{:S(2)}) copy-start(bf16[2,1,256,256]{3,2,1,0:T(8,128)(2,1)} %param.12) | copy-start | bytes 786436
  148.4 25.7 %all-to-all-start.5 = ((bf16[4,32,384]{2,1,0:T(8,128)(2,1)}), bf16[4,32,384]{2,1,0:T(8,128)(2,1)S(1)}, u32[]{:S(2)}, u32[]{:S(2)}) async-start(bf16[4,32,384]{2,1,0:T(8,128)(2,1)} %bitcast.17), calls=%async_computation.5 | async-start | bytes 196608 | tf_op jit(solution)/shard_map/all_to_all | solution.py:299

commit v6 on v5

--- a/solution.py
+++ b/solution.py
@@ -43,13 +43,16 @@
     mb, toks, width = rows.shape
     top = ids.shape[1]
     ahead = iota((top, PAD), 1) - iota((top, PAD), 0)
+    tail = jnp.zeros((toks, PAD), F32)
     for m in range(mb):
         at = me[0] ^ m
-        tail = dot(ids[at].astype(F32).astype(BF), (ahead == 0).astype(F32).astype(BF), 0, 0)
-        tail = tail + dot(probs[at], (ahead == top).astype(F32).astype(BF), 0, 0)
+        base = 2 * m * top
+        for offset, value in ((base, ids[at].astype(F32).astype(BF)), (base + top, probs[at])):
+            tail = tail + dot(value, (ahead == offset).astype(F32).astype(BF), 0, 0)
         for peer in range(out.shape[0]):
-            out[peer, m * toks : (m + 1) * toks, :width] = rows[at]
-            out[peer, m * toks : (m + 1) * toks, width:] = tail.astype(BF)
+            out[peer, :, m * width : (m + 1) * width] = rows[at]
+    for peer in range(out.shape[0]):
+        out[peer, :, mb * width :] = tail.astype(BF)
 
 
 def route_maps(names, first, size, nq, toks, cap):
@@ -65,11 +68,21 @@
     return picks, [jnp.where(slot == s, hits, 0.0) for s in range(cap)]
 
 
+def small_lines(lines, mb, top, width):
+    tail = lines[:, mb * width :]
+    shape = (PAD, PAD)
+    parts = []
+    for m in range(mb):
+        move = (iota(shape, 0) == iota(shape, 1) + 2 * m * top).astype(F32).astype(BF)
+        parts.append(dot(tail, move, 1, 0))
+    return jnp.concatenate(parts, axis=0)
+
+
 def pack_kernel(dims, first, lines, out):
-    nd, nq, toks, top, cap, width = dims
-    tail_in = lines[:, width:].astype(F32)
+    nd, nq, mb, toks, top, cap, width = dims
+    tail_in = small_lines(lines, mb, top, width)
     picks, maps = route_maps(tail_in[:, :top], first[0], nd * nq, nq, toks, cap)
-    grads = lines[:, :width]
+    grads = jnp.concatenate([lines[:, m * width : (m + 1) * width] for m in range(mb)], axis=0)
     tokens = grads.shape[0]
     held = functools.reduce(
         jnp.add, [k * tail_in[:, top + i : top + i + 1] for i, k in enumerate(picks)]
@@ -83,8 +96,8 @@
 
 
 def unpack_kernel(dims, first, lines, home, out):
-    nd, nq, toks, top, cap, width = dims
-    names = lines[:, width:].astype(F32)[:, :top]
+    nd, nq, mb, toks, top, cap, width = dims
+    names = small_lines(lines, mb, top, width)[:, :top]
     picks, maps = route_maps(names, first[0], nd * nq, nq, toks, cap)
     tokens = names.shape[0]
     total = jnp.zeros((tokens, width), F32)
@@ -94,33 +107,33 @@
         total = total + dot(k.astype(BF), home[:, s * width : (s + 1) * width], 1, 0)
         lane = jnp.where(iota((tokens, PAD), 1) == s, 1.0, 0.0).astype(BF)
         held = held + k * dot(lane, tail, 1, 1)
-    out[:, :width] = total.astype(BF)
-    lane = iota((tokens, PAD), 1)
-    picked = jnp.zeros((tokens, PAD), F32)
-    for i, k in enumerate(picks):
-        picked = jnp.where(lane == i, jnp.sum(k * held, axis=1, keepdims=True), picked)
-    out[:, width:] = picked.astype(BF)
+    run = tokens // mb
+    lane = iota((run, PAD), 1)
+    picked = jnp.zeros((run, PAD), F32)
+    for m in range(mb):
+        at = slice(m * run, (m + 1) * run)
+        out[:, m * width : (m + 1) * width] = total[at].astype(BF)
+        for i, k in enumerate(picks):
+            value = jnp.sum(k[at] * held[at], axis=1, keepdims=True)
+            picked = jnp.where(lane == m * top + i, value, picked)
+    out[:, mb * width :] = picked.astype(BF)
 
 
 def total_kernel(me, parts, in_grad, prob_grad):
     mb, toks, width = in_grad.shape
     top = prob_grad.shape[1]
-    column = (iota((top, PAD), 1) == iota((top, PAD), 0)).astype(F32).astype(BF)
+    total = functools.reduce(jnp.add, [parts[i].astype(F32) for i in range(parts.shape[0])])
+    tail = total[:, mb * width :].astype(BF)
+    ahead = iota((top, PAD), 1) - iota((top, PAD), 0)
     for m in range(mb):
-        total = functools.reduce(
-            jnp.add,
-            [
-                parts[i, m * toks : (m + 1) * toks, :].astype(F32)
-                for i in range(parts.shape[0])
-            ],
-        )
-        in_grad[me[0] ^ m] = total[:, :width].astype(BF)
-        prob_grad[me[0] ^ m] = dot(column, total[:, width:].astype(BF), 1, 1).astype(BF)
+        in_grad[me[0] ^ m] = total[:, m * width : (m + 1) * width].astype(BF)
+        column = (ahead == m * top).astype(F32).astype(BF)
+        prob_grad[me[0] ^ m] = dot(column, tail, 1, 1).astype(BF)
 
 
 def first_row(shape, nd, nq, mb, cap):
     column = iota(shape, 1)
-    return (lax.div(lax.rem(column, nq), mb) * nd + lax.div(column, nq)) * cap
+    return (lax.rem(lax.rem(column, nq), nq // mb) * nd + lax.div(column, nq)) * cap
 
 
 def spread(nd, nq, mb, cap, m, s=None):
@@ -128,7 +141,7 @@
     shape = (rows, nd * nq)
     ahead = iota(shape, 0) - first_row(shape, nd, nq, mb, cap)
     here = (ahead >= 0) & (ahead < cap) if s is None else ahead == s
-    here = here & (lax.rem(iota(shape, 1), mb) == m)
+    here = here & (lax.div(lax.rem(iota(shape, 1), nq), nq // mb) == m)
     return jnp.where(here, 1.0, 0.0).astype(BF)
 
 
@@ -226,13 +239,14 @@
 
     n_a, nd = lax.axis_size("za"), lax.axis_size(PLANE)
     nq = n_a * mb
-    dims = (nd, nq, toks, top, cap, width)
+    dims = (nd, nq, mb, toks, top, cap, width)
+    wide = mb * width + PAD
     first = (lax.axis_index("za").astype(jnp.int32) * nd).reshape(1)
 
-    flat = call(flat_kernel, [sds((n_a, mb * toks, width + PAD), BF)], 3, 0, toks * width * 20)(
+    flat = call(flat_kernel, [sds((n_a, toks, wide), BF)], 3, 0, toks * width * 20)(
         me, jnp.swapaxes(expert_ids, 1, 2), jnp.swapaxes(probs, 1, 2), out_grad
     )[0]
-    lines = lax.all_to_all(flat, "za", 0, 0, tiled=True).reshape(nq * toks, width + PAD)
+    lines = lax.all_to_all(flat, "za", 0, 0, tiled=True).reshape(n_a * toks, wide)
     send = call(
         functools.partial(pack_kernel, dims), [sds((nd * nq, line), BF)], 1, product // 4, nd * nq * line * 2
     )(first, lines)[0]
@@ -291,12 +305,12 @@
     home = lax.all_to_all(back.reshape(nd, nq, line), PLANE, 0, 0, tiled=True)
     part = call(
         functools.partial(unpack_kernel, dims),
-        [sds((nq * toks, width + PAD), BF)],
+        [sds((n_a * toks, wide), BF)],
         2,
         product // 4,
         nd * nq * line * 2,
     )(first, lines, home.reshape(nd * nq, line))[0]
-    part = lax.all_to_all(part.reshape(n_a, mb * toks, width + PAD), "za", 0, 0, tiled=True)
+    part = lax.all_to_all(part.reshape(n_a, toks, wide), "za", 0, 0, tiled=True)
     grad_gate, grad_up = call(
         weight_kernel, [sds((width, ff), BF)] * 2, 5, 4 * product, slots * ff * 12
     )(me, saved_inputs[:, 0], dgate0, dup0, dgate1, dup1)

time: 176 us -> 175 us (level)
  the two profiles are of different devices: /device:TPU:2 before, /device:TPU:1 now
where the time goes in v6:
time: 175 us; the launch traced here: 171 us
  waiting for transfers between devices  60.7 us (35%)
  starting transfers between devices  52 us (30%)
  blocking collectives  43.3 us (25%)
  Pallas kernels  10.3 us (6%)
  local copies, waits for them, and re-layouts  3.12 us (2%)
    all_to_all x1, starting transfers between devices, local(): lax.all_to_all(flat, 'za', 0, 0, tiled=True).reshape(n_a * toks, wide)  22.3 us
    ppermute x1, waiting for transfers between devices, local(): other = lax.ppermute(eighth, 'zh', SWAP)  20.5 us
    all_to_all x1, blocking collectives, local(): lax.all_to_all(send.reshape(nd, nq, line), PLANE, 0, 0, tiled=True)  17.4 us
    all_to_all x1, waiting for transfers between devices, local(): lax.all_to_all(flat, 'za', 0, 0, tiled=True).reshape(n_a * toks, wide)  16.4 us
    all_to_all x1, blocking collectives, local(): home = lax.all_to_all(back.reshape(nd, nq, line), PLANE, 0, 0, tiled=True)  15.9 us
    all_to_all x1, waiting for transfers between devices, local(): part = lax.all_to_all(part.reshape(n_a, toks, wide), 'za', 0, 0, tiled=True)  15 us
    ppermute x1, starting transfers between devices, local(): other = lax.ppermute(eighth, 'zh', SWAP)  13.4 us
    all_to_all x1, blocking collectives, local(): u0 = lax.all_to_all(u, 'x', 0, 0, tiled=True).reshape(slots, ff)  10 us
  transfers between devices with their start and end apart: 6, of which 6 were waited for; matrix products, arithmetic and copies ran while one was open for 0% of the time, Pallas kernels for 3%

profile of v6, /device:TPU:1, one launch (start us, length us, event | category | flops | bytes accessed | tf_op | source)
XLA Modules:
  0.0 171.1 jit_solution(554452968867504809)
XLA Ops:
  0.6 0.7 copy-done.6
  1.4 0.7 copy-done.7
  2.1 0.7 copy-done.8
  2.7 0.8 shard_map.128
  3.6 22.3 %all-to-all-start = ((bf16[4,16,640]{2,1,0:T(8,128)(2,1)}), bf16[4,16,640]{2,1,0:T(8,128)(2,1)S(1)}, u32[]{:S(2)}, u32[]{:S(2)}) async-start(bf16[4,16,640]{2,1,0:T(8,128)(2,1)} %shard_map.128), calls=%async_computation | async-start | bytes 163840 | tf_op jit(solution)/shard_map/all_to_all | solution.py:249
  25.8 16.4 %all-to-all-done = bf16[4,16,640]{2,1,0:T(8,128)(2,1)S(1)} async-done(((bf16[4,16,640]{2,1,0:T(8,128)(2,1)}), bf16[4,16,640]{2,1,0:T(8,128)(2,1)S(1)}, u32[]{:S(2)}, u32[]{:S(2)}) %all-to-all-start) | async-done | bytes 81952 | tf_op jit(solution)/shard_map/all_to_all | solution.py:249
  42.2 0.8 shard_map.129
  43.0 17.4 %all_to_all.30 = bf16[16,8,1152]{2,1,0:T(8,128)(2,1)S(1)} all-to-all(bf16[16,8,1152]{2,1,0:T(8,128)(2,1)S(1)} %bitcast.36), channel_id=1, replica_groups=mesh['zh'=2,'x'=4,'core'=2,'za'=4,'zb'=4,'y'=4] {'zb','y'}, dimensions={0} | all-to-all | bytes 589824 | tf_op jit(solution)/shard_map/all_to_all | solution.py:253
  60.4 1.0 copy-done.2
  61.4 0.8 shard_map.131
  62.1 5.3 %collective-permute-start = (f32[256,768]{1,0:T(8,128)S(1)}, f32[256,768]{1,0:T(8,128)S(1)}, u32[]{:S(2)}, u32[]{:S(2)}) collective-permute-start(f32[256,768]{1,0:T(8,128)S(1)} %get-tuple-element.30), channel_id=1, source_target_pairs={{0,64},{64,0},{1,65},{65,1},{2,66},{66,2},{3,67},{67,3},{4,68},{68... | collective-permute-start | bytes 2359304 | tf_op jit(solution)/shard_map/ppermute | solution.py:266
  67.5 0.8 shard_map.130
  68.3 1.1 collective-permute-done
  69.4 0.1 add.3
  69.5 0.8 convert_element_type.3
  70.3 4.0 %all-to-all-start.2 = ((bf16[4,64,768]{2,1,0:T(8,128)(2,1)}), bf16[4,64,768]{2,1,0:T(8,128)(2,1)S(1)}, u32[]{:S(2)}, u32[]{:S(2)}) async-start(bf16[4,64,768]{2,1,0:T(8,128)(2,1)} %convert_element_type.3), calls=%async_computation.2 | async-start | bytes 786432 | tf_op jit(solution)/shard_map/all_to_all | solution.py:269
  74.3 7.2 %all-to-all-done.2.others = bf16[4,64,768]{2,1,0:T(8,128)(2,1)S(1)} async-done(((bf16[4,64,768]{2,1,0:T(8,128)(2,1)}), bf16[4,64,768]{2,1,0:T(8,128)(2,1)S(1)}, u32[]{:S(2)}, u32[]{:S(2)}) %all-to-all-start.2) | async-done | bytes 393248 | tf_op jit(solution)/shard_map/all_to_all | solution.py:269
  81.5 0.1 shard_map.132.first
  81.6 13.4 %collective-permute-start.1 = (bf16[64,768]{1,0:T(8,128)(2,1)S(1)}, bf16[64,768]{1,0:T(8,128)(2,1)S(1)}, u32[]{:S(2)}, u32[]{:S(2)}) collective-permute-start(bf16[64,768]{1,0:T(8,128)(2,1)S(1)} %shard_map.132.first), channel_id=1, source_target_pairs={{0,512},{512,0},{1,513},{513,1},{2,514},{514,2},{3,515},{515,3},{4... | collective-permute-start | bytes 294920 | tf_op jit(solution)/shard_map/ppermute | solution.py:275
  95.0 2.0 %shard_map.133 = (f32[2,256,768]{2,1,0:T(8,128)S(1)}, f32[2,256,768]{2,1,0:T(8,128)S(1)}, f32[2,256,768]{2,1,0:T(8,128)S(1)}, bf16[768,256]{1,0:T(8,128)(2,1)}) custom-call(s32[1]{0:T(128)} %bitcast.me, bf16[2,256,768]{2,1,0:T(8,128)(2,1)S(1)} %bitcast.37, bf16[2,256,768]{2,1,0:T(8,128)(2,1)S(1)} %bitcast.38, f32[256,1]{1,0:T(8,128)S(1)} %get-tuple-element.31.probs0, ...), custom_call_target="tpu_custom_call" | custom-call | flops 201326592 | bytes 6291456 | tf_op jit(solution)/shard_map/pallas_call | solution.py:277
  97.0 20.5 %collective-permute-done.1.second = bf16[64,768]{1,0:T(8,128)(2,1)S(1)} collective-permute-done((bf16[64,768]{1,0:T(8,128)(2,1)S(1)}, bf16[64,768]{1,0:T(8,128)(2,1)S(1)}, u32[]{:S(2)}, u32[]{:S(2)}) %collective-permute-start.1) | collective-permute-done | bytes 98336 | tf_op jit(solution)/shard_map/ppermute | solution.py:275
  117.5 10.0 %all_to_all.31 = bf16[4,64,768]{2,1,0:T(8,128)(2,1)S(1)} all-to-all(bf16[4,64,768]{2,1,0:T(8,128)(2,1)S(1)} %shard_map.134), channel_id=1, replica_groups=mesh['zh'=2,'x'=4,'core'=2,'za'=4,'zb'=4,'y'=4] {'x'}, dimensions={0} | all-to-all | bytes 786432 | tf_op jit(solution)/shard_map/all_to_all | solution.py:290
  127.5 3.3 %collective-permute-start.2 = (bf16[256,768]{1,0:T(8,128)(2,1)S(1)}, bf16[256,768]{1,0:T(8,128)(2,1)S(1)}, u32[]{:S(2)}, u32[]{:S(2)}) collective-permute-start(bf16[256,768]{1,0:T(8,128)(2,1)S(1)} %bitcast.31), channel_id=1, source_target_pairs={{0,64},{64,0},{1,65},{65,1},{2,66},{66,2},{3,67},{67,3},{4,68},{68... | collective-permute-start | bytes 1179656 | tf_op jit(solution)/shard_map/ppermute | solution.py:291
  130.9 0.8 shard_map.135
  131.7 0.5 collective-permute-done.2.u_ref
  132.2 0.8 shard_map.136
  133.0 15.9 %all_to_all.32 = bf16[16,8,1152]{2,1,0:T(8,128)(2,1)S(1)} all-to-all(bf16[16,8,1152]{2,1,0:T(8,128)(2,1)S(1)} %bitcast.41), channel_id=1, replica_groups=mesh['zh'=2,'x'=4,'core'=2,'za'=4,'zb'=4,'y'=4] {'zb','y'}, dimensions={0} | all-to-all | bytes 589824 | tf_op jit(solution)/shard_map/all_to_all | solution.py:305
  148.9 1.4 shard_map.137
  150.3 3.7 %all-to-all-start.5 = ((bf16[4,16,640]{2,1,0:T(8,128)(2,1)}), bf16[4,16,640]{2,1,0:T(8,128)(2,1)S(1)}, u32[]{:S(2)}, u32[]{:S(2)}) async-start(bf16[4,16,640]{2,1,0:T(8,128)(2,1)} %bitcast.17), calls=%async_computation.5 | async-start | bytes 163840 | tf_op jit(solution)/shard_map/all_to_all | solution.py:313
  154.1 1.3 shard_map.139
  155.4 15.0 %all-to-all-done.5.parts = bf16[4,16,640]{2,1,0:T(8,128)(2,1)S(1)} async-done(((bf16[4,16,640]{2,1,0:T(8,128)(2,1)}), bf16[4,16,640]{2,1,0:T(8,128)(2,1)S(1)}, u32[]{:S(2)}, u32[]{:S(2)}) %all-to-all-start.5) | async-done | bytes 81952 | tf_op jit(solution)/shard_map/all_to_all | solution.py:313
  170.4 0.7 shard_map.138
  (15 shorter events, 0.1 us)
Async XLA Ops:
  0.6 0.7 copy-start.6
  1.4 0.7 copy-start.7
  2.1 0.7 copy-start.8
  3.6 38.6 %all-to-all-start = ((bf16[4,16,640]{2,1,0:T(8,128)(2,1)}), bf16[4,16,640]{2,1,0:T(8,128)(2,1)S(1)}, u32[]{:S(2)}, u32[]{:S(2)}) async-start(bf16[4,16,640]{2,1,0:T(8,128)(2,1)} %shard_map.128), calls=%async_computation | async-start | bytes 163840 | tf_op jit(solution)/shard_map/all_to_all | solution.py:249
  60.4 1.0 copy-start.2
  62.1 7.2 %collective-permute-start = (f32[256,768]{1,0:T(8,128)S(1)}, f32[256,768]{1,0:T(8,128)S(1)}, u32[]{:S(2)}, u32[]{:S(2)}) collective-permute-start(f32[256,768]{1,0:T(8,128)S(1)} %get-tuple-element.30), channel_id=1, source_target_pairs={{0,64},{64,0},{1,65},{65,1},{2,66},{66,2},{3,67},{67,3},{4,68},{68... | collective-permute-start | bytes 2359304 | tf_op jit(solution)/shard_map/ppermute | solution.py:266
  69.5 25.5 %copy-start.3 = (bf16[2,1,256,768]{3,2,1,0:T(8,128)(2,1)S(1)}, bf16[2,1,256,768]{3,2,1,0:T(8,128)(2,1)}, u32[]{:S(2)}) copy-start(bf16[2,1,256,768]{3,2,1,0:T(8,128)(2,1)} %param.13) | copy-start | bytes 2359300
  69.5 25.5 %copy-start.4 = (bf16[2,1,256,768]{3,2,1,0:T(8,128)(2,1)S(1)}, bf16[2,1,256,768]{3,2,1,0:T(8,128)(2,1)}, u32[]{:S(2)}) copy-start(bf16[2,1,256,768]{3,2,1,0:T(8,128)(2,1)} %param.14) | copy-start | bytes 2359300
  70.3 11.2 %all-to-all-start.2 = ((bf16[4,64,768]{2,1,0:T(8,128)(2,1)}), bf16[4,64,768]{2,1,0:T(8,128)(2,1)S(1)}, u32[]{:S(2)}, u32[]{:S(2)}) async-start(bf16[4,64,768]{2,1,0:T(8,128)(2,1)} %convert_element_type.3), calls=%async_computation.2 | async-start | bytes 786432 | tf_op jit(solution)/shard_map/all_to_all | solution.py:269
  81.6 35.9 %collective-permute-start.1 = (bf16[64,768]{1,0:T(8,128)(2,1)S(1)}, bf16[64,768]{1,0:T(8,128)(2,1)S(1)}, u32[]{:S(2)}, u32[]{:S(2)}) collective-permute-start(bf16[64,768]{1,0:T(8,128)(2,1)S(1)} %shard_map.132.first), channel_id=1, source_target_pairs={{0,512},{512,0},{1,513},{513,1},{2,514},{514,2},{3,515},{515,3},{4... | collective-permute-start | bytes 294920 | tf_op jit(solution)/shard_map/ppermute | solution.py:275
  95.0 35.9 %copy-start = (bf16[1,256,768]{2,1,0:T(8,128)(2,1)S(1)}, bf16[1,256,768]{2,1,0:T(8,128)(2,1)}, u32[]{:S(2)}) copy-start(bf16[1,256,768]{2,1,0:T(8,128)(2,1)} %param.15) | copy-start | bytes 1179652
  95.0 35.9 %copy-start.1 = (bf16[1,256,768]{2,1,0:T(8,128)(2,1)S(1)}, bf16[1,256,768]{2,1,0:T(8,128)(2,1)}, u32[]{:S(2)}) copy-start(bf16[1,256,768]{2,1,0:T(8,128)(2,1)} %param.16) | copy-start | bytes 1179652
  127.5 4.7 %collective-permute-start.2 = (bf16[256,768]{1,0:T(8,128)(2,1)S(1)}, bf16[256,768]{1,0:T(8,128)(2,1)S(1)}, u32[]{:S(2)}, u32[]{:S(2)}) collective-permute-start(bf16[256,768]{1,0:T(8,128)(2,1)S(1)} %bitcast.31), channel_id=1, source_target_pairs={{0,64},{64,0},{1,65},{65,1},{2,66},{66,2},{3,67},{67,3},{4,68},{68... | collective-permute-start | bytes 1179656 | tf_op jit(solution)/shard_map/ppermute | solution.py:291
  132.2 21.9 %copy-start.5 = (bf16[2,1,256,256]{3,2,1,0:T(8,128)(2,1)S(1)}, bf16[2,1,256,256]{3,2,1,0:T(8,128)(2,1)}, u32[]{:S(2)}) copy-start(bf16[2,1,256,256]{3,2,1,0:T(8,128)(2,1)} %param.12) | copy-start | bytes 786436
  150.3 20.1 %all-to-all-start.5 = ((bf16[4,16,640]{2,1,0:T(8,128)(2,1)}), bf16[4,16,640]{2,1,0:T(8,128)(2,1)S(1)}, u32[]{:S(2)}, u32[]{:S(2)}) async-start(bf16[4,16,640]{2,1,0:T(8,128)(2,1)} %bitcast.17), calls=%async_computation.5 | async-start | bytes 163840 | tf_op jit(solution)/shard_map/all_to_all | solution.py:313

commit v7 on v6

--- a/solution.py
+++ b/solution.py
@@ -39,7 +39,15 @@
     )
 
 
-def flat_kernel(me, ids, probs, rows, out):
+def flat_kernel(me, ids_in, probs_in, rows_in, out, ids, probs, rows, sems):
+    copies = [
+        pltpu.make_async_copy(source, held, sems.at[i])
+        for i, (source, held) in enumerate(((ids_in, ids), (probs_in, probs), (rows_in, rows)))
+    ]
+    for copy in copies:
+        copy.start()
+    for copy in copies:
+        copy.wait()
     mb, toks, width = rows.shape
     top = ids.shape[1]
     ahead = iota((top, PAD), 1) - iota((top, PAD), 0)
@@ -108,14 +116,15 @@
         lane = jnp.where(iota((tokens, PAD), 1) == s, 1.0, 0.0).astype(BF)
         held = held + k * dot(lane, tail, 1, 1)
     run = tokens // mb
-    lane = iota((run, PAD), 1)
+    shape = (nd * nq, PAD)
     picked = jnp.zeros((run, PAD), F32)
+    for i, k in enumerate(picks):
+        value = (k * held).astype(BF)
+        for m in range(mb):
+            lane = (iota(shape, 1) == m * top + i).astype(F32).astype(BF)
+            picked = picked + dot(value[m * run : (m + 1) * run], lane, 1, 0)
     for m in range(mb):
-        at = slice(m * run, (m + 1) * run)
-        out[:, m * width : (m + 1) * width] = total[at].astype(BF)
-        for i, k in enumerate(picks):
-            value = jnp.sum(k[at] * held[at], axis=1, keepdims=True)
-            picked = jnp.where(lane == m * top + i, value, picked)
+        out[:, m * width : (m + 1) * width] = total[m * run : (m + 1) * run].astype(BF)
     out[:, mb * width :] = picked.astype(BF)
 
 
@@ -162,11 +171,16 @@
     )
 
 
-def sum_kernel(mine, own, others, out):
-    n = others.shape[0]
-    total = functools.reduce(
-        jnp.add, [jnp.where(mine[0] == i, own[i], others[i].astype(F32)) for i in range(n)]
-    )
+def join_kernel(part, away, out):
+    out[...] = (part[...] + away[...]).astype(BF)
+
+
+def sum_kernel(mine, part, away, others, out):
+    rows = out.shape[0]
+    at = pl.ds(pl.multiple_of(mine[0] * rows, 8), rows)
+    total = part[at, :] + away[at, :]
+    for i in range(others.shape[0]):
+        total = total + jnp.where(mine[0] == i, 0.0, others[i].astype(F32))
     out[...] = total.astype(BF)
 
 
@@ -243,9 +257,20 @@
     wide = mb * width + PAD
     first = (lax.axis_index("za").astype(jnp.int32) * nd).reshape(1)
 
-    flat = call(flat_kernel, [sds((n_a, toks, wide), BF)], 3, 0, toks * width * 20)(
-        me, jnp.swapaxes(expert_ids, 1, 2), jnp.swapaxes(probs, 1, 2), out_grad
-    )[0]
+    hbm = pl.BlockSpec(memory_space=pltpu.HBM)
+    flat = pl.pallas_call(
+        flat_kernel,
+        out_shape=sds((n_a, toks, wide), BF),
+        in_specs=[SMEM, hbm, hbm, hbm],
+        out_specs=VMEM,
+        scratch_shapes=[
+            pltpu.VMEM((mb, top, toks), jnp.int32),
+            pltpu.VMEM((mb, top, toks), BF),
+            pltpu.VMEM((mb, toks, width), BF),
+            pltpu.SemaphoreType.DMA((3,)),
+        ],
+        compiler_params=pltpu.CompilerParams(vmem_limit_bytes=56 << 20),
+    )(me, jnp.swapaxes(expert_ids, 1, 2), jnp.swapaxes(probs, 1, 2), out_grad)
     lines = lax.all_to_all(flat, "za", 0, 0, tiled=True).reshape(n_a * toks, wide)
     send = call(
         functools.partial(pack_kernel, dims), [sds((nd * nq, line), BF)], 1, product // 4, nd * nq * line * 2
@@ -265,13 +290,15 @@
     part1, rows1, probs1 = down(1)
     away = lax.ppermute(part1, "core", SWAP)
     part0, rows0, probs0 = down(0)
-    half = (part0 + away).reshape(n_x, slots // n_x, ff)
-    others = lax.all_to_all(half.astype(BF), "x", 0, 0, tiled=True)
+    half = call(join_kernel, [sds((slots, ff), BF)], 2, 0, slots * ff * 10, has_me=False)(
+        part0, away
+    )[0]
+    others = lax.all_to_all(half.reshape(n_x, slots // n_x, ff), "x", 0, 0, tiled=True)
     mine = lax.axis_index("x").astype(jnp.int32).reshape(1)
     piece = (slots // n_x, ff)
     eighth = call(
-        sum_kernel, [sds(piece, BF)], 2, 0, slots * ff * 6
-    )(mine, half, others)[0]
+        sum_kernel, [sds(piece, BF)], 3, 0, slots * ff * 4
+    )(mine, part0, away, others)[0]
     other = lax.ppermute(eighth, "zh", SWAP)
 
     f_gate, f_up, hidden, grad_down = call(

time: 175 us -> 176 us (level)
  Pallas kernels: 10.3 us -> 12.3 us
    unnamed x18 -> x32, local copies, waits for them, and re-layouts: 3.12 us -> 3.62 us
  transfers between devices with their start and end apart: 6 -> 6, of which waited for: 6 -> 5; matrix products, arithmetic and copies ran while one was open for 0% -> 0% of each run, Pallas kernels for 3% -> 3%
where the time goes in v7:
time: 176 us; the launch traced here: 172 us
  waiting for transfers between devices  60.1 us (34%)
  starting transfers between devices  52.3 us (30%)
  blocking collectives  43.3 us (25%)
  Pallas kernels  12.3 us (7%)
  local copies, waits for them, and re-layouts  3.62 us (2%)
    all_to_all x1, starting transfers between devices, local(): lax.all_to_all(flat, 'za', 0, 0, tiled=True).reshape(n_a * toks, wide)  22.3 us
    ppermute x1, waiting for transfers between devices, local(): other = lax.ppermute(eighth, 'zh', SWAP)  20.5 us
    all_to_all x1, blocking collectives, local(): lax.all_to_all(send.reshape(nd, nq, line), PLANE, 0, 0, tiled=True)  17.4 us
    all_to_all x1, waiting for transfers between devices, local(): lax.all_to_all(flat, 'za', 0, 0, tiled=True).reshape(n_a * toks, wide)  16.4 us
    all_to_all x1, blocking collectives, local(): home = lax.all_to_all(back.reshape(nd, nq, line), PLANE, 0, 0, tiled=True)  15.9 us
    all_to_all x1, waiting for transfers between devices, local(): part = lax.all_to_all(part.reshape(n_a, toks, wide), 'za', 0, 0, tiled=True)  15 us
    ppermute x1, starting transfers between devices, local(): other = lax.ppermute(eighth, 'zh', SWAP)  13.5 us
    all_to_all x1, blocking collectives, local(): u0 = lax.all_to_all(u, 'x', 0, 0, tiled=True).reshape(slots, ff)  10 us
  transfers between devices with their start and end apart: 6, of which 5 were waited for; matrix products, arithmetic and copies ran while one was open for 0% of the time, Pallas kernels for 3%

profile of v7, /device:TPU:1, one launch (start us, length us, event | category | flops | bytes accessed | tf_op | source)
XLA Modules:
  0.0 172.5 jit_solution(4910895717494990943)
XLA Ops:
  0.6 1.6 shard_map.128
  2.2 22.3 %all-to-all-start = ((bf16[4,16,640]{2,1,0:T(8,128)(2,1)}), bf16[4,16,640]{2,1,0:T(8,128)(2,1)S(1)}, u32[]{:S(2)}, u32[]{:S(2)}) async-start(bf16[4,16,640]{2,1,0:T(8,128)(2,1)} %shard_map.128), calls=%async_computation | async-start | bytes 163840 | tf_op jit(solution)/shard_map/all_to_all | solution.py:274
  24.5 16.4 %all-to-all-done = bf16[4,16,640]{2,1,0:T(8,128)(2,1)S(1)} async-done(((bf16[4,16,640]{2,1,0:T(8,128)(2,1)}), bf16[4,16,640]{2,1,0:T(8,128)(2,1)S(1)}, u32[]{:S(2)}, u32[]{:S(2)}) %all-to-all-start) | async-done | bytes 81952 | tf_op jit(solution)/shard_map/all_to_all | solution.py:274
  40.9 0.8 shard_map.129
  41.7 17.4 %all_to_all.30 = bf16[16,8,1152]{2,1,0:T(8,128)(2,1)S(1)} all-to-all(bf16[16,8,1152]{2,1,0:T(8,128)(2,1)S(1)} %bitcast.34), channel_id=1, replica_groups=mesh['zh'=2,'x'=4,'core'=2,'za'=4,'zb'=4,'y'=4] {'zb','y'}, dimensions={0} | all-to-all | bytes 589824 | tf_op jit(solution)/shard_map/all_to_all | solution.py:278
  59.1 1.0 copy-done.2
  60.1 0.8 shard_map.131
  60.9 0.6 copy-done.8
  61.5 0.7 copy-done.10
  62.1 5.3 %collective-permute-start = (f32[256,768]{1,0:T(8,128)S(1)}, f32[256,768]{1,0:T(8,128)S(1)}, u32[]{:S(2)}, u32[]{:S(2)}) collective-permute-start(f32[256,768]{1,0:T(8,128)S(1)} %get-tuple-element.30), channel_id=1, source_target_pairs={{0,64},{64,0},{1,65},{65,1},{2,66},{66,2},{3,67},{67,3},{4,68},{68... | collective-permute-start | bytes 2359304 | tf_op jit(solution)/shard_map/ppermute | solution.py:291
  67.5 0.8 shard_map.130
  68.3 0.6 copy-done.12
  68.9 0.7 copy-done.14
  69.6 0.8 shard_map.132
  70.4 4.1 %all-to-all-start.2 = ((bf16[4,64,768]{2,1,0:T(8,128)(2,1)}), bf16[4,64,768]{2,1,0:T(8,128)(2,1)S(1)}, u32[]{:S(2)}, u32[]{:S(2)}) async-start(bf16[4,64,768]{2,1,0:T(8,128)(2,1)} %bitcast.9), calls=%async_computation.2 | async-start | bytes 786432 | tf_op jit(solution)/shard_map/all_to_all | solution.py:296
  74.5 7.7 %all-to-all-done.2.others = bf16[4,64,768]{2,1,0:T(8,128)(2,1)S(1)} async-done(((bf16[4,64,768]{2,1,0:T(8,128)(2,1)}), bf16[4,64,768]{2,1,0:T(8,128)(2,1)S(1)}, u32[]{:S(2)}, u32[]{:S(2)}) %all-to-all-start.2) | async-done | bytes 393248 | tf_op jit(solution)/shard_map/all_to_all | solution.py:296
  82.2 0.1 shard_map.133.first
  82.3 13.5 %collective-permute-start.1 = (bf16[64,768]{1,0:T(8,128)(2,1)S(1)}, bf16[64,768]{1,0:T(8,128)(2,1)S(1)}, u32[]{:S(2)}, u32[]{:S(2)}) collective-permute-start(bf16[64,768]{1,0:T(8,128)(2,1)S(1)} %shard_map.133.first), channel_id=1, source_target_pairs={{0,512},{512,0},{1,513},{513,1},{2,514},{514,2},{3,515},{515,3},{4... | collective-permute-start | bytes 294920 | tf_op jit(solution)/shard_map/ppermute | solution.py:302
  95.9 0.0 copy-start
  96.0 2.0 %shard_map.134 = (f32[2,256,768]{2,1,0:T(8,128)S(1)}, f32[2,256,768]{2,1,0:T(8,128)S(1)}, f32[2,256,768]{2,1,0:T(8,128)S(1)}, bf16[768,256]{1,0:T(8,128)(2,1)}) custom-call(s32[1]{0:T(128)} %bitcast.me, bf16[2,256,768]{2,1,0:T(8,128)(2,1)S(1)} %bitcast.35, bf16[2,256,768]{2,1,0:T(8,128)(2,1)S(1)} %bitcast.36, f32[256,1]{1,0:T(8,128)S(1)} %copy-done.15, ...), custom_call_target="tpu_custom_call" | custom-call | flops 201326592 | bytes 6291456 | tf_op jit(solution)/shard_map/pallas_call | solution.py:304
  97.9 20.5 %collective-permute-done.1.second = bf16[64,768]{1,0:T(8,128)(2,1)S(1)} collective-permute-done((bf16[64,768]{1,0:T(8,128)(2,1)S(1)}, bf16[64,768]{1,0:T(8,128)(2,1)S(1)}, u32[]{:S(2)}, u32[]{:S(2)}) %collective-permute-start.1) | collective-permute-done | bytes 98336 | tf_op jit(solution)/shard_map/ppermute | solution.py:302
  118.4 10.0 %all_to_all.31 = bf16[4,64,768]{2,1,0:T(8,128)(2,1)S(1)} all-to-all(bf16[4,64,768]{2,1,0:T(8,128)(2,1)S(1)} %shard_map.135), channel_id=1, replica_groups=mesh['zh'=2,'x'=4,'core'=2,'za'=4,'zb'=4,'y'=4] {'x'}, dimensions={0} | all-to-all | bytes 786432 | tf_op jit(solution)/shard_map/all_to_all | solution.py:317
  128.4 3.3 %collective-permute-start.2 = (bf16[256,768]{1,0:T(8,128)(2,1)S(1)}, bf16[256,768]{1,0:T(8,128)(2,1)S(1)}, u32[]{:S(2)}, u32[]{:S(2)}) collective-permute-start(bf16[256,768]{1,0:T(8,128)(2,1)S(1)} %bitcast.29), channel_id=1, source_target_pairs={{0,64},{64,0},{1,65},{65,1},{2,66},{66,2},{3,67},{67,3},{4,68},{68... | collective-permute-start | bytes 1179656 | tf_op jit(solution)/shard_map/ppermute | solution.py:318
  131.8 0.8 shard_map.136
  132.6 0.5 collective-permute-done.2.u_ref
  133.1 0.8 shard_map.137
  133.9 15.9 %all_to_all.32 = bf16[16,8,1152]{2,1,0:T(8,128)(2,1)S(1)} all-to-all(bf16[16,8,1152]{2,1,0:T(8,128)(2,1)S(1)} %bitcast.39), channel_id=1, replica_groups=mesh['zh'=2,'x'=4,'core'=2,'za'=4,'zb'=4,'y'=4] {'zb','y'}, dimensions={0} | all-to-all | bytes 589824 | tf_op jit(solution)/shard_map/all_to_all | solution.py:332
  149.8 1.8 %shard_map.138 = bf16[64,640]{1,0:T(8,128)(2,1)} custom-call(s32[1]{0:T(128)} %bitcast.1.first, bf16[64,640]{1,0:T(8,128)(2,1)S(1)} %bitcast.38, bf16[128,1152]{1,0:T(8,128)(2,1)S(1)} %bitcast.33), custom_call_target="tpu_custom_call" | custom-call | flops 25165824 | bytes 294912 | tf_op jit(solution)/shard_map/pallas_call | solution.py:333
  151.7 3.7 %all-to-all-start.5 = ((bf16[4,16,640]{2,1,0:T(8,128)(2,1)}), bf16[4,16,640]{2,1,0:T(8,128)(2,1)S(1)}, u32[]{:S(2)}, u32[]{:S(2)}) async-start(bf16[4,16,640]{2,1,0:T(8,128)(2,1)} %bitcast.17), calls=%async_computation.5 | async-start | bytes 163840 | tf_op jit(solution)/shard_map/all_to_all | solution.py:340
  155.4 1.3 shard_map.140
  156.7 15.0 %all-to-all-done.5.parts = bf16[4,16,640]{2,1,0:T(8,128)(2,1)S(1)} async-done(((bf16[4,16,640]{2,1,0:T(8,128)(2,1)}), bf16[4,16,640]{2,1,0:T(8,128)(2,1)S(1)}, u32[]{:S(2)}, u32[]{:S(2)}) %all-to-all-start.5) | async-done | bytes 81952 | tf_op jit(solution)/shard_map/all_to_all | solution.py:340
  171.7 0.7 shard_map.139
  (28 shorter events, 0.1 us)
Async XLA Ops:
  2.2 38.6 %all-to-all-start = ((bf16[4,16,640]{2,1,0:T(8,128)(2,1)}), bf16[4,16,640]{2,1,0:T(8,128)(2,1)S(1)}, u32[]{:S(2)}, u32[]{:S(2)}) async-start(bf16[4,16,640]{2,1,0:T(8,128)(2,1)} %shard_map.128), calls=%async_computation | async-start | bytes 163840 | tf_op jit(solution)/shard_map/all_to_all | solution.py:274
  40.9 20.0 %copy-start.5 = (bf16[4,16,640]{2,1,0:T(8,128)(2,1)}, bf16[4,16,640]{2,1,0:T(8,128)(2,1)S(1)}, u32[]{:S(2)}) copy-start(bf16[4,16,640]{2,1,0:T(8,128)(2,1)S(1)} %all-to-all-done) | copy-start | bytes 245764
  59.1 1.0 copy-start.2
  60.8 0.6 copy-start.8
  61.5 0.7 copy-start.10
  62.1 7.4 %collective-permute-start = (f32[256,768]{1,0:T(8,128)S(1)}, f32[256,768]{1,0:T(8,128)S(1)}, u32[]{:S(2)}, u32[]{:S(2)}) collective-permute-start(f32[256,768]{1,0:T(8,128)S(1)} %get-tuple-element.30), channel_id=1, source_target_pairs={{0,64},{64,0},{1,65},{65,1},{2,66},{66,2},{3,67},{67,3},{4,68},{68... | collective-permute-start | bytes 2359304 | tf_op jit(solution)/shard_map/ppermute | solution.py:291
  68.2 0.7 copy-start.12
  68.9 0.7 copy-start.14
  70.4 25.5 %copy-start.3 = (bf16[2,1,256,768]{3,2,1,0:T(8,128)(2,1)S(1)}, bf16[2,1,256,768]{3,2,1,0:T(8,128)(2,1)}, u32[]{:S(2)}) copy-start(bf16[2,1,256,768]{3,2,1,0:T(8,128)(2,1)} %param.13) | copy-start | bytes 2359300
  70.4 25.5 %copy-start.4 = (bf16[2,1,256,768]{3,2,1,0:T(8,128)(2,1)S(1)}, bf16[2,1,256,768]{3,2,1,0:T(8,128)(2,1)}, u32[]{:S(2)}) copy-start(bf16[2,1,256,768]{3,2,1,0:T(8,128)(2,1)} %param.14) | copy-start | bytes 2359300
  70.4 11.9 %all-to-all-start.2 = ((bf16[4,64,768]{2,1,0:T(8,128)(2,1)}), bf16[4,64,768]{2,1,0:T(8,128)(2,1)S(1)}, u32[]{:S(2)}, u32[]{:S(2)}) async-start(bf16[4,64,768]{2,1,0:T(8,128)(2,1)} %bitcast.9), calls=%async_computation.2 | async-start | bytes 786432 | tf_op jit(solution)/shard_map/all_to_all | solution.py:296
  82.2 13.7 %copy-start.9 = (bf16[256,256]{1,0:T(8,128)(2,1)S(1)}, bf16[256,256]{1,0:T(8,128)(2,1)}, u32[]{:S(2)}) copy-start(bf16[256,256]{1,0:T(8,128)(2,1)} %copy-done.8) | copy-start | bytes 393220
  82.2 13.7 %copy-start.11 = (f32[256,1]{1,0:T(8,128)S(1)}, f32[256,1]{1,0:T(8,128)}, u32[]{:S(2)}) copy-start(f32[256,1]{1,0:T(8,128)} %copy-done.10) | copy-start | bytes 3076
  82.2 13.7 %copy-start.13 = (bf16[256,256]{1,0:T(8,128)(2,1)S(1)}, bf16[256,256]{1,0:T(8,128)(2,1)}, u32[]{:S(2)}) copy-start(bf16[256,256]{1,0:T(8,128)(2,1)} %copy-done.12) | copy-start | bytes 393220
  82.2 13.7 %copy-start.15 = (f32[256,1]{1,0:T(8,128)S(1)}, f32[256,1]{1,0:T(8,128)}, u32[]{:S(2)}) copy-start(f32[256,1]{1,0:T(8,128)} %copy-done.14) | copy-start | bytes 3076
  82.3 36.1 %collective-permute-start.1 = (bf16[64,768]{1,0:T(8,128)(2,1)S(1)}, bf16[64,768]{1,0:T(8,128)(2,1)S(1)}, u32[]{:S(2)}, u32[]{:S(2)}) collective-permute-start(bf16[64,768]{1,0:T(8,128)(2,1)S(1)} %shard_map.133.first), channel_id=1, source_target_pairs={{0,512},{512,0},{1,513},{513,1},{2,514},{514,2},{3,515},{515,3},{4... | collective-permute-start | bytes 294920 | tf_op jit(solution)/shard_map/ppermute | solution.py:302
  95.9 35.8 %copy-start = (bf16[1,256,768]{2,1,0:T(8,128)(2,1)S(1)}, bf16[1,256,768]{2,1,0:T(8,128)(2,1)}, u32[]{:S(2)}) copy-start(bf16[1,256,768]{2,1,0:T(8,128)(2,1)} %param.15) | copy-start | bytes 1179652
  96.0 35.8 %copy-start.1 = (bf16[1,256,768]{2,1,0:T(8,128)(2,1)S(1)}, bf16[1,256,768]{2,1,0:T(8,128)(2,1)}, u32[]{:S(2)}) copy-start(bf16[1,256,768]{2,1,0:T(8,128)(2,1)} %param.16) | copy-start | bytes 1179652
  128.4 4.7 %collective-permute-start.2 = (bf16[256,768]{1,0:T(8,128)(2,1)S(1)}, bf16[256,768]{1,0:T(8,128)(2,1)S(1)}, u32[]{:S(2)}, u32[]{:S(2)}) collective-permute-start(bf16[256,768]{1,0:T(8,128)(2,1)S(1)} %bitcast.29), channel_id=1, source_target_pairs={{0,64},{64,0},{1,65},{65,1},{2,66},{66,2},{3,67},{67,3},{4,68},{68... | collective-permute-start | bytes 1179656 | tf_op jit(solution)/shard_map/ppermute | solution.py:318
  133.1 16.7 %copy-start.6 = (bf16[4,16,640]{2,1,0:T(8,128)(2,1)S(1)}, bf16[4,16,640]{2,1,0:T(8,128)(2,1)}, u32[]{:S(2)}) copy-start(bf16[4,16,640]{2,1,0:T(8,128)(2,1)} %copy-done.5) | copy-start | bytes 245764
  133.1 22.3 %copy-start.7 = (bf16[2,1,256,256]{3,2,1,0:T(8,128)(2,1)S(1)}, bf16[2,1,256,256]{3,2,1,0:T(8,128)(2,1)}, u32[]{:S(2)}) copy-start(bf16[2,1,256,256]{3,2,1,0:T(8,128)(2,1)} %param.12) | copy-start | bytes 786436
  151.7 20.1 %all-to-all-start.5 = ((bf16[4,16,640]{2,1,0:T(8,128)(2,1)}), bf16[4,16,640]{2,1,0:T(8,128)(2,1)S(1)}, u32[]{:S(2)}, u32[]{:S(2)}) async-start(bf16[4,16,640]{2,1,0:T(8,128)(2,1)} %bitcast.17), calls=%async_computation.5 | async-start | bytes 163840 | tf_op jit(solution)/shard_map/all_to_all | solution.py:340

commit v8 on v6

--- a/solution.py
+++ b/solution.py
@@ -39,7 +39,15 @@
     )
 
 
-def flat_kernel(me, ids, probs, rows, out):
+def flat_kernel(me, ids_in, probs_in, rows_in, out, ids, probs, rows, sems):
+    copies = [
+        pltpu.make_async_copy(source, held, sems.at[i])
+        for i, (source, held) in enumerate(((ids_in, ids), (probs_in, probs), (rows_in, rows)))
+    ]
+    for copy in copies:
+        copy.start()
+    for copy in copies:
+        copy.wait()
     mb, toks, width = rows.shape
     top = ids.shape[1]
     ahead = iota((top, PAD), 1) - iota((top, PAD), 0)
@@ -243,12 +251,23 @@
     wide = mb * width + PAD
     first = (lax.axis_index("za").astype(jnp.int32) * nd).reshape(1)
 
-    flat = call(flat_kernel, [sds((n_a, toks, wide), BF)], 3, 0, toks * width * 20)(
-        me, jnp.swapaxes(expert_ids, 1, 2), jnp.swapaxes(probs, 1, 2), out_grad
-    )[0]
+    hbm = pl.BlockSpec(memory_space=pltpu.HBM)
+    flat = pl.pallas_call(
+        flat_kernel,
+        out_shape=sds((n_a, toks, wide), BF),
+        in_specs=[SMEM, hbm, hbm, hbm],
+        out_specs=VMEM,
+        scratch_shapes=[
+            pltpu.VMEM((mb, top, toks), jnp.int32),
+            pltpu.VMEM((mb, top, toks), BF),
+            pltpu.VMEM((mb, toks, width), BF),
+            pltpu.SemaphoreType.DMA((3,)),
+        ],
+        compiler_params=pltpu.CompilerParams(vmem_limit_bytes=56 << 20),
+    )(me, jnp.swapaxes(expert_ids, 1, 2), jnp.swapaxes(probs, 1, 2), out_grad)
     lines = lax.all_to_all(flat, "za", 0, 0, tiled=True).reshape(n_a * toks, wide)
     send = call(
-        functools.partial(pack_kernel, dims), [sds((nd * nq, line), BF)], 1, product // 4, nd * nq * line * 2
+        functools.partial(pack_kernel, dims), [sds((nd * nq, line), BF)], 1, 16 * product, nd * nq * line * 64
     )(first, lines)[0]
     got = lax.all_to_all(send.reshape(nd, nq, line), PLANE, 0, 0, tiled=True).reshape(nd * nq, line)
 

time: 175 us -> 172 us (0.983)
  local copies, waits for them, and re-layouts: 3.12 us -> 0.03 us
    unnamed x18 -> x12, local copies, waits for them, and re-layouts: 3.12 us -> 0.03 us
where the time goes in v8:
time: 172 us; the launch traced here: 169 us
  waiting for transfers between devices  60.7 us (35%)
  starting transfers between devices  52 us (30%)
  blocking collectives  43.3 us (25%)
  Pallas kernels  11.1 us (6%)
    all_to_all x1, starting transfers between devices, local(): lax.all_to_all(flat, 'za', 0, 0, tiled=True).reshape(n_a * toks, wide)  22.3 us
    ppermute x1, waiting for transfers between devices, local(): other = lax.ppermute(eighth, 'zh', SWAP)  20.5 us
    all_to_all x1, blocking collectives, local(): lax.all_to_all(send.reshape(nd, nq, line), PLANE, 0, 0, tiled=True)  17.4 us
    all_to_all x1, waiting for transfers between devices, local(): lax.all_to_all(flat, 'za', 0, 0, tiled=True).reshape(n_a * toks, wide)  16.4 us
    all_to_all x1, blocking collectives, local(): home = lax.all_to_all(back.reshape(nd, nq, line), PLANE, 0, 0, tiled=True)  15.9 us
    all_to_all x1, waiting for transfers between devices, local(): part = lax.all_to_all(part.reshape(n_a, toks, wide), 'za', 0, 0, tiled=True)  15 us
    ppermute x1, starting transfers between devices, local(): other = lax.ppermute(eighth, 'zh', SWAP)  13.4 us
    all_to_all x1, blocking collectives, local(): u0 = lax.all_to_all(u, 'x', 0, 0, tiled=True).reshape(slots, ff)  10 us
  transfers between devices with their start and end apart: 6, of which 6 were waited for; matrix products, arithmetic and copies ran while one was open for 0% of the time, Pallas kernels for 3%

profile of v8, /device:TPU:1, one launch (start us, length us, event | category | flops | bytes accessed | tf_op | source)
XLA Modules:
  0.0 168.9 jit_solution(10243607713303550471)
XLA Ops:
  0.6 1.6 shard_map.128
  2.2 22.3 %all-to-all-start = ((bf16[4,16,640]{2,1,0:T(8,128)(2,1)}), bf16[4,16,640]{2,1,0:T(8,128)(2,1)S(1)}, u32[]{:S(2)}, u32[]{:S(2)}) async-start(bf16[4,16,640]{2,1,0:T(8,128)(2,1)} %shard_map.128), calls=%async_computation | async-start | bytes 163840 | tf_op jit(solution)/shard_map/all_to_all | solution.py:268
  24.5 16.4 %all-to-all-done = bf16[4,16,640]{2,1,0:T(8,128)(2,1)S(1)} async-done(((bf16[4,16,640]{2,1,0:T(8,128)(2,1)}), bf16[4,16,640]{2,1,0:T(8,128)(2,1)S(1)}, u32[]{:S(2)}, u32[]{:S(2)}) %all-to-all-start) | async-done | bytes 81952 | tf_op jit(solution)/shard_map/all_to_all | solution.py:268
  40.9 0.8 shard_map.129
  41.7 17.4 %all_to_all.30 = bf16[16,8,1152]{2,1,0:T(8,128)(2,1)S(1)} all-to-all(bf16[16,8,1152]{2,1,0:T(8,128)(2,1)S(1)} %bitcast.41), channel_id=1, replica_groups=mesh['zh'=2,'x'=4,'core'=2,'za'=4,'zb'=4,'y'=4] {'zb','y'}, dimensions={0} | all-to-all | bytes 589824 | tf_op jit(solution)/shard_map/all_to_all | solution.py:272
  59.1 0.8 shard_map.131
  59.8 5.3 %collective-permute-start = (f32[256,768]{1,0:T(8,128)S(1)}, f32[256,768]{1,0:T(8,128)S(1)}, u32[]{:S(2)}, u32[]{:S(2)}) collective-permute-start(f32[256,768]{1,0:T(8,128)S(1)} %get-tuple-element.30), channel_id=1, source_target_pairs={{0,64},{64,0},{1,65},{65,1},{2,66},{66,2},{3,67},{67,3},{4,68},{68... | collective-permute-start | bytes 2359304 | tf_op jit(solution)/shard_map/ppermute | solution.py:285
  65.2 0.8 shard_map.130
  66.0 1.1 collective-permute-done
  67.1 0.1 add.3
  67.2 0.0 copy-start.3
  67.2 0.0 copy-start.4
  67.2 0.8 convert_element_type.3
  68.0 4.0 %all-to-all-start.2 = ((bf16[4,64,768]{2,1,0:T(8,128)(2,1)}), bf16[4,64,768]{2,1,0:T(8,128)(2,1)S(1)}, u32[]{:S(2)}, u32[]{:S(2)}) async-start(bf16[4,64,768]{2,1,0:T(8,128)(2,1)} %convert_element_type.3), calls=%async_computation.2 | async-start | bytes 786432 | tf_op jit(solution)/shard_map/all_to_all | solution.py:288
  72.0 7.2 %all-to-all-done.2.others = bf16[4,64,768]{2,1,0:T(8,128)(2,1)S(1)} async-done(((bf16[4,64,768]{2,1,0:T(8,128)(2,1)}), bf16[4,64,768]{2,1,0:T(8,128)(2,1)S(1)}, u32[]{:S(2)}, u32[]{:S(2)}) %all-to-all-start.2) | async-done | bytes 393248 | tf_op jit(solution)/shard_map/all_to_all | solution.py:288
  79.2 0.1 shard_map.132.first
  79.3 13.4 %collective-permute-start.1 = (bf16[64,768]{1,0:T(8,128)(2,1)S(1)}, bf16[64,768]{1,0:T(8,128)(2,1)S(1)}, u32[]{:S(2)}, u32[]{:S(2)}) collective-permute-start(bf16[64,768]{1,0:T(8,128)(2,1)S(1)} %shard_map.132.first), channel_id=1, source_target_pairs={{0,512},{512,0},{1,513},{513,1},{2,514},{514,2},{3,515},{515,3},{4... | collective-permute-start | bytes 294920 | tf_op jit(solution)/shard_map/ppermute | solution.py:294
  92.7 0.0 copy-start
  92.7 0.0 copy-start.1
  92.7 2.0 %shard_map.133 = (f32[2,256,768]{2,1,0:T(8,128)S(1)}, f32[2,256,768]{2,1,0:T(8,128)S(1)}, f32[2,256,768]{2,1,0:T(8,128)S(1)}, bf16[768,256]{1,0:T(8,128)(2,1)}) custom-call(s32[1]{0:T(128)} %bitcast.me, bf16[2,256,768]{2,1,0:T(8,128)(2,1)S(1)} %bitcast.36, bf16[2,256,768]{2,1,0:T(8,128)(2,1)S(1)} %bitcast.37, f32[256,1]{1,0:T(8,128)S(1)} %get-tuple-element.31.probs0, ...), custom_call_target="tpu_custom_call" | custom-call | flops 201326592 | bytes 6291456 | tf_op jit(solution)/shard_map/pallas_call | solution.py:296
  94.7 20.5 %collective-permute-done.1.second = bf16[64,768]{1,0:T(8,128)(2,1)S(1)} collective-permute-done((bf16[64,768]{1,0:T(8,128)(2,1)S(1)}, bf16[64,768]{1,0:T(8,128)(2,1)S(1)}, u32[]{:S(2)}, u32[]{:S(2)}) %collective-permute-start.1) | collective-permute-done | bytes 98336 | tf_op jit(solution)/shard_map/ppermute | solution.py:294
  115.3 10.0 %all_to_all.31 = bf16[4,64,768]{2,1,0:T(8,128)(2,1)S(1)} all-to-all(bf16[4,64,768]{2,1,0:T(8,128)(2,1)S(1)} %shard_map.134), channel_id=1, replica_groups=mesh['zh'=2,'x'=4,'core'=2,'za'=4,'zb'=4,'y'=4] {'x'}, dimensions={0} | all-to-all | bytes 786432 | tf_op jit(solution)/shard_map/all_to_all | solution.py:309
  125.3 3.3 %collective-permute-start.2 = (bf16[256,768]{1,0:T(8,128)(2,1)S(1)}, bf16[256,768]{1,0:T(8,128)(2,1)S(1)}, u32[]{:S(2)}, u32[]{:S(2)}) collective-permute-start(bf16[256,768]{1,0:T(8,128)(2,1)S(1)} %bitcast.31), channel_id=1, source_target_pairs={{0,64},{64,0},{1,65},{65,1},{2,66},{66,2},{3,67},{67,3},{4,68},{68... | collective-permute-start | bytes 1179656 | tf_op jit(solution)/shard_map/ppermute | solution.py:310
  128.6 0.8 shard_map.135
  129.4 0.5 collective-permute-done.2.u_ref
  129.9 0.8 shard_map.136
  130.7 15.9 %all_to_all.32 = bf16[16,8,1152]{2,1,0:T(8,128)(2,1)S(1)} all-to-all(bf16[16,8,1152]{2,1,0:T(8,128)(2,1)S(1)} %bitcast.40), channel_id=1, replica_groups=mesh['zh'=2,'x'=4,'core'=2,'za'=4,'zb'=4,'y'=4] {'zb','y'}, dimensions={0} | all-to-all | bytes 589824 | tf_op jit(solution)/shard_map/all_to_all | solution.py:324
  146.6 1.4 shard_map.137
  148.1 3.7 %all-to-all-start.5 = ((bf16[4,16,640]{2,1,0:T(8,128)(2,1)}), bf16[4,16,640]{2,1,0:T(8,128)(2,1)S(1)}, u32[]{:S(2)}, u32[]{:S(2)}) async-start(bf16[4,16,640]{2,1,0:T(8,128)(2,1)} %bitcast.17), calls=%async_computation.5 | async-start | bytes 163840 | tf_op jit(solution)/shard_map/all_to_all | solution.py:332
  151.8 1.3 shard_map.139
  153.1 15.0 %all-to-all-done.5.parts = bf16[4,16,640]{2,1,0:T(8,128)(2,1)S(1)} async-done(((bf16[4,16,640]{2,1,0:T(8,128)(2,1)}), bf16[4,16,640]{2,1,0:T(8,128)(2,1)S(1)}, u32[]{:S(2)}, u32[]{:S(2)}) %all-to-all-start.5) | async-done | bytes 81952 | tf_op jit(solution)/shard_map/all_to_all | solution.py:332
  168.1 0.7 shard_map.138
  (9 shorter events, 0.0 us)
Async XLA Ops:
  2.2 38.6 %all-to-all-start = ((bf16[4,16,640]{2,1,0:T(8,128)(2,1)}), bf16[4,16,640]{2,1,0:T(8,128)(2,1)S(1)}, u32[]{:S(2)}, u32[]{:S(2)}) async-start(bf16[4,16,640]{2,1,0:T(8,128)(2,1)} %shard_map.128), calls=%async_computation | async-start | bytes 163840 | tf_op jit(solution)/shard_map/all_to_all | solution.py:268
  40.9 18.2 %copy-start.2 = (bf16[1,768,256]{2,1,0:T(8,128)(2,1)S(1)}, bf16[1,768,256]{2,1,0:T(8,128)(2,1)}, u32[]{:S(2)}) copy-start(bf16[1,768,256]{2,1,0:T(8,128)(2,1)} %param.17) | copy-start | bytes 1179652
  59.8 7.2 %collective-permute-start = (f32[256,768]{1,0:T(8,128)S(1)}, f32[256,768]{1,0:T(8,128)S(1)}, u32[]{:S(2)}, u32[]{:S(2)}) collective-permute-start(f32[256,768]{1,0:T(8,128)S(1)} %get-tuple-element.30), channel_id=1, source_target_pairs={{0,64},{64,0},{1,65},{65,1},{2,66},{66,2},{3,67},{67,3},{4,68},{68... | collective-permute-start | bytes 2359304 | tf_op jit(solution)/shard_map/ppermute | solution.py:285
  67.2 25.5 %copy-start.3 = (bf16[2,1,256,768]{3,2,1,0:T(8,128)(2,1)S(1)}, bf16[2,1,256,768]{3,2,1,0:T(8,128)(2,1)}, u32[]{:S(2)}) copy-start(bf16[2,1,256,768]{3,2,1,0:T(8,128)(2,1)} %param.13) | copy-start | bytes 2359300
  67.2 25.5 %copy-start.4 = (bf16[2,1,256,768]{3,2,1,0:T(8,128)(2,1)S(1)}, bf16[2,1,256,768]{3,2,1,0:T(8,128)(2,1)}, u32[]{:S(2)}) copy-start(bf16[2,1,256,768]{3,2,1,0:T(8,128)(2,1)} %param.14) | copy-start | bytes 2359300
  68.0 11.2 %all-to-all-start.2 = ((bf16[4,64,768]{2,1,0:T(8,128)(2,1)}), bf16[4,64,768]{2,1,0:T(8,128)(2,1)S(1)}, u32[]{:S(2)}, u32[]{:S(2)}) async-start(bf16[4,64,768]{2,1,0:T(8,128)(2,1)} %convert_element_type.3), calls=%async_computation.2 | async-start | bytes 786432 | tf_op jit(solution)/shard_map/all_to_all | solution.py:288
  79.3 35.9 %collective-permute-start.1 = (bf16[64,768]{1,0:T(8,128)(2,1)S(1)}, bf16[64,768]{1,0:T(8,128)(2,1)S(1)}, u32[]{:S(2)}, u32[]{:S(2)}) collective-permute-start(bf16[64,768]{1,0:T(8,128)(2,1)S(1)} %shard_map.132.first), channel_id=1, source_target_pairs={{0,512},{512,0},{1,513},{513,1},{2,514},{514,2},{3,515},{515,3},{4... | collective-permute-start | bytes 294920 | tf_op jit(solution)/shard_map/ppermute | solution.py:294
  92.7 35.9 %copy-start = (bf16[1,256,768]{2,1,0:T(8,128)(2,1)S(1)}, bf16[1,256,768]{2,1,0:T(8,128)(2,1)}, u32[]{:S(2)}) copy-start(bf16[1,256,768]{2,1,0:T(8,128)(2,1)} %param.15) | copy-start | bytes 1179652
  92.7 35.9 %copy-start.1 = (bf16[1,256,768]{2,1,0:T(8,128)(2,1)S(1)}, bf16[1,256,768]{2,1,0:T(8,128)(2,1)}, u32[]{:S(2)}) copy-start(bf16[1,256,768]{2,1,0:T(8,128)(2,1)} %param.16) | copy-start | bytes 1179652
  125.3 4.6 %collective-permute-start.2 = (bf16[256,768]{1,0:T(8,128)(2,1)S(1)}, bf16[256,768]{1,0:T(8,128)(2,1)S(1)}, u32[]{:S(2)}, u32[]{:S(2)}) collective-permute-start(bf16[256,768]{1,0:T(8,128)(2,1)S(1)} %bitcast.31), channel_id=1, source_target_pairs={{0,64},{64,0},{1,65},{65,1},{2,66},{66,2},{3,67},{67,3},{4,68},{68... | collective-permute-start | bytes 1179656 | tf_op jit(solution)/shard_map/ppermute | solution.py:310
  129.9 21.9 %copy-start.5 = (bf16[2,1,256,256]{3,2,1,0:T(8,128)(2,1)S(1)}, bf16[2,1,256,256]{3,2,1,0:T(8,128)(2,1)}, u32[]{:S(2)}) copy-start(bf16[2,1,256,256]{3,2,1,0:T(8,128)(2,1)} %param.12) | copy-start | bytes 786436
  148.1 20.1 %all-to-all-start.5 = ((bf16[4,16,640]{2,1,0:T(8,128)(2,1)}), bf16[4,16,640]{2,1,0:T(8,128)(2,1)S(1)}, u32[]{:S(2)}, u32[]{:S(2)}) async-start(bf16[4,16,640]{2,1,0:T(8,128)(2,1)} %bitcast.17), calls=%async_computation.5 | async-start | bytes 163840 | tf_op jit(solution)/shard_map/all_to_all | solution.py:332

commit v9 on v5

v9 whole, which is shorter than its diff:
```python
import functools

import jax
import jax.numpy as jnp
from jax import lax
from jax.experimental import pallas as pl
from jax.experimental.pallas import tpu as pltpu
from jax.sharding import Mesh
from jax.sharding import PartitionSpec as P

BF = jnp.bfloat16
F32 = jnp.float32
DP = ("zh", "x", "core")
EX = ("za", "zb", "y")
PLANE = ("zb", "y")
PAD = 128
SWAP = [(0, 1), (1, 0)]
VMEM = pl.BlockSpec(memory_space=pltpu.VMEM)
SMEM = pl.BlockSpec(memory_space=pltpu.SMEM)


def dot(a, b, ca, cb):
    return lax.dot_general(a, b, (((ca,), (cb,)), ((), ())), preferred_element_type=F32)


def iota(shape, dim):
    return lax.broadcasted_iota(jnp.int32, shape, dim)


def call(body, outs, n_in, flops, bytes_moved, limit=24, has_me=True):
    first = [SMEM] if has_me else []
    return pl.pallas_call(
        body,
        out_shape=outs,
        in_specs=first + [VMEM] * n_in,
        out_specs=[VMEM] * len(outs),
        cost_estimate=pl.CostEstimate(flops=flops, bytes_accessed=bytes_moved, transcendentals=0),
        compiler_params=pltpu.CompilerParams(vmem_limit_bytes=limit << 20),
    )


def flat_kernel(ids_in, probs_in, rows_in, out, ids, probs, rows, sems):
    copies = [
        pltpu.make_async_copy(source, held, sems.at[i])
        for i, (source, held) in enumerate(((ids_in, ids), (probs_in, probs), (rows_in, rows)))
    ]
    for copy in copies:
        copy.start()
    for copy in copies:
        copy.wait()
    mb, toks, width = rows.shape
    top = ids.shape[1]
    peers = out.shape[0] // mb
    ahead = iota((top, PAD), 1) - iota((top, PAD), 0)
    for m in range(mb):
        tail = dot(ids[m].astype(F32).astype(BF), (ahead == 0).astype(F32).astype(BF), 0, 0)
        tail = tail + dot(probs[m], (ahead == top).astype(F32).astype(BF), 0, 0)
        for peer in range(m * peers, (m + 1) * peers):
            out[peer, :, :width] = rows[m]
            out[peer, :, width:] = tail.astype(BF)


def route_maps(names, first, size, nq, toks, cap):
    tokens, top = names.shape
    shape = (tokens, size)
    column = iota(shape, 1)
    expert = (first + lax.div(column, nq)).astype(F32)
    same = lax.div(iota(shape, 0), toks) == lax.rem(column, nq)
    picks = [jnp.where(same & (names[:, k : k + 1] == expert), 1.0, 0.0) for k in range(top)]
    hits = functools.reduce(jnp.add, picks)
    lower = jnp.where(iota((tokens, tokens), 0) > iota((tokens, tokens), 1), 1.0, 0.0)
    slot = dot(lower.astype(BF), hits.astype(BF), 1, 0)
    return picks, [jnp.where(slot == s, hits, 0.0) for s in range(cap)]


def pack_kernel(dims, first, lines, out):
    nd, nq, toks, top, cap, width = dims
    tail_in = lines[:, width:].astype(F32)
    picks, maps = route_maps(tail_in[:, :top], first[0], nd * nq, nq, toks, cap)
    grads = lines[:, :width]
    tokens = grads.shape[0]
    held = functools.reduce(
        jnp.add, [k * tail_in[:, top + i : top + i + 1] for i, k in enumerate(picks)]
    )
    tail = jnp.zeros((nd * nq, PAD), F32)
    for s, k in enumerate(maps):
        out[:, s * width : (s + 1) * width] = dot(k.astype(BF), grads, 0, 0).astype(BF)
        lane = jnp.where(iota((tokens, PAD), 1) == s, 1.0, 0.0).astype(BF)
        tail = tail + dot((k * held).astype(BF), lane, 0, 0)
    out[:, cap * width :] = tail.astype(BF)


def unpack_kernel(dims, first, lines, home, out):
    nd, nq, toks, top, cap, width = dims
    names = lines[:, width:].astype(F32)[:, :top]
    picks, maps = route_maps(names, first[0], nd * nq, nq, toks, cap)
    tokens = names.shape[0]
    total = jnp.zeros((tokens, width), F32)
    held = jnp.zeros((tokens, nd * nq), F32)
    tail = home[:, cap * width :]
    for s, k in enumerate(maps):
        total = total + dot(k.astype(BF), home[:, s * width : (s + 1) * width], 1, 0)
        lane = jnp.where(iota((tokens, PAD), 1) == s, 1.0, 0.0).astype(BF)
        held = held + k * dot(lane, tail, 1, 1)
    out[:, :width] = total.astype(BF)
    lane = iota((tokens, PAD), 1)
    picked = jnp.zeros((tokens, PAD), F32)
    for i, k in enumerate(picks):
        picked = jnp.where(lane == i, jnp.sum(k * held, axis=1, keepdims=True), picked)
    out[:, width:] = picked.astype(BF)


def total_kernel(parts, in_grad, prob_grad):
    mb, toks, width = in_grad.shape
    top = prob_grad.shape[1]
    n = parts.shape[0] // mb
    column = (iota((top, PAD), 1) == iota((top, PAD), 0)).astype(F32).astype(BF)
    for m in range(mb):
        total = functools.reduce(
            jnp.add, [parts[i].astype(F32) for i in range(m * n, (m + 1) * n)]
        )
        in_grad[m] = total[:, :width].astype(BF)
        prob_grad[m] = dot(column, total[:, width:].astype(BF), 1, 1).astype(BF)


def first_row(shape, nd, nq, mb, cap):
    column = iota(shape, 1)
    return (lax.rem(lax.rem(column, nq), nq // mb) * nd + lax.div(column, nq)) * cap


def spread(nd, nq, mb, cap, m, s=None):
    rows = (nd * nq // mb) * cap
    shape = (rows, nd * nq)
    ahead = iota(shape, 0) - first_row(shape, nd, nq, mb, cap)
    here = (ahead >= 0) & (ahead < cap) if s is None else ahead == s
    here = here & (lax.div(lax.rem(iota(shape, 1), nq), nq // mb) == m)
    return jnp.where(here, 1.0, 0.0).astype(BF)


def down_kernel(nd, nq, nb, cap, me, got, w_mine, w_other, part, half, mine, other, probs):
    slots, width = mine.shape
    blocks = []
    for d in range(nb):
        total = jnp.zeros((slots, width), F32)
        for s in range(cap):
            total = total + dot(
                spread(nd, nq, nb, cap, d, s), got[:, s * width : (s + 1) * width], 1, 0
            )
        blocks.append(total)
    own = jnp.where(me[0] == 0, blocks[0], blocks[1]).astype(BF)
    far = jnp.where(me[0] == 0, blocks[1], blocks[0]).astype(BF)
    mine[...] = own
    other[...] = far
    total = dot(own, w_mine[...], 1, 1) + dot(far, w_other[...], 1, 1)
    part[...] = total
    half[...] = total.astype(BF)
    tail = dot(spread(nd, nq, nb, cap, 0), got[:, cap * width :], 1, 0)
    shape = (slots, PAD)
    probs[...] = jnp.sum(
        jnp.where(iota(shape, 1) == lax.rem(iota(shape, 0), cap), tail, 0.0), axis=1, keepdims=True
    )


def sum_kernel(mine, own, others, out):
    n = others.shape[0]
    total = functools.reduce(
        jnp.add, [jnp.where(mine[0] == i, own[i], others[i].astype(F32)) for i in range(n)]
    )
    out[...] = total.astype(BF)


def pair_kernel(first, second, out):
    total = (first[...].astype(F32) + second[...].astype(F32)).astype(BF)
    for i in range(out.shape[0]):
        out[i] = total


def act_kernel(me, gate, up, probs, f_gate, f_up, hidden):
    gate_f = gate[me[0]].astype(F32)
    up_f = up[me[0]].astype(F32)
    p = probs[...]
    sig = 1.0 / (1.0 + jnp.exp(-gate_f))
    act = gate_f * sig
    f_gate[...] = p * up_f * (sig * (1.0 + gate_f * (1.0 - sig)))
    f_up[...] = p * act
    hidden[...] = act * up_f


def down_grad_kernel(me, gate, up, probs0, probs1, rows0, rows1, grad):
    total = None
    for m, (probs, rows) in enumerate(((probs0, rows0), (probs1, rows1))):
        gate_f = gate[me[0] ^ m].astype(F32)
        act = gate_f * (1.0 / (1.0 + jnp.exp(-gate_f)))
        scaled = (probs[...] * (act * up[me[0] ^ m].astype(F32))).astype(BF)
        term = dot(scaled, rows[...], 0, 0)
        total = term if total is None else total + term
    grad[...] = total.astype(BF)


def slot_kernel(nd, nq, nb, cap, me, u_ref, f_gate, f_up, hidden, wg, wu, wg_far, wu_far, grads, out):
    u = u_ref[...].astype(F32)
    dg = (u * f_gate[...]).astype(BF)
    du = (u * f_up[...]).astype(BF)
    grads[0] = dg
    grads[1] = du
    own = dot(dg, wg[...], 1, 1) + dot(du, wu[...], 1, 1)
    far = dot(dg, wg_far[...], 1, 1) + dot(du, wu_far[...], 1, 1)
    blocks = [
        jnp.where(me[0] == 0, own, far).astype(BF),
        jnp.where(me[0] == 0, far, own).astype(BF),
    ]
    slots, width = blocks[0].shape
    for s in range(cap):
        lines = functools.reduce(
            jnp.add, [dot(spread(nd, nq, nb, cap, d, s), blocks[d], 0, 0) for d in range(nb)]
        )
        out[:, s * width : (s + 1) * width] = lines.astype(BF)
    slot_prob = jnp.sum(u * hidden[...], axis=1, keepdims=True)
    shape = (slots, PAD)
    tail = jnp.where(iota(shape, 1) == lax.rem(iota(shape, 0), cap), slot_prob, 0.0).astype(BF)
    tails = functools.reduce(
        jnp.add, [dot(spread(nd, nq, nb, cap, d), tail, 0, 0) for d in range(nb)]
    )
    out[:, cap * width :] = tails.astype(BF)


def weight_kernel(me, inputs, grads0, grads1, grad_gate, grad_up):
    first, second = inputs[me[0]], inputs[me[0] ^ 1]
    for i, out in enumerate((grad_gate, grad_up)):
        out[...] = (dot(first, grads0[i], 0, 0) + dot(second, grads1[i], 0, 0)).astype(BF)


def local(out_grad, expert_ids, probs, saved_inputs, gate_pre, up_pre, w_gate, w_up, w_down):
    sds = jax.ShapeDtypeStruct
    ne = lax.axis_size(EX)
    n_x = lax.axis_size("x")
    mb, toks, top = expert_ids.shape
    slots = saved_inputs.shape[2]
    cap = slots // ne
    width = out_grad.shape[2]
    ff = w_gate.shape[2]
    line = cap * width + PAD
    w_gate, w_up, w_down = w_gate[0], w_up[0], w_down[0]
    core = lax.axis_index("core")
    me = core.astype(jnp.int32).reshape(1)
    product = 2 * slots * width * ff

    n_a, nd = lax.axis_size("za"), lax.axis_size(PLANE)
    nb = mb
    nq = n_a * nb
    dims = (nd, nq, toks, top, cap, width)
    wide = width + PAD
    first = (lax.axis_index("za").astype(jnp.int32) * nd).reshape(1)

    hbm = pl.BlockSpec(memory_space=pltpu.HBM)
    flat = pl.pallas_call(
        flat_kernel,
        out_shape=sds((nq, toks, wide), BF),
        in_specs=[hbm, hbm, hbm],
        out_specs=VMEM,
        scratch_shapes=[
            pltpu.VMEM((mb, top, toks), jnp.int32),
            pltpu.VMEM((mb, top, toks), BF),
            pltpu.VMEM((mb, toks, width), BF),
            pltpu.SemaphoreType.DMA((3,)),
        ],
        compiler_params=pltpu.CompilerParams(vmem_limit_bytes=56 << 20),
    )(jnp.swapaxes(expert_ids, 1, 2), jnp.swapaxes(probs, 1, 2), out_grad)
    flat, w_down = lax.optimization_barrier((flat, w_down))
    w_far = lax.ppermute(w_down, "core", SWAP)
    lines = lax.all_to_all(flat, ("core", "za"), 0, 0, tiled=True).reshape(nq * toks, wide)
    send = call(
        functools.partial(pack_kernel, dims), [sds((nd * nq, line), BF)], 1, 16 * product, nd * nq * line * 64
    )(first, lines)[0]
    got = lax.all_to_all(send.reshape(nd, nq, line), PLANE, 0, 0, tiled=True).reshape(nd * nq, line)
    part, half, rows0, rows_far, probs0 = call(
        functools.partial(down_kernel, nd, nq, nb, cap),
        [
            sds((slots, ff), F32),
            sds((slots, ff), BF),
            sds((slots, width), BF),
            sds((slots, width), BF),
            sds((slots, 1), F32),
        ],
        3,
        2 * product,
        slots * ff * 6,
    )(me, got, w_down, w_far)
    half = half.reshape(n_x, slots // n_x, ff)
    part = part.reshape(n_x, slots // n_x, ff)
    others = lax.all_to_all(half, "x", 0, 0, tiled=True)
    mine = lax.axis_index("x").astype(jnp.int32).reshape(1)
    piece = (slots // n_x, ff)
    eighth = call(
        sum_kernel, [sds(piece, BF)], 2, 0, slots * ff * 6
    )(mine, part, others)[0]
    other = lax.ppermute(eighth, "zh", SWAP)

    probs_later, _ = lax.optimization_barrier((probs0, eighth))
    f_gate, f_up, hidden = call(
        act_kernel, [sds((slots, ff), F32)] * 3, 3, slots * ff * 20, slots * ff * 16
    )(me, gate_pre[:, 0], up_pre[:, 0], probs_later)
    f_gate, w_gate_now, w_up_now, rows_far, probs_now = lax.optimization_barrier(
        (f_gate, w_gate, w_up, rows_far, probs0)
    )
    wg_far = lax.ppermute(w_gate_now, "core", SWAP)
    wu_far = lax.ppermute(w_up_now, "core", SWAP)
    rows1 = lax.ppermute(rows_far, "core", SWAP)
    probs1 = lax.ppermute(probs_now, "core", SWAP)
    grad_down = call(
        down_grad_kernel, [sds((ff, width), BF)], 6, 2 * product, slots * ff * 12
    )(me, gate_pre[:, 0], up_pre[:, 0], probs0, probs1, rows0, rows1)[0]

    other, f_gate, f_up, hidden, wg_far, wu_far, grad_down = lax.optimization_barrier(
        (other, f_gate, f_up, hidden, wg_far, wu_far, grad_down)
    )
    u = call(
        pair_kernel, [sds((n_x,) + piece, BF)], 2, 0, slots * ff * 2, has_me=False
    )(eighth, other)[0]
    u0 = lax.all_to_all(u, "x", 0, 0, tiled=True).reshape(slots, ff)
    grads0, back = call(
        functools.partial(slot_kernel, nd, nq, nb, cap),
        [sds((2, slots, ff), BF), sds((nd * nq, line), BF)],
        8,
        4 * product,
        slots * ff * 24,
    )(me, u0, f_gate, f_up, hidden, w_gate, w_up, wg_far, wu_far)
    home = lax.all_to_all(back.reshape(nd, nq, line), PLANE, 0, 0, tiled=True)
    part = call(
        functools.partial(unpack_kernel, dims),
        [sds((nq * toks, wide), BF)],
        2,
        product // 4,
        nd * nq * line * 2,
    )(first, lines, home.reshape(nd * nq, line))[0]
    grads1 = lax.ppermute(grads0, "core", SWAP)
    part = lax.all_to_all(part.reshape(nq, toks, wide), ("core", "za"), 0, 0, tiled=True)
    grad_gate, grad_up = call(
        weight_kernel, [sds((width, ff), BF)] * 2, 3, 4 * product, slots * ff * 12
    )(me, saved_inputs[:, 0], grads0, grads1)
    in_grad, prob_grad = call(
        total_kernel,
        [sds((mb, toks, width), BF), sds((mb, top, toks), BF)],
        1,
        0,
        toks * width * 20,
        has_me=False,
    )(part)
    prob_grad = jnp.swapaxes(prob_grad, 1, 2)
    return in_grad, prob_grad, grad_gate[None], grad_up[None], grad_down[None]


def solution(mesh):
    n_dp, n_ex = mesh.devices.shape
    n_a = 4 if n_ex >= 64 else 2
    fine = Mesh(
        mesh.devices.reshape(2, n_dp // 4, 2, n_a, n_ex // (4 * n_a), 4),
        ("zh", "x", "core", "za", "zb", "y"),
    )
    specs = (
        P(None, EX, DP),
        P(None, EX, None),
        P(None, EX, None),
        P(None, EX, None, DP),
        P(None, EX, None, None),
        P(None, EX, None, None),
        P(EX, DP, None),
        P(EX, DP, None),
        P(EX, None, DP),
    )
    return jax.shard_map(
        local,
        mesh=fine,
        in_specs=specs,
        out_specs=(specs[0], specs[1], specs[6], specs[7], specs[8]),
        check_vma=False,
    )
```

time: 176 us -> 181 us (1.028)
  the two profiles are of different devices: /device:TPU:2 before, /device:TPU:1 now
where the time goes in v9:
time: 181 us; the launch traced here: 180 us
  starting transfers between devices  79.9 us (44%)
  waiting for transfers between devices  77.3 us (43%)
  Pallas kernels  11.6 us (6%)
  blocking collectives  10 us (6%)
    all_to_all x1, starting transfers between devices, local(): lax.all_to_all(flat, ('core', 'za'), 0, 0, tiled=True)  23.2 us
    all_to_all x1, waiting for transfers between devices, local(): lax.all_to_all(flat, ('core', 'za'), 0, 0, tiled=True)  22.4 us
    all_to_all x1, waiting for transfers between devices, local(): lax.all_to_all(part.reshape(nq, toks, wide), ('core', 'za'), 0, 0, tiled=...  21.2 us
    ppermute x1, starting transfers between devices, local(): other = lax.ppermute(eighth, 'zh', SWAP)  14.3 us
    ppermute x1, waiting for transfers between devices, local(): other = lax.ppermute(eighth, 'zh', SWAP)  12.8 us
    all_to_all x1, blocking collectives, local(): u0 = lax.all_to_all(u, 'x', 0, 0, tiled=True).reshape(slots, ff)  10 us
    all_to_all x1, starting transfers between devices, local(): home = lax.all_to_all(back.reshape(nd, nq, line), PLANE, 0, 0, tiled=True)  9.94 us
    all_to_all x1, waiting for transfers between devices, local(): lax.all_to_all(send.reshape(nd, nq, line), PLANE, 0, 0, tiled=True)  6.41 us
  transfers between devices with their start and end apart: 12, of which 8 were waited for; matrix products, arithmetic and copies ran while one was open for 0% of the time, Pallas kernels for 2%

profile of v9, /device:TPU:1, one launch (start us, length us, event | category | flops | bytes accessed | tf_op | source)
XLA Modules:
  0.0 180.2 jit_solution(8559401530285877026)
XLA Ops:
  0.6 1.6 shard_map.128
  2.2 23.2 %all-to-all-start = ((bf16[8,16,384]{2,1,0:T(8,128)(2,1)}), bf16[8,16,384]{2,1,0:T(8,128)(2,1)S(1)}, u32[]{:S(2)}, u32[]{:S(2)}) async-start(bf16[8,16,384]{2,1,0:T(8,128)(2,1)} %shard_map.128), calls=%async_computation | async-start | bytes 196608 | tf_op jit(solution)/shard_map/all_to_all | solution.py:271
  25.5 22.4 %all-to-all-done = bf16[8,16,384]{2,1,0:T(8,128)(2,1)S(1)} async-done(((bf16[8,16,384]{2,1,0:T(8,128)(2,1)}), bf16[8,16,384]{2,1,0:T(8,128)(2,1)S(1)}, u32[]{:S(2)}, u32[]{:S(2)}) %all-to-all-start) | async-done | bytes 98336 | tf_op jit(solution)/shard_map/all_to_all | solution.py:271
  47.9 1.3 shard_map.129
  49.2 4.4 %all-to-all-start.1 = ((bf16[16,8,1152]{2,1,0:T(8,128)(2,1)}), bf16[16,8,1152]{2,1,0:T(8,128)(2,1)S(1)}, u32[]{:S(2)}, u32[]{:S(2)}) async-start(bf16[16,8,1152]{2,1,0:T(8,128)(2,1)} %bitcast.7), calls=%async_computation.1 | async-start | bytes 589824 | tf_op jit(solution)/shard_map/all_to_all | solution.py:275
  53.6 2.6 %collective-permute-start = (bf16[768,256]{1,0:T(8,128)(2,1)S(1)}, bf16[768,256]{1,0:T(8,128)(2,1)S(1)}, u32[]{:S(2)}, u32[]{:S(2)}) collective-permute-start(bf16[768,256]{1,0:T(8,128)(2,1)S(1)} %bitcast.38), channel_id=1, source_target_pairs={{0,64},{64,0},{1,65},{65,1},{2,66},{66,2},{3,67},{67,3},{4,68},{68... | collective-permute-start | bytes 1179656 | tf_op jit(solution)/shard_map/ppermute | solution.py:270
  56.3 1.3 collective-permute-done.w_other
  57.6 6.4 %all-to-all-done.1 = bf16[16,8,1152]{2,1,0:T(8,128)(2,1)S(1)} async-done(((bf16[16,8,1152]{2,1,0:T(8,128)(2,1)}), bf16[16,8,1152]{2,1,0:T(8,128)(2,1)S(1)}, u32[]{:S(2)}, u32[]{:S(2)}) %all-to-all-start.1) | async-done | bytes 294944 | tf_op jit(solution)/shard_map/all_to_all | solution.py:275
  64.0 1.6 shard_map.130
  65.6 4.1 %all-to-all-start.2 = ((bf16[4,64,768]{2,1,0:T(8,128)(2,1)}), bf16[4,64,768]{2,1,0:T(8,128)(2,1)S(1)}, u32[]{:S(2)}, u32[]{:S(2)}) async-start(bf16[4,64,768]{2,1,0:T(8,128)(2,1)} %bitcast.10), calls=%async_computation.2 | async-start | bytes 786432 | tf_op jit(solution)/shard_map/all_to_all | solution.py:291
  69.7 6.2 %all-to-all-done.2.others = bf16[4,64,768]{2,1,0:T(8,128)(2,1)S(1)} async-done(((bf16[4,64,768]{2,1,0:T(8,128)(2,1)}), bf16[4,64,768]{2,1,0:T(8,128)(2,1)S(1)}, u32[]{:S(2)}, u32[]{:S(2)}) %all-to-all-start.2) | async-done | bytes 393248 | tf_op jit(solution)/shard_map/all_to_all | solution.py:291
  76.0 0.1 shard_map.131.first
  76.1 0.4 shard_map.132
  76.6 0.5 copy-done.2
  77.1 5.2 %collective-permute-start.2 = (bf16[256,768]{1,0:T(8,128)(2,1)S(1)}, bf16[256,768]{1,0:T(8,128)(2,1)S(1)}, u32[]{:S(2)}, u32[]{:S(2)}) collective-permute-start(bf16[256,768]{1,0:T(8,128)(2,1)S(1)} %bitcast.32), channel_id=1, source_target_pairs={{0,64},{64,0},{1,65},{65,1},{2,66},{66,2},{3,67},{67,3},{4,68},{68... | collective-permute-start | bytes 1179656 | tf_op jit(solution)/shard_map/ppermute | solution.py:306
  82.2 1.9 %collective-permute-start.3 = (bf16[256,768]{1,0:T(8,128)(2,1)S(1)}, bf16[256,768]{1,0:T(8,128)(2,1)S(1)}, u32[]{:S(2)}, u32[]{:S(2)}) collective-permute-start(bf16[256,768]{1,0:T(8,128)(2,1)S(1)} %bitcast.34), channel_id=1, source_target_pairs={{0,64},{64,0},{1,65},{65,1},{2,66},{66,2},{3,67},{67,3},{4,68},{68... | collective-permute-start | bytes 1179656 | tf_op jit(solution)/shard_map/ppermute | solution.py:307
  84.2 2.4 %collective-permute-start.5 = (bf16[256,256]{1,0:T(8,128)(2,1)S(1)}, bf16[256,256]{1,0:T(8,128)(2,1)S(1)}, u32[]{:S(2)}, u32[]{:S(2)}) collective-permute-start(bf16[256,256]{1,0:T(8,128)(2,1)S(1)} %get-tuple-element.49), channel_id=1, source_target_pairs={{0,64},{64,0},{1,65},{65,1},{2,66},{66,2},{3,67},{67,3},{4,68},{68... | collective-permute-start | bytes 393224 | tf_op jit(solution)/shard_map/ppermute | solution.py:308
  86.6 14.3 %collective-permute-start.1 = (bf16[64,768]{1,0:T(8,128)(2,1)S(1)}, bf16[64,768]{1,0:T(8,128)(2,1)S(1)}, u32[]{:S(2)}, u32[]{:S(2)}) collective-permute-start(bf16[64,768]{1,0:T(8,128)(2,1)S(1)} %shard_map.131.first), channel_id=1, source_target_pairs={{0,512},{512,0},{1,513},{513,1},{2,514},{514,2},{3,515},{515,3},{4... | collective-permute-start | bytes 294920 | tf_op jit(solution)/shard_map/ppermute | solution.py:297
  100.9 2.2 %collective-permute-start.4 = (f32[256,1]{1,0:T(8,128)S(1)}, f32[256,1]{1,0:T(8,128)S(1)}, u32[]{:S(2)}, u32[]{:S(2)}) collective-permute-start(f32[256,1]{1,0:T(8,128)S(1)} %get-tuple-element.47.probs.probs0), channel_id=1, source_target_pairs={{0,64},{64,0},{1,65},{65,1},{2,66},{66,2},{3,67},{67,3},{4,68},{68... | collective-permute-start | bytes 3080 | tf_op jit(solution)/shard_map/ppermute | solution.py:309
  103.2 1.0 collective-permute-done.4.probs1
  104.2 1.7 shard_map.133
  105.8 12.8 %collective-permute-done.1.second = bf16[64,768]{1,0:T(8,128)(2,1)S(1)} collective-permute-done((bf16[64,768]{1,0:T(8,128)(2,1)S(1)}, bf16[64,768]{1,0:T(8,128)(2,1)S(1)}, u32[]{:S(2)}, u32[]{:S(2)}) %collective-permute-start.1) | collective-permute-done | bytes 98336 | tf_op jit(solution)/shard_map/ppermute | solution.py:297
  118.7 10.0 %all_to_all.30 = bf16[4,64,768]{2,1,0:T(8,128)(2,1)S(1)} all-to-all(bf16[4,64,768]{2,1,0:T(8,128)(2,1)S(1)} %shard_map.134), channel_id=1, replica_groups=mesh['zh'=2,'x'=4,'core'=2,'za'=4,'zb'=4,'y'=4] {'x'}, dimensions={0} | all-to-all | bytes 786432 | tf_op jit(solution)/shard_map/all_to_all | solution.py:320
  128.7 1.7 shard_map.135
  130.4 9.9 %all-to-all-start.4 = ((bf16[16,8,1152]{2,1,0:T(8,128)(2,1)}), bf16[16,8,1152]{2,1,0:T(8,128)(2,1)S(1)}, u32[]{:S(2)}, u32[]{:S(2)}) async-start(bf16[16,8,1152]{2,1,0:T(8,128)(2,1)} %bitcast.16), calls=%async_computation.4 | async-start | bytes 589824 | tf_op jit(solution)/shard_map/all_to_all | solution.py:328
  140.3 3.5 %collective-permute-start.6 = (bf16[2,256,768]{2,1,0:T(8,128)(2,1)S(1)}, bf16[2,256,768]{2,1,0:T(8,128)(2,1)S(1)}, u32[]{:S(2)}, u32[]{:S(2)}) collective-permute-start(bf16[2,256,768]{2,1,0:T(8,128)(2,1)S(1)} %get-tuple-element.59.grads0), channel_id=1, source_target_pairs={{0,64},{64,0},{1,65},{65,1},{2,66},{66,2},{3,67},{67,3},{4,68},{68... | collective-permute-start | bytes 2359304 | tf_op jit(solution)/shard_map/ppermute | solution.py:336
  143.8 5.9 %all-to-all-done.4 = bf16[16,8,1152]{2,1,0:T(8,128)(2,1)S(1)} async-done(((bf16[16,8,1152]{2,1,0:T(8,128)(2,1)}), bf16[16,8,1152]{2,1,0:T(8,128)(2,1)S(1)}, u32[]{:S(2)}, u32[]{:S(2)}) %all-to-all-start.4) | async-done | bytes 294944 | tf_op jit(solution)/shard_map/all_to_all | solution.py:328
  149.7 1.2 shard_map.136
  150.9 6.1 %all-to-all-start.5 = ((bf16[8,16,384]{2,1,0:T(8,128)(2,1)}), bf16[8,16,384]{2,1,0:T(8,128)(2,1)S(1)}, u32[]{:S(2)}, u32[]{:S(2)}) async-start(bf16[8,16,384]{2,1,0:T(8,128)(2,1)} %bitcast.18), calls=%async_computation.5 | async-start | bytes 196608 | tf_op jit(solution)/shard_map/all_to_all | solution.py:337
  157.0 1.3 shard_map.138
  158.3 21.2 %all-to-all-done.5.parts = bf16[8,16,384]{2,1,0:T(8,128)(2,1)S(1)} async-done(((bf16[8,16,384]{2,1,0:T(8,128)(2,1)}), bf16[8,16,384]{2,1,0:T(8,128)(2,1)S(1)}, u32[]{:S(2)}, u32[]{:S(2)}) %all-to-all-start.5) | async-done | bytes 98336 | tf_op jit(solution)/shard_map/all_to_all | solution.py:337
  179.5 0.7 shard_map.137
  (16 shorter events, 0.1 us)
Async XLA Ops:
  2.2 45.7 %all-to-all-start = ((bf16[8,16,384]{2,1,0:T(8,128)(2,1)}), bf16[8,16,384]{2,1,0:T(8,128)(2,1)S(1)}, u32[]{:S(2)}, u32[]{:S(2)}) async-start(bf16[8,16,384]{2,1,0:T(8,128)(2,1)} %shard_map.128), calls=%async_computation | async-start | bytes 196608 | tf_op jit(solution)/shard_map/all_to_all | solution.py:271
  49.2 4.4 %copy-start.4 = (bf16[1,768,256]{2,1,0:T(8,128)(2,1)S(1)}, bf16[1,768,256]{2,1,0:T(8,128)(2,1)}, u32[]{:S(2)}) copy-start(bf16[1,768,256]{2,1,0:T(8,128)(2,1)} %param.17) | copy-start | bytes 1179652
  49.2 14.8 %all-to-all-start.1 = ((bf16[16,8,1152]{2,1,0:T(8,128)(2,1)}), bf16[16,8,1152]{2,1,0:T(8,128)(2,1)S(1)}, u32[]{:S(2)}, u32[]{:S(2)}) async-start(bf16[16,8,1152]{2,1,0:T(8,128)(2,1)} %bitcast.7), calls=%async_computation.1 | async-start | bytes 589824 | tf_op jit(solution)/shard_map/all_to_all | solution.py:275
  53.6 4.0 %collective-permute-start = (bf16[768,256]{1,0:T(8,128)(2,1)S(1)}, bf16[768,256]{1,0:T(8,128)(2,1)S(1)}, u32[]{:S(2)}, u32[]{:S(2)}) collective-permute-start(bf16[768,256]{1,0:T(8,128)(2,1)S(1)} %bitcast.38), channel_id=1, source_target_pairs={{0,64},{64,0},{1,65},{65,1},{2,66},{66,2},{3,67},{67,3},{4,68},{68... | collective-permute-start | bytes 1179656 | tf_op jit(solution)/shard_map/ppermute | solution.py:270
  65.6 10.5 %copy-start.1 = (bf16[2,1,256,768]{3,2,1,0:T(8,128)(2,1)S(1)}, bf16[2,1,256,768]{3,2,1,0:T(8,128)(2,1)}, u32[]{:S(2)}) copy-start(bf16[2,1,256,768]{3,2,1,0:T(8,128)(2,1)} %param.14) | copy-start | bytes 2359300
  65.6 10.4 %all-to-all-start.2 = ((bf16[4,64,768]{2,1,0:T(8,128)(2,1)}), bf16[4,64,768]{2,1,0:T(8,128)(2,1)S(1)}, u32[]{:S(2)}, u32[]{:S(2)}) async-start(bf16[4,64,768]{2,1,0:T(8,128)(2,1)} %bitcast.10), calls=%async_computation.2 | async-start | bytes 786432 | tf_op jit(solution)/shard_map/all_to_all | solution.py:291
  69.7 6.3 %copy-start = (bf16[2,1,256,768]{3,2,1,0:T(8,128)(2,1)S(1)}, bf16[2,1,256,768]{3,2,1,0:T(8,128)(2,1)}, u32[]{:S(2)}) copy-start(bf16[2,1,256,768]{3,2,1,0:T(8,128)(2,1)} %param.13) | copy-start | bytes 2359300
  76.1 1.0 copy-start.2
  76.1 6.2 %copy-start.3 = (bf16[1,256,768]{2,1,0:T(8,128)(2,1)S(1)}, bf16[1,256,768]{2,1,0:T(8,128)(2,1)}, u32[]{:S(2)}) copy-start(bf16[1,256,768]{2,1,0:T(8,128)(2,1)} %param.16) | copy-start | bytes 1179652
  77.1 41.6 %collective-permute-start.2 = (bf16[256,768]{1,0:T(8,128)(2,1)S(1)}, bf16[256,768]{1,0:T(8,128)(2,1)S(1)}, u32[]{:S(2)}, u32[]{:S(2)}) collective-permute-start(bf16[256,768]{1,0:T(8,128)(2,1)S(1)} %bitcast.32), channel_id=1, source_target_pairs={{0,64},{64,0},{1,65},{65,1},{2,66},{66,2},{3,67},{67,3},{4,68},{68... | collective-permute-start | bytes 1179656 | tf_op jit(solution)/shard_map/ppermute | solution.py:306
  82.2 36.4 %collective-permute-start.3 = (bf16[256,768]{1,0:T(8,128)(2,1)S(1)}, bf16[256,768]{1,0:T(8,128)(2,1)S(1)}, u32[]{:S(2)}, u32[]{:S(2)}) collective-permute-start(bf16[256,768]{1,0:T(8,128)(2,1)S(1)} %bitcast.34), channel_id=1, source_target_pairs={{0,64},{64,0},{1,65},{65,1},{2,66},{66,2},{3,67},{67,3},{4,68},{68... | collective-permute-start | bytes 1179656 | tf_op jit(solution)/shard_map/ppermute | solution.py:307
  84.2 20.0 %collective-permute-start.5 = (bf16[256,256]{1,0:T(8,128)(2,1)S(1)}, bf16[256,256]{1,0:T(8,128)(2,1)S(1)}, u32[]{:S(2)}, u32[]{:S(2)}) collective-permute-start(bf16[256,256]{1,0:T(8,128)(2,1)S(1)} %get-tuple-element.49), channel_id=1, source_target_pairs={{0,64},{64,0},{1,65},{65,1},{2,66},{66,2},{3,67},{67,3},{4,68},{68... | collective-permute-start | bytes 393224 | tf_op jit(solution)/shard_map/ppermute | solution.py:308
  86.6 32.0 %collective-permute-start.1 = (bf16[64,768]{1,0:T(8,128)(2,1)S(1)}, bf16[64,768]{1,0:T(8,128)(2,1)S(1)}, u32[]{:S(2)}, u32[]{:S(2)}) collective-permute-start(bf16[64,768]{1,0:T(8,128)(2,1)S(1)} %shard_map.131.first), channel_id=1, source_target_pairs={{0,512},{512,0},{1,513},{513,1},{2,514},{514,2},{3,515},{515,3},{4... | collective-permute-start | bytes 294920 | tf_op jit(solution)/shard_map/ppermute | solution.py:297
  100.9 3.2 %collective-permute-start.4 = (f32[256,1]{1,0:T(8,128)S(1)}, f32[256,1]{1,0:T(8,128)S(1)}, u32[]{:S(2)}, u32[]{:S(2)}) collective-permute-start(f32[256,1]{1,0:T(8,128)S(1)} %get-tuple-element.47.probs.probs0), channel_id=1, source_target_pairs={{0,64},{64,0},{1,65},{65,1},{2,66},{66,2},{3,67},{67,3},{4,68},{68... | collective-permute-start | bytes 3080 | tf_op jit(solution)/shard_map/ppermute | solution.py:309
  130.4 19.3 %all-to-all-start.4 = ((bf16[16,8,1152]{2,1,0:T(8,128)(2,1)}), bf16[16,8,1152]{2,1,0:T(8,128)(2,1)S(1)}, u32[]{:S(2)}, u32[]{:S(2)}) async-start(bf16[16,8,1152]{2,1,0:T(8,128)(2,1)} %bitcast.16), calls=%async_computation.4 | async-start | bytes 589824 | tf_op jit(solution)/shard_map/all_to_all | solution.py:328
  140.3 16.6 %collective-permute-start.6 = (bf16[2,256,768]{2,1,0:T(8,128)(2,1)S(1)}, bf16[2,256,768]{2,1,0:T(8,128)(2,1)S(1)}, u32[]{:S(2)}, u32[]{:S(2)}) collective-permute-start(bf16[2,256,768]{2,1,0:T(8,128)(2,1)S(1)} %get-tuple-element.59.grads0), channel_id=1, source_target_pairs={{0,64},{64,0},{1,65},{65,1},{2,66},{66,2},{3,67},{67,3},{4,68},{68... | collective-permute-start | bytes 2359304 | tf_op jit(solution)/shard_map/ppermute | solution.py:336
  149.7 7.3 %copy-start.5 = (bf16[2,1,256,256]{3,2,1,0:T(8,128)(2,1)S(1)}, bf16[2,1,256,256]{3,2,1,0:T(8,128)(2,1)}, u32[]{:S(2)}) copy-start(bf16[2,1,256,256]{3,2,1,0:T(8,128)(2,1)} %param.12) | copy-start | bytes 786436
  150.9 28.6 %all-to-all-start.5 = ((bf16[8,16,384]{2,1,0:T(8,128)(2,1)}), bf16[8,16,384]{2,1,0:T(8,128)(2,1)S(1)}, u32[]{:S(2)}, u32[]{:S(2)}) async-start(bf16[8,16,384]{2,1,0:T(8,128)(2,1)} %bitcast.18), calls=%async_computation.5 | async-start | bytes 196608 | tf_op jit(solution)/shard_map/all_to_all | solution.py:337

commit v10 on v9

--- a/solution.py
+++ b/solution.py
@@ -266,9 +266,10 @@
         ],
         compiler_params=pltpu.CompilerParams(vmem_limit_bytes=56 << 20),
     )(jnp.swapaxes(expert_ids, 1, 2), jnp.swapaxes(probs, 1, 2), out_grad)
-    flat, w_down = lax.optimization_barrier((flat, w_down))
-    w_far = lax.ppermute(w_down, "core", SWAP)
+    flat, *sent = lax.optimization_barrier((flat, w_down, w_gate, w_up))
+    w_far, wg_far, wu_far = [lax.ppermute(w, "core", SWAP) for w in sent]
     lines = lax.all_to_all(flat, ("core", "za"), 0, 0, tiled=True).reshape(nq * toks, wide)
+    lines, w_far, wg_far, wu_far = lax.optimization_barrier((lines, w_far, wg_far, wu_far))
     send = call(
         functools.partial(pack_kernel, dims), [sds((nd * nq, line), BF)], 1, 16 * product, nd * nq * line * 64
     )(first, lines)[0]
@@ -300,20 +301,8 @@
     f_gate, f_up, hidden = call(
         act_kernel, [sds((slots, ff), F32)] * 3, 3, slots * ff * 20, slots * ff * 16
     )(me, gate_pre[:, 0], up_pre[:, 0], probs_later)
-    f_gate, w_gate_now, w_up_now, rows_far, probs_now = lax.optimization_barrier(
-        (f_gate, w_gate, w_up, rows_far, probs0)
-    )
-    wg_far = lax.ppermute(w_gate_now, "core", SWAP)
-    wu_far = lax.ppermute(w_up_now, "core", SWAP)
-    rows1 = lax.ppermute(rows_far, "core", SWAP)
-    probs1 = lax.ppermute(probs_now, "core", SWAP)
-    grad_down = call(
-        down_grad_kernel, [sds((ff, width), BF)], 6, 2 * product, slots * ff * 12
-    )(me, gate_pre[:, 0], up_pre[:, 0], probs0, probs1, rows0, rows1)[0]
-
-    other, f_gate, f_up, hidden, wg_far, wu_far, grad_down = lax.optimization_barrier(
-        (other, f_gate, f_up, hidden, wg_far, wu_far, grad_down)
-    )
+
+    other, f_gate, f_up, hidden = lax.optimization_barrier((other, f_gate, f_up, hidden))
     u = call(
         pair_kernel, [sds((n_x,) + piece, BF)], 2, 0, slots * ff * 2, has_me=False
     )(eighth, other)[0]
@@ -333,7 +322,15 @@
         product // 4,
         nd * nq * line * 2,
     )(first, lines, home.reshape(nd * nq, line))[0]
-    grads1 = lax.ppermute(grads0, "core", SWAP)
+    part, grads_now, rows_far, probs_now = lax.optimization_barrier(
+        (part, grads0, rows_far, probs0)
+    )
+    grads1 = lax.ppermute(grads_now, "core", SWAP)
+    rows1 = lax.ppermute(rows_far, "core", SWAP)
+    probs1 = lax.ppermute(probs_now, "core", SWAP)
+    grad_down = call(
+        down_grad_kernel, [sds((ff, width), BF)], 6, 2 * product, slots * ff * 12
+    )(me, gate_pre[:, 0], up_pre[:, 0], probs0, probs1, rows0, rows1)[0]
     part = lax.all_to_all(part.reshape(nq, toks, wide), ("core", "za"), 0, 0, tiled=True)
     grad_gate, grad_up = call(
         weight_kernel, [sds((width, ff), BF)] * 2, 3, 4 * product, slots * ff * 12

time: 181 us -> 175 us (0.967)
  blocking collectives: 10 us -> 27 us
  starting transfers between devices: 79.9 us -> 64.9 us
  waiting for transfers between devices: 77.3 us -> 69.1 us
    all_to_all x0 -> x1, blocking collectives: none -> 17.4 us  [local(): home = lax.all_to_all(back.reshape(nd, nq, line), PLANE, 0, 0, tiled=True)]
    all_to_all x1 -> x0, starting transfers between devices: 9.94 us -> none  [local(): home = lax.all_to_all(back.reshape(nd, nq, line), PLANE, 0, 0, tiled=True)]
    all_to_all x1, waiting for transfers between devices: 22.4 us -> 14.3 us  [local(): lax.all_to_all(flat, ('core', 'za'), 0, 0, tiled=True)]
    ppermute x1, waiting for transfers between devices: 12.8 us -> 19.9 us  [local(): other = lax.ppermute(eighth, 'zh', SWAP)]
    all_to_all x1 -> x0, waiting for transfers between devices: 5.91 us -> none  [local(): home = lax.all_to_all(back.reshape(nd, nq, line), PLANE, 0, 0, tiled=True)]
    all_to_all x1, waiting for transfers between devices: 21.2 us -> 15.5 us  [local(): lax.all_to_all(part.reshape(nq, toks, wide), ('core', 'za'), 0, 0, tiled=...]
    all_to_all x1, waiting for transfers between devices: 6.41 us -> 10.4 us  [local(): lax.all_to_all(send.reshape(nd, nq, line), PLANE, 0, 0, tiled=True)]
    all_to_all x1, starting transfers between devices: 6.06 us -> 3.32 us  [local(): lax.all_to_all(part.reshape(nq, toks, wide), ('core', 'za'), 0, 0, tiled=...]
  transfers between devices with their start and end apart: 12 -> 11, of which waited for: 8 -> 7; matrix products, arithmetic and copies ran while one was open for 0% -> 0% of each run, Pallas kernels for 2% -> 2%
where the time goes in v10:
time: 175 us; the launch traced here: 174 us
  waiting for transfers between devices  69.1 us (39%)
  starting transfers between devices  64.9 us (37%)
  blocking collectives  27 us (15%)
  Pallas kernels  11 us (6%)
    all_to_all x1, starting transfers between devices, local(): lax.all_to_all(flat, ('core', 'za'), 0, 0, tiled=True)  23.2 us
    ppermute x1, waiting for transfers between devices, local(): other = lax.ppermute(eighth, 'zh', SWAP)  19.9 us
    all_to_all x1, blocking collectives, local(): home = lax.all_to_all(back.reshape(nd, nq, line), PLANE, 0, 0, tiled=True)  17.4 us
    all_to_all x1, waiting for transfers between devices, local(): lax.all_to_all(part.reshape(nq, toks, wide), ('core', 'za'), 0, 0, tiled=...  15.5 us
    ppermute x1, starting transfers between devices, local(): other = lax.ppermute(eighth, 'zh', SWAP)  14.4 us
    all_to_all x1, waiting for transfers between devices, local(): lax.all_to_all(flat, ('core', 'za'), 0, 0, tiled=True)  14.3 us
    all_to_all x1, waiting for transfers between devices, local(): lax.all_to_all(send.reshape(nd, nq, line), PLANE, 0, 0, tiled=True)  10.4 us
    all_to_all x1, blocking collectives, local(): u0 = lax.all_to_all(u, 'x', 0, 0, tiled=True).reshape(slots, ff)  9.64 us
  transfers between devices with their start and end apart: 11, of which 7 were waited for; matrix products, arithmetic and copies ran while one was open for 0% of the time, Pallas kernels for 2%

profile of v10, /device:TPU:1, one launch (start us, length us, event | category | flops | bytes accessed | tf_op | source)
XLA Modules:
  0.0 174.5 jit_solution(7841830406988470290)
XLA Ops:
  0.6 1.6 shard_map.128
  2.2 23.2 %all-to-all-start = ((bf16[8,16,384]{2,1,0:T(8,128)(2,1)}), bf16[8,16,384]{2,1,0:T(8,128)(2,1)S(1)}, u32[]{:S(2)}, u32[]{:S(2)}) async-start(bf16[8,16,384]{2,1,0:T(8,128)(2,1)} %shard_map.128), calls=%async_computation | async-start | bytes 196608 | tf_op jit(solution)/shard_map/all_to_all | solution.py:271
  25.5 1.9 %collective-permute-start = (bf16[768,256]{1,0:T(8,128)(2,1)}, bf16[768,256]{1,0:T(8,128)(2,1)S(1)}, u32[]{:S(2)}, u32[]{:S(2)}) collective-permute-start(bf16[768,256]{1,0:T(8,128)(2,1)} %bitcast.38), channel_id=1, source_target_pairs={{0,64},{64,0},{1,65},{65,1},{2,66},{66,2},{3,67},{67,3},{4,68},{68... | collective-permute-start | bytes 1179656 | tf_op jit(solution)/shard_map/ppermute | solution.py:270
  27.4 2.4 %collective-permute-start.1 = (bf16[256,768]{1,0:T(8,128)(2,1)}, bf16[256,768]{1,0:T(8,128)(2,1)S(1)}, u32[]{:S(2)}, u32[]{:S(2)}) collective-permute-start(bf16[256,768]{1,0:T(8,128)(2,1)} %bitcast.32), channel_id=1, source_target_pairs={{0,64},{64,0},{1,65},{65,1},{2,66},{66,2},{3,67},{67,3},{4,68},{68... | collective-permute-start | bytes 1179656 | tf_op jit(solution)/shard_map/ppermute | solution.py:270
  29.8 1.9 %collective-permute-start.2 = (bf16[256,768]{1,0:T(8,128)(2,1)}, bf16[256,768]{1,0:T(8,128)(2,1)S(1)}, u32[]{:S(2)}, u32[]{:S(2)}) collective-permute-start(bf16[256,768]{1,0:T(8,128)(2,1)} %bitcast.34), channel_id=1, source_target_pairs={{0,64},{64,0},{1,65},{65,1},{2,66},{66,2},{3,67},{67,3},{4,68},{68... | collective-permute-start | bytes 1179656 | tf_op jit(solution)/shard_map/ppermute | solution.py:270
  31.8 1.9 %collective-permute-done.2.wu_far = bf16[256,768]{1,0:T(8,128)(2,1)S(1)} collective-permute-done((bf16[256,768]{1,0:T(8,128)(2,1)}, bf16[256,768]{1,0:T(8,128)(2,1)S(1)}, u32[]{:S(2)}, u32[]{:S(2)}) %collective-permute-start.2) | collective-permute-done | bytes 393248 | tf_op jit(solution)/shard_map/ppermute | solution.py:270
  33.6 14.3 %all-to-all-done = bf16[8,16,384]{2,1,0:T(8,128)(2,1)S(1)} async-done(((bf16[8,16,384]{2,1,0:T(8,128)(2,1)}), bf16[8,16,384]{2,1,0:T(8,128)(2,1)S(1)}, u32[]{:S(2)}, u32[]{:S(2)}) %all-to-all-start) | async-done | bytes 98336 | tf_op jit(solution)/shard_map/all_to_all | solution.py:271
  47.9 1.3 shard_map.129
  49.2 4.4 %all-to-all-start.1 = ((bf16[16,8,1152]{2,1,0:T(8,128)(2,1)}), bf16[16,8,1152]{2,1,0:T(8,128)(2,1)S(1)}, u32[]{:S(2)}, u32[]{:S(2)}) async-start(bf16[16,8,1152]{2,1,0:T(8,128)(2,1)} %bitcast.9), calls=%async_computation.1 | async-start | bytes 589824 | tf_op jit(solution)/shard_map/all_to_all | solution.py:276
  53.6 10.4 %all-to-all-done.1 = bf16[16,8,1152]{2,1,0:T(8,128)(2,1)S(1)} async-done(((bf16[16,8,1152]{2,1,0:T(8,128)(2,1)}), bf16[16,8,1152]{2,1,0:T(8,128)(2,1)S(1)}, u32[]{:S(2)}, u32[]{:S(2)}) %all-to-all-start.1) | async-done | bytes 294944 | tf_op jit(solution)/shard_map/all_to_all | solution.py:276
  64.0 1.6 shard_map.130
  65.6 0.7 copy-done.8
  66.2 4.2 %all-to-all-start.2 = ((bf16[4,64,768]{2,1,0:T(8,128)(2,1)}), bf16[4,64,768]{2,1,0:T(8,128)(2,1)S(1)}, u32[]{:S(2)}, u32[]{:S(2)}) async-start(bf16[4,64,768]{2,1,0:T(8,128)(2,1)} %bitcast.12), calls=%async_computation.2 | async-start | bytes 786432 | tf_op jit(solution)/shard_map/all_to_all | solution.py:292
  70.4 6.2 %all-to-all-done.2.others = bf16[4,64,768]{2,1,0:T(8,128)(2,1)S(1)} async-done(((bf16[4,64,768]{2,1,0:T(8,128)(2,1)}), bf16[4,64,768]{2,1,0:T(8,128)(2,1)S(1)}, u32[]{:S(2)}, u32[]{:S(2)}) %all-to-all-start.2) | async-done | bytes 393248 | tf_op jit(solution)/shard_map/all_to_all | solution.py:292
  76.6 0.1 shard_map.131.first
  76.7 14.4 %collective-permute-start.3 = (bf16[64,768]{1,0:T(8,128)(2,1)S(1)}, bf16[64,768]{1,0:T(8,128)(2,1)S(1)}, u32[]{:S(2)}, u32[]{:S(2)}) collective-permute-start(bf16[64,768]{1,0:T(8,128)(2,1)S(1)} %shard_map.131.first), channel_id=1, source_target_pairs={{0,512},{512,0},{1,513},{513,1},{2,514},{514,2},{3,515},{515,3},{4... | collective-permute-start | bytes 294920 | tf_op jit(solution)/shard_map/ppermute | solution.py:298
  91.2 0.4 shard_map.132
  91.6 19.9 %collective-permute-done.3.second = bf16[64,768]{1,0:T(8,128)(2,1)S(1)} collective-permute-done((bf16[64,768]{1,0:T(8,128)(2,1)S(1)}, bf16[64,768]{1,0:T(8,128)(2,1)S(1)}, u32[]{:S(2)}, u32[]{:S(2)}) %collective-permute-start.3) | collective-permute-done | bytes 98336 | tf_op jit(solution)/shard_map/ppermute | solution.py:298
  111.6 9.6 %all_to_all.30 = bf16[4,64,768]{2,1,0:T(8,128)(2,1)S(1)} all-to-all(bf16[4,64,768]{2,1,0:T(8,128)(2,1)S(1)} %shard_map.133), channel_id=1, replica_groups=mesh['zh'=2,'x'=4,'core'=2,'za'=4,'zb'=4,'y'=4] {'x'}, dimensions={0} | all-to-all | bytes 786432 | tf_op jit(solution)/shard_map/all_to_all | solution.py:309
  121.2 1.0 shard_map.134
  122.2 17.4 %all_to_all.31 = bf16[16,8,1152]{2,1,0:T(8,128)(2,1)S(1)} all-to-all(bf16[16,8,1152]{2,1,0:T(8,128)(2,1)S(1)} %bitcast.40), channel_id=1, replica_groups=mesh['zh'=2,'x'=4,'core'=2,'za'=4,'zb'=4,'y'=4] {'zb','y'}, dimensions={0} | all-to-all | bytes 589824 | tf_op jit(solution)/shard_map/all_to_all | solution.py:317
  139.6 1.2 shard_map.135
  140.8 4.7 %collective-permute-start.4 = (bf16[2,256,768]{2,1,0:T(8,128)(2,1)S(1)}, bf16[2,256,768]{2,1,0:T(8,128)(2,1)S(1)}, u32[]{:S(2)}, u32[]{:S(2)}) collective-permute-start(bf16[2,256,768]{2,1,0:T(8,128)(2,1)S(1)} %get-tuple-element.61.grads0), channel_id=1, source_target_pairs={{0,64},{64,0},{1,65},{65,1},{2,66},{66,2},{3,67},{67,3},{4,68},{68... | collective-permute-start | bytes 2359304 | tf_op jit(solution)/shard_map/ppermute | solution.py:328
  145.6 3.3 %all-to-all-start.5 = ((bf16[8,16,384]{2,1,0:T(8,128)(2,1)}), bf16[8,16,384]{2,1,0:T(8,128)(2,1)S(1)}, u32[]{:S(2)}, u32[]{:S(2)}) async-start(bf16[8,16,384]{2,1,0:T(8,128)(2,1)} %bitcast.18), calls=%async_computation.5 | async-start | bytes 196608 | tf_op jit(solution)/shard_map/all_to_all | solution.py:334
  148.9 2.0 %collective-permute-start.6 = (bf16[256,256]{1,0:T(8,128)(2,1)}, bf16[256,256]{1,0:T(8,128)(2,1)S(1)}, u32[]{:S(2)}, u32[]{:S(2)}) collective-permute-start(bf16[256,256]{1,0:T(8,128)(2,1)} %copy-done.8), channel_id=1, source_target_pairs={{0,64},{64,0},{1,65},{65,1},{2,66},{66,2},{3,67},{67,3},{4,68},{68... | collective-permute-start | bytes 393224 | tf_op jit(solution)/shard_map/ppermute | solution.py:329
  150.9 2.4 %collective-permute-start.5 = (f32[256,1]{1,0:T(8,128)S(1)}, f32[256,1]{1,0:T(8,128)S(1)}, u32[]{:S(2)}, u32[]{:S(2)}) collective-permute-start(f32[256,1]{1,0:T(8,128)S(1)} %get-tuple-element.64.probs.probs0), channel_id=1, source_target_pairs={{0,64},{64,0},{1,65},{65,1},{2,66},{66,2},{3,67},{67,3},{4,68},{68... | collective-permute-start | bytes 3080 | tf_op jit(solution)/shard_map/ppermute | solution.py:330
  153.2 1.0 collective-permute-done.5.probs1
  154.2 1.7 shard_map.138
  155.9 15.5 %all-to-all-done.5.parts = bf16[8,16,384]{2,1,0:T(8,128)(2,1)S(1)} async-done(((bf16[8,16,384]{2,1,0:T(8,128)(2,1)}), bf16[8,16,384]{2,1,0:T(8,128)(2,1)S(1)}, u32[]{:S(2)}, u32[]{:S(2)}) %all-to-all-start.5) | async-done | bytes 98336 | tf_op jit(solution)/shard_map/all_to_all | solution.py:334
  171.4 0.7 shard_map.136
  172.2 0.9 copy-done.7
  173.1 1.4 shard_map.137
  (21 shorter events, 0.1 us)
Async XLA Ops:
  2.2 45.7 %all-to-all-start = ((bf16[8,16,384]{2,1,0:T(8,128)(2,1)}), bf16[8,16,384]{2,1,0:T(8,128)(2,1)S(1)}, u32[]{:S(2)}, u32[]{:S(2)}) async-start(bf16[8,16,384]{2,1,0:T(8,128)(2,1)} %shard_map.128), calls=%async_computation | async-start | bytes 196608 | tf_op jit(solution)/shard_map/all_to_all | solution.py:271
  25.5 6.3 %collective-permute-start = (bf16[768,256]{1,0:T(8,128)(2,1)}, bf16[768,256]{1,0:T(8,128)(2,1)S(1)}, u32[]{:S(2)}, u32[]{:S(2)}) collective-permute-start(bf16[768,256]{1,0:T(8,128)(2,1)} %bitcast.38), channel_id=1, source_target_pairs={{0,64},{64,0},{1,65},{65,1},{2,66},{66,2},{3,67},{67,3},{4,68},{68... | collective-permute-start | bytes 1179656 | tf_op jit(solution)/shard_map/ppermute | solution.py:270
  27.4 4.4 %collective-permute-start.1 = (bf16[256,768]{1,0:T(8,128)(2,1)}, bf16[256,768]{1,0:T(8,128)(2,1)S(1)}, u32[]{:S(2)}, u32[]{:S(2)}) collective-permute-start(bf16[256,768]{1,0:T(8,128)(2,1)} %bitcast.32), channel_id=1, source_target_pairs={{0,64},{64,0},{1,65},{65,1},{2,66},{66,2},{3,67},{67,3},{4,68},{68... | collective-permute-start | bytes 1179656 | tf_op jit(solution)/shard_map/ppermute | solution.py:270
  29.8 3.8 %collective-permute-start.2 = (bf16[256,768]{1,0:T(8,128)(2,1)}, bf16[256,768]{1,0:T(8,128)(2,1)S(1)}, u32[]{:S(2)}, u32[]{:S(2)}) collective-permute-start(bf16[256,768]{1,0:T(8,128)(2,1)} %bitcast.34), channel_id=1, source_target_pairs={{0,64},{64,0},{1,65},{65,1},{2,66},{66,2},{3,67},{67,3},{4,68},{68... | collective-permute-start | bytes 1179656 | tf_op jit(solution)/shard_map/ppermute | solution.py:270
  33.6 15.6 %copy-start.4 = (bf16[256,768]{1,0:T(8,128)(2,1)}, bf16[256,768]{1,0:T(8,128)(2,1)S(1)}, u32[]{:S(2)}) copy-start(bf16[256,768]{1,0:T(8,128)(2,1)S(1)} %collective-permute-done.2.wu_far) | copy-start | bytes 1179652
  49.2 14.8 %copy-start.6 = (bf16[1,768,256]{2,1,0:T(8,128)(2,1)S(1)}, bf16[1,768,256]{2,1,0:T(8,128)(2,1)}, u32[]{:S(2)}) copy-start(bf16[1,768,256]{2,1,0:T(8,128)(2,1)} %param.17) | copy-start | bytes 1179652
  49.2 14.8 %all-to-all-start.1 = ((bf16[16,8,1152]{2,1,0:T(8,128)(2,1)}), bf16[16,8,1152]{2,1,0:T(8,128)(2,1)S(1)}, u32[]{:S(2)}, u32[]{:S(2)}) async-start(bf16[16,8,1152]{2,1,0:T(8,128)(2,1)} %bitcast.9), calls=%async_computation.1 | async-start | bytes 589824 | tf_op jit(solution)/shard_map/all_to_all | solution.py:276
  65.6 0.7 copy-start.8
  66.2 24.9 %copy-start.1 = (bf16[2,1,256,768]{3,2,1,0:T(8,128)(2,1)S(1)}, bf16[2,1,256,768]{3,2,1,0:T(8,128)(2,1)}, u32[]{:S(2)}) copy-start(bf16[2,1,256,768]{3,2,1,0:T(8,128)(2,1)} %param.14) | copy-start | bytes 2359300
  66.2 10.4 %all-to-all-start.2 = ((bf16[4,64,768]{2,1,0:T(8,128)(2,1)}), bf16[4,64,768]{2,1,0:T(8,128)(2,1)S(1)}, u32[]{:S(2)}, u32[]{:S(2)}) async-start(bf16[4,64,768]{2,1,0:T(8,128)(2,1)} %bitcast.12), calls=%async_computation.2 | async-start | bytes 786432 | tf_op jit(solution)/shard_map/all_to_all | solution.py:292
  70.4 20.8 %copy-start = (bf16[2,1,256,768]{3,2,1,0:T(8,128)(2,1)S(1)}, bf16[2,1,256,768]{3,2,1,0:T(8,128)(2,1)}, u32[]{:S(2)}) copy-start(bf16[2,1,256,768]{3,2,1,0:T(8,128)(2,1)} %param.13) | copy-start | bytes 2359300
  76.7 34.8 %collective-permute-start.3 = (bf16[64,768]{1,0:T(8,128)(2,1)S(1)}, bf16[64,768]{1,0:T(8,128)(2,1)S(1)}, u32[]{:S(2)}, u32[]{:S(2)}) collective-permute-start(bf16[64,768]{1,0:T(8,128)(2,1)S(1)} %shard_map.131.first), channel_id=1, source_target_pairs={{0,512},{512,0},{1,513},{513,1},{2,514},{514,2},{3,515},{515,3},{4... | collective-permute-start | bytes 294920 | tf_op jit(solution)/shard_map/ppermute | solution.py:298
  111.5 9.7 %copy-start.5 = (bf16[256,768]{1,0:T(8,128)(2,1)S(1)}, bf16[256,768]{1,0:T(8,128)(2,1)}, u32[]{:S(2)}) copy-start(bf16[256,768]{1,0:T(8,128)(2,1)} %copy-done.4) | copy-start | bytes 1179652
  111.6 9.7 %copy-start.2 = (bf16[1,256,768]{2,1,0:T(8,128)(2,1)S(1)}, bf16[1,256,768]{2,1,0:T(8,128)(2,1)}, u32[]{:S(2)}) copy-start(bf16[1,256,768]{2,1,0:T(8,128)(2,1)} %param.15) | copy-start | bytes 1179652
  111.6 9.7 %copy-start.3 = (bf16[1,256,768]{2,1,0:T(8,128)(2,1)S(1)}, bf16[1,256,768]{2,1,0:T(8,128)(2,1)}, u32[]{:S(2)}) copy-start(bf16[1,256,768]{2,1,0:T(8,128)(2,1)} %param.16) | copy-start | bytes 1179652
  140.8 31.3 %collective-permute-start.4 = (bf16[2,256,768]{2,1,0:T(8,128)(2,1)S(1)}, bf16[2,256,768]{2,1,0:T(8,128)(2,1)S(1)}, u32[]{:S(2)}, u32[]{:S(2)}) collective-permute-start(bf16[2,256,768]{2,1,0:T(8,128)(2,1)S(1)} %get-tuple-element.61.grads0), channel_id=1, source_target_pairs={{0,64},{64,0},{1,65},{65,1},{2,66},{66,2},{3,67},{67,3},{4,68},{68... | collective-permute-start | bytes 2359304 | tf_op jit(solution)/shard_map/ppermute | solution.py:328
  145.6 25.9 %all-to-all-start.5 = ((bf16[8,16,384]{2,1,0:T(8,128)(2,1)}), bf16[8,16,384]{2,1,0:T(8,128)(2,1)S(1)}, u32[]{:S(2)}, u32[]{:S(2)}) async-start(bf16[8,16,384]{2,1,0:T(8,128)(2,1)} %bitcast.18), calls=%async_computation.5 | async-start | bytes 196608 | tf_op jit(solution)/shard_map/all_to_all | solution.py:334
  148.9 5.3 %collective-permute-start.6 = (bf16[256,256]{1,0:T(8,128)(2,1)}, bf16[256,256]{1,0:T(8,128)(2,1)S(1)}, u32[]{:S(2)}, u32[]{:S(2)}) collective-permute-start(bf16[256,256]{1,0:T(8,128)(2,1)} %copy-done.8), channel_id=1, source_target_pairs={{0,64},{64,0},{1,65},{65,1},{2,66},{66,2},{3,67},{67,3},{4,68},{68... | collective-permute-start | bytes 393224 | tf_op jit(solution)/shard_map/ppermute | solution.py:329
  150.9 3.3 %collective-permute-start.5 = (f32[256,1]{1,0:T(8,128)S(1)}, f32[256,1]{1,0:T(8,128)S(1)}, u32[]{:S(2)}, u32[]{:S(2)}) collective-permute-start(f32[256,1]{1,0:T(8,128)S(1)} %get-tuple-element.64.probs.probs0), channel_id=1, source_target_pairs={{0,64},{64,0},{1,65},{65,1},{2,66},{66,2},{3,67},{67,3},{4,68},{68... | collective-permute-start | bytes 3080 | tf_op jit(solution)/shard_map/ppermute | solution.py:330
  172.1 1.0 copy-start.7

commit v11 on v10

--- a/solution.py
+++ b/solution.py
@@ -322,12 +322,11 @@
         product // 4,
         nd * nq * line * 2,
     )(first, lines, home.reshape(nd * nq, line))[0]
-    part, grads_now, rows_far, probs_now = lax.optimization_barrier(
-        (part, grads0, rows_far, probs0)
-    )
-    grads1 = lax.ppermute(grads_now, "core", SWAP)
+    part, rows_far, probs_now = lax.optimization_barrier((part, rows_far, probs0))
     rows1 = lax.ppermute(rows_far, "core", SWAP)
     probs1 = lax.ppermute(probs_now, "core", SWAP)
+    grads_now, rows1 = lax.optimization_barrier((grads0, rows1))
+    grads1 = lax.ppermute(grads_now, "core", SWAP)
     grad_down = call(
         down_grad_kernel, [sds((ff, width), BF)], 6, 2 * product, slots * ff * 12
     )(me, gate_pre[:, 0], up_pre[:, 0], probs0, probs1, rows0, rows1)[0]
@@ -335,6 +334,9 @@
     grad_gate, grad_up = call(
         weight_kernel, [sds((width, ff), BF)] * 2, 3, 4 * product, slots * ff * 12
     )(me, saved_inputs[:, 0], grads0, grads1)
+    part, grad_gate, grad_up, grad_down = lax.optimization_barrier(
+        (part, grad_gate, grad_up, grad_down)
+    )
     in_grad, prob_grad = call(
         total_kernel,
         [sds((mb, toks, width), BF), sds((mb, top, toks), BF)],

time: 175 us -> 177 us (1.011)
    ppermute x1, starting transfers between devices: 1.97 us -> 4.74 us  [local(): rows1 = lax.ppermute(rows_far, 'core', SWAP)]
    ppermute x1, starting transfers between devices: 4.74 us -> 2.26 us  [local(): grads1 = lax.ppermute(grads_now, 'core', SWAP)]
  transfers between devices with their start and end apart: 11 -> 11, of which waited for: 7 -> 8; matrix products, arithmetic and copies ran while one was open for 0% -> 0% of each run, Pallas kernels for 2% -> 2%
where the time goes in v11:
time: 177 us; the launch traced here: 176 us
  waiting for transfers between devices  70.2 us (40%)
  starting transfers between devices  64.9 us (37%)
  blocking collectives  27 us (15%)
  Pallas kernels  11 us (6%)
  local copies, waits for them, and re-layouts  2.25 us (1%)
    all_to_all x1, starting transfers between devices, local(): lax.all_to_all(flat, ('core', 'za'), 0, 0, tiled=True)  23.2 us
    ppermute x1, waiting for transfers between devices, local(): other = lax.ppermute(eighth, 'zh', SWAP)  19.9 us
    all_to_all x1, blocking collectives, local(): home = lax.all_to_all(back.reshape(nd, nq, line), PLANE, 0, 0, tiled=True)  17.4 us
    all_to_all x1, waiting for transfers between devices, local(): lax.all_to_all(part.reshape(nq, toks, wide), ('core', 'za'), 0, 0, tiled=...  15.4 us
    ppermute x1, starting transfers between devices, local(): other = lax.ppermute(eighth, 'zh', SWAP)  14.4 us
    all_to_all x1, waiting for transfers between devices, local(): lax.all_to_all(flat, ('core', 'za'), 0, 0, tiled=True)  14.3 us
    all_to_all x1, waiting for transfers between devices, local(): lax.all_to_all(send.reshape(nd, nq, line), PLANE, 0, 0, tiled=True)  10.4 us
    all_to_all x1, blocking collectives, local(): u0 = lax.all_to_all(u, 'x', 0, 0, tiled=True).reshape(slots, ff)  9.64 us
  transfers between devices with their start and end apart: 11, of which 8 were waited for; matrix products, arithmetic and copies ran while one was open for 0% of the time, Pallas kernels for 2%

profile of v11, /device:TPU:1, one launch (start us, length us, event | category | flops | bytes accessed | tf_op | source)
XLA Modules:
  0.0 176.2 jit_solution(2060704689693726168)
XLA Ops:
  0.6 1.6 shard_map.128
  2.2 23.2 %all-to-all-start = ((bf16[8,16,384]{2,1,0:T(8,128)(2,1)}), bf16[8,16,384]{2,1,0:T(8,128)(2,1)S(1)}, u32[]{:S(2)}, u32[]{:S(2)}) async-start(bf16[8,16,384]{2,1,0:T(8,128)(2,1)} %shard_map.128), calls=%async_computation | async-start | bytes 196608 | tf_op jit(solution)/shard_map/all_to_all | solution.py:271
  25.5 1.9 %collective-permute-start = (bf16[768,256]{1,0:T(8,128)(2,1)}, bf16[768,256]{1,0:T(8,128)(2,1)S(1)}, u32[]{:S(2)}, u32[]{:S(2)}) collective-permute-start(bf16[768,256]{1,0:T(8,128)(2,1)} %bitcast.38), channel_id=1, source_target_pairs={{0,64},{64,0},{1,65},{65,1},{2,66},{66,2},{3,67},{67,3},{4,68},{68... | collective-permute-start | bytes 1179656 | tf_op jit(solution)/shard_map/ppermute | solution.py:270
  27.4 2.4 %collective-permute-start.1 = (bf16[256,768]{1,0:T(8,128)(2,1)}, bf16[256,768]{1,0:T(8,128)(2,1)S(1)}, u32[]{:S(2)}, u32[]{:S(2)}) collective-permute-start(bf16[256,768]{1,0:T(8,128)(2,1)} %bitcast.32), channel_id=1, source_target_pairs={{0,64},{64,0},{1,65},{65,1},{2,66},{66,2},{3,67},{67,3},{4,68},{68... | collective-permute-start | bytes 1179656 | tf_op jit(solution)/shard_map/ppermute | solution.py:270
  29.8 1.9 %collective-permute-start.2 = (bf16[256,768]{1,0:T(8,128)(2,1)}, bf16[256,768]{1,0:T(8,128)(2,1)S(1)}, u32[]{:S(2)}, u32[]{:S(2)}) collective-permute-start(bf16[256,768]{1,0:T(8,128)(2,1)} %bitcast.34), channel_id=1, source_target_pairs={{0,64},{64,0},{1,65},{65,1},{2,66},{66,2},{3,67},{67,3},{4,68},{68... | collective-permute-start | bytes 1179656 | tf_op jit(solution)/shard_map/ppermute | solution.py:270
  31.8 1.9 %collective-permute-done.2.wu_far = bf16[256,768]{1,0:T(8,128)(2,1)S(1)} collective-permute-done((bf16[256,768]{1,0:T(8,128)(2,1)}, bf16[256,768]{1,0:T(8,128)(2,1)S(1)}, u32[]{:S(2)}, u32[]{:S(2)}) %collective-permute-start.2) | collective-permute-done | bytes 393248 | tf_op jit(solution)/shard_map/ppermute | solution.py:270
  33.6 14.3 %all-to-all-done = bf16[8,16,384]{2,1,0:T(8,128)(2,1)S(1)} async-done(((bf16[8,16,384]{2,1,0:T(8,128)(2,1)}), bf16[8,16,384]{2,1,0:T(8,128)(2,1)S(1)}, u32[]{:S(2)}, u32[]{:S(2)}) %all-to-all-start) | async-done | bytes 98336 | tf_op jit(solution)/shard_map/all_to_all | solution.py:271
  47.9 1.3 shard_map.129
  49.2 4.4 %all-to-all-start.1 = ((bf16[16,8,1152]{2,1,0:T(8,128)(2,1)}), bf16[16,8,1152]{2,1,0:T(8,128)(2,1)S(1)}, u32[]{:S(2)}, u32[]{:S(2)}) async-start(bf16[16,8,1152]{2,1,0:T(8,128)(2,1)} %bitcast.9), calls=%async_computation.1 | async-start | bytes 589824 | tf_op jit(solution)/shard_map/all_to_all | solution.py:276
  53.6 10.4 %all-to-all-done.1 = bf16[16,8,1152]{2,1,0:T(8,128)(2,1)S(1)} async-done(((bf16[16,8,1152]{2,1,0:T(8,128)(2,1)}), bf16[16,8,1152]{2,1,0:T(8,128)(2,1)S(1)}, u32[]{:S(2)}, u32[]{:S(2)}) %all-to-all-start.1) | async-done | bytes 294944 | tf_op jit(solution)/shard_map/all_to_all | solution.py:276
  64.0 1.6 shard_map.130
  65.6 0.7 copy-done.10
  66.2 4.2 %all-to-all-start.2 = ((bf16[4,64,768]{2,1,0:T(8,128)(2,1)}), bf16[4,64,768]{2,1,0:T(8,128)(2,1)S(1)}, u32[]{:S(2)}, u32[]{:S(2)}) async-start(bf16[4,64,768]{2,1,0:T(8,128)(2,1)} %bitcast.12), calls=%async_computation.2 | async-start | bytes 786432 | tf_op jit(solution)/shard_map/all_to_all | solution.py:292
  70.4 6.2 %all-to-all-done.2.others = bf16[4,64,768]{2,1,0:T(8,128)(2,1)S(1)} async-done(((bf16[4,64,768]{2,1,0:T(8,128)(2,1)}), bf16[4,64,768]{2,1,0:T(8,128)(2,1)S(1)}, u32[]{:S(2)}, u32[]{:S(2)}) %all-to-all-start.2) | async-done | bytes 393248 | tf_op jit(solution)/shard_map/all_to_all | solution.py:292
  76.7 14.4 %collective-permute-start.3 = (bf16[64,768]{1,0:T(8,128)(2,1)S(1)}, bf16[64,768]{1,0:T(8,128)(2,1)S(1)}, u32[]{:S(2)}, u32[]{:S(2)}) collective-permute-start(bf16[64,768]{1,0:T(8,128)(2,1)S(1)} %shard_map.131.first), channel_id=1, source_target_pairs={{0,512},{512,0},{1,513},{513,1},{2,514},{514,2},{3,515},{515,3},{4... | collective-permute-start | bytes 294920 | tf_op jit(solution)/shard_map/ppermute | solution.py:298
  91.6 19.9 %collective-permute-done.3.second = bf16[64,768]{1,0:T(8,128)(2,1)S(1)} collective-permute-done((bf16[64,768]{1,0:T(8,128)(2,1)S(1)}, bf16[64,768]{1,0:T(8,128)(2,1)S(1)}, u32[]{:S(2)}, u32[]{:S(2)}) %collective-permute-start.3) | collective-permute-done | bytes 98336 | tf_op jit(solution)/shard_map/ppermute | solution.py:298
  111.6 9.6 %all_to_all.30 = bf16[4,64,768]{2,1,0:T(8,128)(2,1)S(1)} all-to-all(bf16[4,64,768]{2,1,0:T(8,128)(2,1)S(1)} %shard_map.133), channel_id=1, replica_groups=mesh['zh'=2,'x'=4,'core'=2,'za'=4,'zb'=4,'y'=4] {'x'}, dimensions={0} | all-to-all | bytes 786432 | tf_op jit(solution)/shard_map/all_to_all | solution.py:309
  121.2 1.0 shard_map.134
  122.2 17.4 %all_to_all.31 = bf16[16,8,1152]{2,1,0:T(8,128)(2,1)S(1)} all-to-all(bf16[16,8,1152]{2,1,0:T(8,128)(2,1)S(1)} %bitcast.40), channel_id=1, replica_groups=mesh['zh'=2,'x'=4,'core'=2,'za'=4,'zb'=4,'y'=4] {'zb','y'}, dimensions={0} | all-to-all | bytes 589824 | tf_op jit(solution)/shard_map/all_to_all | solution.py:317
  139.6 1.2 shard_map.135
  140.8 4.7 %collective-permute-start.4 = (bf16[256,256]{1,0:T(8,128)(2,1)S(1)}, bf16[256,256]{1,0:T(8,128)(2,1)S(1)}, u32[]{:S(2)}, u32[]{:S(2)}) collective-permute-start(bf16[256,256]{1,0:T(8,128)(2,1)S(1)} %copy-done.11), channel_id=1, source_target_pairs={{0,64},{64,0},{1,65},{65,1},{2,66},{66,2},{3,67},{67,3},{4,68},{68... | collective-permute-start | bytes 393224 | tf_op jit(solution)/shard_map/ppermute | solution.py:326
  145.6 1.0 collective-permute-done.4.rows1
  146.5 0.7 copy-done.8
  147.2 2.3 %collective-permute-start.5 = (bf16[2,256,768]{2,1,0:T(8,128)(2,1)S(1)}, bf16[2,256,768]{2,1,0:T(8,128)(2,1)S(1)}, u32[]{:S(2)}, u32[]{:S(2)}) collective-permute-start(bf16[2,256,768]{2,1,0:T(8,128)(2,1)S(1)} %get-tuple-element.65.grads0), channel_id=1, source_target_pairs={{0,64},{64,0},{1,65},{65,1},{2,66},{66,2},{3,67},{67,3},{4,68},{68... | collective-permute-start | bytes 2359304 | tf_op jit(solution)/shard_map/ppermute | solution.py:329
  149.5 3.4 %all-to-all-start.5 = ((bf16[8,16,384]{2,1,0:T(8,128)(2,1)}), bf16[8,16,384]{2,1,0:T(8,128)(2,1)S(1)}, u32[]{:S(2)}, u32[]{:S(2)}) async-start(bf16[8,16,384]{2,1,0:T(8,128)(2,1)} %bitcast.18), calls=%async_computation.5 | async-start | bytes 196608 | tf_op jit(solution)/shard_map/all_to_all | solution.py:333
  152.9 2.0 %collective-permute-start.6 = (f32[256,1]{1,0:T(8,128)S(1)}, f32[256,1]{1,0:T(8,128)S(1)}, u32[]{:S(2)}, u32[]{:S(2)}) collective-permute-start(f32[256,1]{1,0:T(8,128)S(1)} %get-tuple-element.68.probs.probs0), channel_id=1, source_target_pairs={{0,64},{64,0},{1,65},{65,1},{2,66},{66,2},{3,67},{67,3},{4,68},{68... | collective-permute-start | bytes 3080 | tf_op jit(solution)/shard_map/ppermute | solution.py:327
  154.9 1.2 collective-permute-done.6.probs1
  156.1 0.9 copy-done.9
  157.0 1.7 shard_map.137
  158.7 1.4 shard_map.136
  160.1 15.4 %all-to-all-done.5.parts = bf16[8,16,384]{2,1,0:T(8,128)(2,1)S(1)} async-done(((bf16[8,16,384]{2,1,0:T(8,128)(2,1)}), bf16[8,16,384]{2,1,0:T(8,128)(2,1)S(1)}, u32[]{:S(2)}, u32[]{:S(2)}) %all-to-all-start.5) | async-done | bytes 98336 | tf_op jit(solution)/shard_map/all_to_all | solution.py:333
  175.4 0.7 shard_map.138
  (27 shorter events, 0.6 us)
Async XLA Ops:
  2.2 45.7 %all-to-all-start = ((bf16[8,16,384]{2,1,0:T(8,128)(2,1)}), bf16[8,16,384]{2,1,0:T(8,128)(2,1)S(1)}, u32[]{:S(2)}, u32[]{:S(2)}) async-start(bf16[8,16,384]{2,1,0:T(8,128)(2,1)} %shard_map.128), calls=%async_computation | async-start | bytes 196608 | tf_op jit(solution)/shard_map/all_to_all | solution.py:271
  25.5 6.3 %collective-permute-start = (bf16[768,256]{1,0:T(8,128)(2,1)}, bf16[768,256]{1,0:T(8,128)(2,1)S(1)}, u32[]{:S(2)}, u32[]{:S(2)}) collective-permute-start(bf16[768,256]{1,0:T(8,128)(2,1)} %bitcast.38), channel_id=1, source_target_pairs={{0,64},{64,0},{1,65},{65,1},{2,66},{66,2},{3,67},{67,3},{4,68},{68... | collective-permute-start | bytes 1179656 | tf_op jit(solution)/shard_map/ppermute | solution.py:270
  27.4 4.4 %collective-permute-start.1 = (bf16[256,768]{1,0:T(8,128)(2,1)}, bf16[256,768]{1,0:T(8,128)(2,1)S(1)}, u32[]{:S(2)}, u32[]{:S(2)}) collective-permute-start(bf16[256,768]{1,0:T(8,128)(2,1)} %bitcast.32), channel_id=1, source_target_pairs={{0,64},{64,0},{1,65},{65,1},{2,66},{66,2},{3,67},{67,3},{4,68},{68... | collective-permute-start | bytes 1179656 | tf_op jit(solution)/shard_map/ppermute | solution.py:270
  29.8 3.8 %collective-permute-start.2 = (bf16[256,768]{1,0:T(8,128)(2,1)}, bf16[256,768]{1,0:T(8,128)(2,1)S(1)}, u32[]{:S(2)}, u32[]{:S(2)}) collective-permute-start(bf16[256,768]{1,0:T(8,128)(2,1)} %bitcast.34), channel_id=1, source_target_pairs={{0,64},{64,0},{1,65},{65,1},{2,66},{66,2},{3,67},{67,3},{4,68},{68... | collective-permute-start | bytes 1179656 | tf_op jit(solution)/shard_map/ppermute | solution.py:270
  33.6 15.6 %copy-start.4 = (bf16[256,768]{1,0:T(8,128)(2,1)}, bf16[256,768]{1,0:T(8,128)(2,1)S(1)}, u32[]{:S(2)}) copy-start(bf16[256,768]{1,0:T(8,128)(2,1)S(1)} %collective-permute-done.2.wu_far) | copy-start | bytes 1179652
  49.2 14.8 %copy-start.6 = (bf16[1,768,256]{2,1,0:T(8,128)(2,1)S(1)}, bf16[1,768,256]{2,1,0:T(8,128)(2,1)}, u32[]{:S(2)}) copy-start(bf16[1,768,256]{2,1,0:T(8,128)(2,1)} %param.17) | copy-start | bytes 1179652
  49.2 14.8 %all-to-all-start.1 = ((bf16[16,8,1152]{2,1,0:T(8,128)(2,1)}), bf16[16,8,1152]{2,1,0:T(8,128)(2,1)S(1)}, u32[]{:S(2)}, u32[]{:S(2)}) async-start(bf16[16,8,1152]{2,1,0:T(8,128)(2,1)} %bitcast.9), calls=%async_computation.1 | async-start | bytes 589824 | tf_op jit(solution)/shard_map/all_to_all | solution.py:276
  65.6 0.7 copy-start.10
  66.2 24.9 %copy-start.1 = (bf16[2,1,256,768]{3,2,1,0:T(8,128)(2,1)S(1)}, bf16[2,1,256,768]{3,2,1,0:T(8,128)(2,1)}, u32[]{:S(2)}) copy-start(bf16[2,1,256,768]{3,2,1,0:T(8,128)(2,1)} %param.14) | copy-start | bytes 2359300
  66.2 10.4 %all-to-all-start.2 = ((bf16[4,64,768]{2,1,0:T(8,128)(2,1)}), bf16[4,64,768]{2,1,0:T(8,128)(2,1)S(1)}, u32[]{:S(2)}, u32[]{:S(2)}) async-start(bf16[4,64,768]{2,1,0:T(8,128)(2,1)} %bitcast.12), calls=%async_computation.2 | async-start | bytes 786432 | tf_op jit(solution)/shard_map/all_to_all | solution.py:292
  70.4 20.8 %copy-start = (bf16[2,1,256,768]{3,2,1,0:T(8,128)(2,1)S(1)}, bf16[2,1,256,768]{3,2,1,0:T(8,128)(2,1)}, u32[]{:S(2)}) copy-start(bf16[2,1,256,768]{3,2,1,0:T(8,128)(2,1)} %param.13) | copy-start | bytes 2359300
  76.7 34.8 %collective-permute-start.3 = (bf16[64,768]{1,0:T(8,128)(2,1)S(1)}, bf16[64,768]{1,0:T(8,128)(2,1)S(1)}, u32[]{:S(2)}, u32[]{:S(2)}) collective-permute-start(bf16[64,768]{1,0:T(8,128)(2,1)S(1)} %shard_map.131.first), channel_id=1, source_target_pairs={{0,512},{512,0},{1,513},{513,1},{2,514},{514,2},{3,515},{515,3},{4... | collective-permute-start | bytes 294920 | tf_op jit(solution)/shard_map/ppermute | solution.py:298
  111.5 9.7 %copy-start.5 = (bf16[256,768]{1,0:T(8,128)(2,1)S(1)}, bf16[256,768]{1,0:T(8,128)(2,1)}, u32[]{:S(2)}) copy-start(bf16[256,768]{1,0:T(8,128)(2,1)} %copy-done.4) | copy-start | bytes 1179652
  111.6 9.7 %copy-start.2 = (bf16[1,256,768]{2,1,0:T(8,128)(2,1)S(1)}, bf16[1,256,768]{2,1,0:T(8,128)(2,1)}, u32[]{:S(2)}) copy-start(bf16[1,256,768]{2,1,0:T(8,128)(2,1)} %param.15) | copy-start | bytes 1179652
  111.6 9.7 %copy-start.3 = (bf16[1,256,768]{2,1,0:T(8,128)(2,1)S(1)}, bf16[1,256,768]{2,1,0:T(8,128)(2,1)}, u32[]{:S(2)}) copy-start(bf16[1,256,768]{2,1,0:T(8,128)(2,1)} %param.16) | copy-start | bytes 1179652
  139.6 1.2 copy-start.11
  140.8 5.7 %collective-permute-start.4 = (bf16[256,256]{1,0:T(8,128)(2,1)S(1)}, bf16[256,256]{1,0:T(8,128)(2,1)S(1)}, u32[]{:S(2)}, u32[]{:S(2)}) collective-permute-start(bf16[256,256]{1,0:T(8,128)(2,1)S(1)} %copy-done.11), channel_id=1, source_target_pairs={{0,64},{64,0},{1,65},{65,1},{2,66},{66,2},{3,67},{67,3},{4,68},{68... | collective-permute-start | bytes 393224 | tf_op jit(solution)/shard_map/ppermute | solution.py:326
  146.5 0.7 copy-start.8
  147.2 11.5 %collective-permute-start.5 = (bf16[2,256,768]{2,1,0:T(8,128)(2,1)S(1)}, bf16[2,256,768]{2,1,0:T(8,128)(2,1)S(1)}, u32[]{:S(2)}, u32[]{:S(2)}) collective-permute-start(bf16[2,256,768]{2,1,0:T(8,128)(2,1)S(1)} %get-tuple-element.65.grads0), channel_id=1, source_target_pairs={{0,64},{64,0},{1,65},{65,1},{2,66},{66,2},{3,67},{67,3},{4,68},{68... | collective-permute-start | bytes 2359304 | tf_op jit(solution)/shard_map/ppermute | solution.py:329
  149.5 26.0 %all-to-all-start.5 = ((bf16[8,16,384]{2,1,0:T(8,128)(2,1)}), bf16[8,16,384]{2,1,0:T(8,128)(2,1)S(1)}, u32[]{:S(2)}, u32[]{:S(2)}) async-start(bf16[8,16,384]{2,1,0:T(8,128)(2,1)} %bitcast.18), calls=%async_computation.5 | async-start | bytes 196608 | tf_op jit(solution)/shard_map/all_to_all | solution.py:333
  152.9 3.2 %collective-permute-start.6 = (f32[256,1]{1,0:T(8,128)S(1)}, f32[256,1]{1,0:T(8,128)S(1)}, u32[]{:S(2)}, u32[]{:S(2)}) collective-permute-start(f32[256,1]{1,0:T(8,128)S(1)} %get-tuple-element.68.probs.probs0), channel_id=1, source_target_pairs={{0,64},{64,0},{1,65},{65,1},{2,66},{66,2},{3,67},{67,3},{4,68},{68... | collective-permute-start | bytes 3080 | tf_op jit(solution)/shard_map/ppermute | solution.py:327
  156.1 0.9 copy-start.9
  157.0 1.7 copy-start.7
